TPU v7x, 256 devices: a whole 4x4x8 slice. The times are simulated.
256 devices in a mesh: qrow: 16 (over z, x_lo), kcol: 8 (over x_hi, y), head: 2 (over core).
Axes of the slice: x: 4 (x_hi: 2, x_lo: 2; x = x_hi * 2 + x_lo), y: 4, z: 8, core: 2. Of those that a mesh axis runs over, the one named last changes fastest.
Arguments:
- query: bfloat16 [16384, 1024], P(('qrow', 'kcol'), 'head'), parts along dimension 1, may hold values from -5 to 5, as said below
- key: bfloat16 [16384, 256], P(('kcol', 'qrow'), 'head'), parts along dimension 1, may hold values from -5 to 5, as said below
- value: bfloat16 [16384, 256], P(('kcol', 'qrow'), 'head'), parts along dimension 1, may hold values from -0.5 to 2.5
- dout: bfloat16 [16384, 1024], P(('qrow', 'kcol'), 'head'), parts along dimension 1, may hold values from -6 to 6
- document: int32 [16384], replicated, may hold values from 0 to 7, never falling along the last dimension, each value on 1 to 8192 neighbouring positions
Outputs:
- attended: bfloat16 [16384, 1024], P(('qrow', 'kcol'), 'head'), parts along dimension 1
- grad_query: bfloat16 [16384, 1024], P(('qrow', 'kcol'), 'head'), parts along dimension 1
- grad_key: bfloat16 [16384, 256], P(('kcol', 'qrow'), 'head'), parts along dimension 1
- grad_value: bfloat16 [16384, 256], P(('kcol', 'qrow'), 'head'), parts along dimension 1
There are 2 independent parts, one for each index of `head`. A program takes and returns all parts, laid end to end along the dimension named above; an argument that names none is the same for every part. Nothing has to cross between parts.
Inputs may be any that keep to these rules, and one draw needn't show every extreme that they name: `query`: entries of order one. `key`: entries of order one. Document numbers never fall along the sequence; each document is a run of 1 to 8192 positions, and one has exactly 8192.
All inputs are finite; a program needn't handle non-finite values.
Results may differ from a plain program's by a relative error of at most 0.035.
Values may be sent and summed in bfloat16 or wider, within the bound.
No kernel may reach another device: no remote copies, remote signals or barrier semaphores. Data moves between devices by JAX's collectives and lax.ppermute only.
A program may use at most 128 MiB of HBM per device.

v0:
```python
import math

import jax
import jax.numpy as jnp
from jax import lax
from jax.sharding import PartitionSpec as P

NEG = -1e30


def local(query, key, value, dout, document):
    rows = query.shape[0]
    dim = key.shape[1]
    width = query.shape[1]
    group = width // dim
    scale = 1.0 / math.sqrt(dim)
    q_all, do_all = (
        lax.all_gather(query, "kcol", axis=0, tiled=True),
        lax.all_gather(dout, "kcol", axis=0, tiled=True),
    )
    k_all, v_all = (
        lax.all_gather(key, "qrow", axis=0, tiled=True),
        lax.all_gather(value, "qrow", axis=0, tiled=True),
    )
    qlen = q_all.shape[0]
    klen = k_all.shape[0]
    q_start = lax.axis_index("qrow") * qlen
    k_start = lax.axis_index("kcol") * klen
    q_doc = lax.dynamic_slice_in_dim(document, q_start, qlen)
    k_doc = lax.dynamic_slice_in_dim(document, k_start, klen)
    q_pos = q_start + jnp.arange(qlen, dtype=jnp.int32)
    k_pos = k_start + jnp.arange(klen, dtype=jnp.int32)

    def scores_of(q_begin, q_size):
        row_doc = lax.dynamic_slice_in_dim(q_doc, q_begin, q_size)
        row_pos = lax.dynamic_slice_in_dim(q_pos, q_begin, q_size)
        allowed = (row_doc[:, None] == k_doc[None, :]) & (k_pos[None, :] <= row_pos[:, None])
        heads = lax.dynamic_slice_in_dim(q_all, q_begin, q_size).reshape(q_size, group, dim)
        score = jnp.einsum("rhd,cd->hrc", heads, k_all, preferred_element_type=jnp.float32) * scale
        return (jnp.where(allowed[None], score, NEG), allowed)

    q_step = math.gcd(qlen, 512)
    q_count = qlen // q_step

    def stat_block(index):
        score, allowed = scores_of(index * q_step, q_step)
        high = jnp.max(score, axis=2)
        total = jnp.sum(jnp.where(allowed[None], jnp.exp(score - high[:, :, None]), 0.0), axis=2)
        return (high, total)

    highs, totals = lax.map(stat_block, jnp.arange(q_count, dtype=jnp.int32))
    high = jnp.transpose(highs, (1, 0, 2)).reshape(group, qlen)
    total = jnp.transpose(totals, (1, 0, 2)).reshape(group, qlen)
    top = lax.pmax(high, "kcol")
    whole = lax.psum(total * jnp.exp(high - top), "kcol")
    lse = top + jnp.log(whole)
    step = math.gcd(rows * lax.axis_size("kcol"), 512)

    def work(index):
        begin = index * step
        score, allowed = scores_of(begin, step)
        part = lax.dynamic_slice_in_dim(lse, begin, step, 1)
        prob_low = jnp.where(allowed[None], jnp.exp(score - part[:, :, None]), 0.0).astype(
            jnp.bfloat16
        )
        mixed = jnp.einsum("hrc,cd->rhd", prob_low, v_all, preferred_element_type=jnp.float32)
        return mixed.reshape(step, width)

    pieces = lax.map(work, jnp.arange(rows * lax.axis_size("kcol") // step, dtype=jnp.int32))
    attended = lax.psum_scatter(
        pieces.reshape(rows * lax.axis_size("kcol"), width), "kcol", scatter_dimension=0, tiled=True
    ).astype(jnp.bfloat16)
    own_delta = jnp.sum(
        (dout.astype(jnp.float32) * attended.astype(jnp.float32)).reshape(rows, group, dim), axis=2
    )
    delta = jnp.transpose(lax.all_gather(own_delta, "kcol", axis=0, tiled=True))

    def tile_grads(q_begin, q_size):
        score, allowed = scores_of(q_begin, q_size)
        part_lse = lax.dynamic_slice_in_dim(lse, q_begin, q_size, 1)
        part_delta = lax.dynamic_slice_in_dim(delta, q_begin, q_size, 1)
        prob = jnp.where(allowed[None], jnp.exp(score - part_lse[:, :, None]), 0.0)
        prob_low = prob.astype(jnp.bfloat16)
        grad_heads = lax.dynamic_slice_in_dim(do_all, q_begin, q_size).reshape(q_size, group, dim)
        dprob = jnp.einsum("rhd,cd->hrc", grad_heads, v_all, preferred_element_type=jnp.float32)
        dscore = (prob * (dprob - part_delta[:, :, None])).astype(jnp.bfloat16)
        return (prob_low, dscore, grad_heads)

    def row_step(carry, index):
        begin = index * q_step
        prob_low, dscore, grad_heads = tile_grads(begin, q_step)
        heads = lax.dynamic_slice_in_dim(q_all, begin, q_step).reshape(q_step, group, dim)
        grad_q = scale * jnp.einsum(
            "hrc,cd->rhd", dscore, k_all, preferred_element_type=jnp.float32
        )
        next_k = carry[0] + scale * jnp.einsum(
            "hrc,rhd->cd", dscore, heads, preferred_element_type=jnp.float32
        )
        next_v = carry[1] + jnp.einsum(
            "hrc,rhd->cd", prob_low, grad_heads, preferred_element_type=jnp.float32
        )
        return ((next_k, next_v), grad_q.reshape(q_step, width))

    empty = jnp.zeros((klen, dim), jnp.float32)
    (grad_k_part, grad_v_part), grad_blocks = lax.scan(
        row_step, (empty, empty), jnp.arange(q_count, dtype=jnp.int32)
    )
    grad_query = lax.psum_scatter(
        grad_blocks.reshape(qlen, width), "kcol", scatter_dimension=0, tiled=True
    )
    grad_key, grad_value = (
        lax.psum_scatter(grad_k_part, "qrow", scatter_dimension=0, tiled=True),
        lax.psum_scatter(grad_v_part, "qrow", scatter_dimension=0, tiled=True),
    )
    return (
        attended,
        grad_query.astype(jnp.bfloat16),
        grad_key.astype(jnp.bfloat16),
        grad_value.astype(jnp.bfloat16),
    )


def solution(mesh):
    placed = (
        P(("qrow", "kcol"), "head"),
        P(("kcol", "qrow"), "head"),
        P(("kcol", "qrow"), "head"),
        P(("qrow", "kcol"), "head"),
        P(),
    )
    return jax.shard_map(
        local,
        mesh=mesh,
        in_specs=placed,
        out_specs=(
            P(("qrow", "kcol"), "head"),
            P(("qrow", "kcol"), "head"),
            P(("kcol", "qrow"), "head"),
            P(("kcol", "qrow"), "head"),
        ),
        check_vma=False,
    )
```

profile of v0, /device:TPU:32, one launch (start us, length us, event | category | flops | bytes accessed | tf_op | source)
XLA Modules:
  0.0 662.9 jit_solution(15974868421595199832)
XLA Ops:
  11.2 39.2 %all_gather.16 = bf16[2048,128]{0,1:T(8,128)(2,1)} all-gather(bf16[128,128]{0,1:T(8,128)(2,1)S(1)} %copy.63), channel_id=1, replica_groups=mesh['qrow'=16,'kcol'=8,'head'=2] {'qrow'}, dimensions={0}, use_global_device_ids=true | all-gather | bytes 557056 | tf_op jit(solution)/shard_map/all_gather | solution.py:22
  51.7 32.7 %all_gather.17 = bf16[2048,128]{1,0:T(8,128)(2,1)S(1)} all-gather(bf16[128,128]{1,0:T(8,128)(2,1)} %param.13), channel_id=1, replica_groups=mesh['qrow'=16,'kcol'=8,'head'=2] {'qrow'}, dimensions={0}, use_global_device_ids=true | all-gather | bytes 557056 | tf_op jit(solution)/shard_map/all_gather | solution.py:23
  85.4 24.9 %while.39 = (s32[]{:T(128)}, f32[2,4,512]{2,1,0:T(4,128)S(1)}, f32[2,4,512]{2,1,0:T(4,128)S(1)}, s32[2]{0:T(128)S(1)}, s32[1024]{0:T(1024)S(1)}, /*index=5*/s32[...) while((s32[]{:T(128)}, f32[2,4,512]{2,1,0:T(4,128)S(1)}, ...), condition=%wide.region_3.4_spmd.clone, body=%wide.region_0.3_spmd.clone.sunk | while | flops 1110439936 | bytes 38891740 | solution.py:51
  92.8 5.0 fusion.80
  101.3 4.0 bitcast_reduce_fusion.2
  105.3 5.0 fusion.80
  110.3 42.0 %pmax.7 = f32[4,1024]{1,0:T(4,128)S(1)} all-reduce(f32[4,1024]{1,0:T(4,128)S(1)} %bitcast.179), channel_id=1, replica_groups=mesh['qrow'=16,'kcol'=8,'head'=2] {'kcol'}, use_global_device_ids=true, to_apply=%region_4.5 | all-reduce | flops 4096 | bytes 32768 | tf_op jit(solution)/shard_map/pmax | solution.py:54
  152.4 36.8 %psum.7 = f32[4,1024]{1,0:T(4,128)S(1)} all-reduce(f32[4,1024]{1,0:T(4,128)S(1)} %exponential_multiply_fusion), channel_id=1, replica_groups=mesh['qrow'=16,'kcol'=8,'head'=2] {'kcol'}, use_global_device_ids=true, to_apply=%region_5.6 | all-reduce | flops 4096 | bytes 32768 | tf_op jit(solution)/shard_map/psum | solution.py:55
  190.8 26.6 %while.40 = (s32[]{:T(128)}, f32[2,512,512]{2,1,0:T(8,128)}, s32[2]{0:T(128)S(1)}, s32[1024]{0:T(1024)S(1)}, s32[2048]{0:T(1024)S(1)}, /*index=5*/s32[1024]{0:T(...) while((s32[]{:T(128)}, f32[2,512,512]{2,1,0:T(8,128)}, ...), condition=%wide.region_7.8_spmd.clone, body=%wide.region_6.7_spmd.clone.sunk | while | flops 2171602944 | bytes 10023143 | solution.py:69
  194.2 8.5 %fusion.85 = f32[4,512,128]{1,2,0:T(8,128)S(1)} fusion(f32[4,512]{1,0:T(4,128)S(1)} %constant_dynamic-slice_fusion.13, pred[512,2048]{1,0:T(8,128)(4,1)S(1)} %compare_and_fusion.7, bf16[512,4,128]{0,2,1:T(8,128)(2,1)S(1)} %bitcast.175, bf16[2048,128]{0,1:T(8,128)(2,1)} %get-tuple-element.810, bf16[2048,128]{1,0:T(8,128)(2,1)S(1)} %get-tuple-element.808), kind=kOutput, calls=%fused_computation.20.clone.1 | convolution fusion | flops 2168455168 | bytes 3678208 | tf_op jit(solution)/shard_map/while/body/eval_jaxpr/hrc,cd->rhd/dot_general | solution.py:66
  207.5 8.5 %fusion.85 = f32[4,512,128]{1,2,0:T(8,128)S(1)} fusion(f32[4,512]{1,0:T(4,128)S(1)} %constant_dynamic-slice_fusion.13, pred[512,2048]{1,0:T(8,128)(4,1)S(1)} %compare_and_fusion.7, bf16[512,4,128]{0,2,1:T(8,128)(2,1)S(1)} %bitcast.175, bf16[2048,128]{0,1:T(8,128)(2,1)} %get-tuple-element.810, bf16[2048,128]{1,0:T(8,128)(2,1)S(1)} %get-tuple-element.808), kind=kOutput, calls=%fused_computation.20.clone.1 | convolution fusion | flops 2168455168 | bytes 3678208 | tf_op jit(solution)/shard_map/while/body/eval_jaxpr/hrc,cd->rhd/dot_general | solution.py:66
  218.4 75.3 %reduce-scatter.5.cloned.1.call-done = f32[128,512]{1,0:T(8,128)} async-done(((f32[1024,512]{1,0:T(8,128)}), f32[128,512]{1,0:T(8,128)}) %reduce-scatter.5.cloned.1.call-update) | async-done | bytes 262160 | tf_op jit(solution)/shard_map/reduce_scatter | solution.py:70
  295.6 35.0 %all_gather.19 = f32[1024,4]{1,0:T(8,128)S(1)} all-gather(f32[128,4]{1,0:T(8,128)S(1)} %reduce_sum.18), channel_id=1, replica_groups=mesh['qrow'=16,'kcol'=8,'head'=2] {'kcol'}, dimensions={0}, use_global_device_ids=true | all-gather | bytes 18432 | tf_op jit(solution)/shard_map/all_gather | solution.py:76
  330.9 15.4 %all-gather.5.cloned.1.call-done = bf16[1024,512]{0,1:T(8,128)(2,1)} async-done(((bf16[128,512]{0,1:T(8,128)(2,1)}), bf16[1024,512]{0,1:T(8,128)(2,1)}) %all-gather.5.cloned.1.call-update) | async-done | bytes 1048592 | tf_op jit(solution)/shard_map/all_gather | solution.py:19
  347.8 80.8 %while.41 = (s32[]{:T(128)}, f32[2048,128]{1,0:T(8,128)S(1)}, f32[2048,128]{1,0:T(8,128)}, f32[2,512,512]{2,1,0:T(8,128)}, s32[2]{0:T(128)S(1)}, /*index=5*/s32[...) while((s32[]{:T(128)}, f32[2048,128]{1,0:T(8,128)S(1)}, ...), condition=%wide.region_11.12_spmd.clone, body=%wide.region_10.11_spmd.clone.sunk | while | flops 5423761408 | bytes 163148080 | solution.py:105
  354.9 5.7 copy-done
  360.6 7.8 %fusion.99 = f32[2048,128]{1,0:T(8,128)} fusion(bf16[512,4,128]{0,2,1:T(8,128)(2,1)S(1)} %bitcast.173, f32[512,4,2048]{2,0,1:T(8,128)S(1)} %fusion.96, f32[4,512]{1,0:T(4,128)S(1)} %get-tuple-element.727, pred[512,2048]{1,0:T(8,128)(4,1)S(1)} %compare_and_fusion.8, f32[2048,128]{1,0:T(8,128)} %get-tuple-element.837, pred[]{:T(512)S(6)} %compare.3), kind=kOutput, calls=%fused_computation.48.clone.1 | convolution fusion | flops 1095237632 | bytes 20455424 | tf_op jit(solution)/shard_map/while/body/eval_jaxpr/hrc,rhd->cd/dot_general | solution.py:99
  368.4 11.0 %fusion.97 = bf16[4,512,2048]{2,1,0:T(8,128)(2,1)S(1)} fusion(f32[512,4,2048]{2,0,1:T(8,128)} %copy-done, f32[4,512]{1,0:T(4,128)S(1)} %get-tuple-element.726, f32[4,512]{1,0:T(4,128)S(1)} %get-tuple-element.727, pred[512,2048]{1,0:T(8,128)(4,1)S(1)} %compare_and_fusion.8, bf16[512,4,128]{0,2,1:T(8,128)(2,1)S(1)} %bitcast.174, ...), kind=kOutput, calls=%fused_computation.36.clone.1 | convolution fusion | flops 1103101952 | bytes 27279360 | tf_op jit(solution)/shard_map/while/body/eval_jaxpr/rhd,cd->hrc/dot_general | solution.py:85
  394.6 5.7 copy-done
  400.3 9.1 %fusion.99 = f32[2048,128]{1,0:T(8,128)} fusion(bf16[512,4,128]{0,2,1:T(8,128)(2,1)S(1)} %bitcast.173, f32[512,4,2048]{2,0,1:T(8,128)S(1)} %fusion.96, f32[4,512]{1,0:T(4,128)S(1)} %get-tuple-element.727, pred[512,2048]{1,0:T(8,128)(4,1)S(1)} %compare_and_fusion.8, f32[2048,128]{1,0:T(8,128)} %get-tuple-element.837, pred[]{:T(512)S(6)} %compare.3), kind=kOutput, calls=%fused_computation.48.clone.1 | convolution fusion | flops 1095237632 | bytes 20455424 | tf_op jit(solution)/shard_map/while/body/eval_jaxpr/hrc,rhd->cd/dot_general | solution.py:99
  409.3 11.0 %fusion.97 = bf16[4,512,2048]{2,1,0:T(8,128)(2,1)S(1)} fusion(f32[512,4,2048]{2,0,1:T(8,128)} %copy-done, f32[4,512]{1,0:T(4,128)S(1)} %get-tuple-element.726, f32[4,512]{1,0:T(4,128)S(1)} %get-tuple-element.727, pred[512,2048]{1,0:T(8,128)(4,1)S(1)} %compare_and_fusion.8, bf16[512,4,128]{0,2,1:T(8,128)(2,1)S(1)} %bitcast.174, ...), kind=kOutput, calls=%fused_computation.36.clone.1 | convolution fusion | flops 1103101952 | bytes 27279360 | tf_op jit(solution)/shard_map/while/body/eval_jaxpr/rhd,cd->hrc/dot_general | solution.py:85
  430.8 66.5 %reduce-scatter.9.cloned.1.call-done = f32[128,128]{1,0:T(8,128)} async-done(((f32[2048,128]{1,0:T(8,128)}), f32[128,128]{1,0:T(8,128)}) %reduce-scatter.9.cloned.1.call-update) | async-done | bytes 65552 | tf_op jit(solution)/shard_map/reduce_scatter | solution.py:112
  498.7 71.1 %reduce-scatter.11.cloned.1.call-done = f32[128,128]{1,0:T(8,128)} async-done(((f32[2048,128]{1,0:T(8,128)}), f32[128,128]{1,0:T(8,128)}) %reduce-scatter.11.cloned.1.call-update) | async-done | bytes 65552 | tf_op jit(solution)/shard_map/reduce_scatter | solution.py:113
  571.3 83.2 %reduce-scatter.7.cloned.1.call-done = f32[128,512]{1,0:T(8,128)} async-done(((f32[1024,512]{1,0:T(8,128)}), f32[128,512]{1,0:T(8,128)}) %reduce-scatter.7.cloned.1.call-update) | async-done | bytes 262160 | tf_op jit(solution)/shard_map/reduce_scatter | solution.py:108
  (108 shorter events, 66.0 us)
Async XLA Ops:
  7.2 78.3 %all-gather.3.cloned.1.call-start = ((), (), s32[]{:S(2)}) async-start(), calls=%async_computation.4 | async-start | bytes 1179648 | tf_op jit(solution)/shard_map/all_gather | solution.py:18
  8.9 284.8 %reduce-scatter.5.cloned.1.call-start = ((), (), s32[]{:S(2)}) async-start(), calls=%async_computation.5 | async-start | bytes 2359296 | tf_op jit(solution)/shard_map/reduce_scatter | solution.py:70
  84.4 1.0 copy-start.2
  190.8 26.7 %copy-start.4 = (bf16[128,512]{1,0:T(8,128)(2,1)S(1)}, bf16[128,512]{1,0:T(8,128)(2,1)}, u32[]{:S(2)}) copy-start(bf16[128,512]{1,0:T(8,128)(2,1)} %param.14) | copy-start | bytes 393220
  217.5 128.8 %all-gather.5.cloned.1.call-start = ((), (), s32[]{:S(2)}) async-start(), calls=%async_computation.6 | async-start | bytes 1179648 | tf_op jit(solution)/shard_map/all_gather | solution.py:19
  218.3 279.0 %reduce-scatter.9.cloned.1.call-start = ((), (), s32[]{:S(2)}) async-start(), calls=%async_computation.8 | async-start | bytes 1114112 | tf_op jit(solution)/shard_map/reduce_scatter | solution.py:112
  354.8 5.7 copy-start
  360.6 7.8 %copy-start.3 = (bf16[2048,128]{1,0:T(8,128)(2,1)S(1)}, bf16[2048,128]{1,0:T(8,128)(2,1)}, u32[]{:S(2)}) copy-start(bf16[2048,128]{1,0:T(8,128)(2,1)} %get-tuple-element.866) | copy-start | bytes 1572868 | tf_op jit(solution)/shard_map/while
  394.6 5.7 copy-start
  400.3 9.1 %copy-start.3 = (bf16[2048,128]{1,0:T(8,128)(2,1)S(1)}, bf16[2048,128]{1,0:T(8,128)(2,1)}, u32[]{:S(2)}) copy-start(bf16[2048,128]{1,0:T(8,128)(2,1)} %get-tuple-element.866) | copy-start | bytes 1572868 | tf_op jit(solution)/shard_map/while
  428.6 1.0 copy-start.1
  429.6 140.3 %reduce-scatter.11.cloned.1.call-start = ((), (), s32[]{:S(2)}) async-start(), calls=%async_computation.9 | async-start | bytes 1114112 | tf_op jit(solution)/shard_map/reduce_scatter | solution.py:113
  430.2 224.3 %reduce-scatter.7.cloned.1.call-start = ((), (), s32[]{:S(2)}) async-start(), calls=%async_computation.7 | async-start | bytes 2359296 | tf_op jit(solution)/shard_map/reduce_scatter | solution.py:108
Sparse Core Ops, SparseCore 0:
  11.0 55.9 all-gather.2
  217.6 76.0 reduce-scatter.4
  296.7 49.4 all-gather.4
  429.7 67.4 reduce-scatter.8
  499.8 70.0 reduce-scatter.10
  573.7 80.7 reduce-scatter.6
where the time goes:
time: 664 us; the launch traced here: 663 us
  waiting for transfers between devices  313 us (47%)
  blocking collectives  186 us (28%)
  matrix products  84.2 us (13%)
  local copies, waits for them, and re-layouts  39.8 us (6%)
  other arithmetic  22 us (3%)
  between operations  14.2 us (2%)
    reduce_scatter x1, waiting for transfers between devices, local(): lax.psum_scatter(grad_blocks.reshape(qlen, width), 'kcol', scatter_dimens...  83.2 us
    reduce_scatter x1, waiting for transfers between devices, local(): lax.psum_scatter(pieces.reshape(rows * lax.axis_size('kcol'), width), 'kc...  75.3 us
    reduce_scatter x1, waiting for transfers between devices, local(): lax.psum_scatter(grad_v_part, 'qrow', scatter_dimension=0, tiled=True)  71.1 us
    reduce_scatter x1, waiting for transfers between devices, local(): lax.psum_scatter(grad_k_part, 'qrow', scatter_dimension=0, tiled=True)  66.5 us
    pmax x1, blocking collectives, local(): top = lax.pmax(high, 'kcol')  42 us
    all_gather x1, blocking collectives, local(): lax.all_gather(key, 'qrow', axis=0, tiled=True)  39.2 us
    psum x1, blocking collectives, local(): whole = lax.psum(total * jnp.exp(high - top), 'kcol')  36.8 us
    all_gather x1, blocking collectives, local(): delta = jnp.transpose(lax.all_gather(own_delta, 'kcol', axis=0, tiled=True))  35 us
  transfers between devices with their start and end apart: 6, of which 5 were waited for; matrix products, arithmetic and copies ran while one was open for 2% of the time, Pallas kernels for 0%

commit v1 on v0

v1 whole, which is shorter than its diff:
```python
import functools
import math

import jax
import jax.numpy as jnp
from jax import lax
from jax.experimental import pallas as pl
from jax.experimental.pallas import tpu as pltpu
from jax.sharding import PartitionSpec as P

AXES = ("qrow", "kcol")
DEVICES = 128
CHUNK = 128
SLOTS = 4
TILES = 2
ROWS = SLOTS * CHUNK
PAIR = 2 * CHUNK
PLANE = 16 * CHUNK
NEG = -1e30
FLOOR = -1e29
LOG2E = math.log2(math.e)
F32 = jnp.float32
BF16 = jnp.bfloat16


def flip(mask):
    return [(d, d ^ mask) for d in range(DEVICES)]


X_LO, X_HI = flip(8), flip(4)
Y = [flip(s) for s in range(SLOTS)]
EVEN = flip(16)
ODD = [(d, (d + (16 if d // 16 % 2 else -16)) % DEVICES) for d in range(DEVICES)]


def dot(a, b):
    return lax.dot_general(a, b, (((1,), (0,)), ((), ())), preferred_element_type=F32)


def dot_t(a, b):
    return lax.dot_general(a, b, (((1,), (1,)), ((), ())), preferred_element_type=F32)


def fill(rows, keys, q_s, do_s, k_s, v_s, t_s, group, width, which):
    own, other, near, last, far_own, far_other = rows
    top, low = pl.ds(0, CHUNK), pl.ds(CHUNK, CHUNK)
    parts = [
        [(own, top), (near, top), (far_own, top), (last, top)],
        [(other, top), (near, low), (far_other, top), (last, low)],
    ]
    for t in range(TILES):
        for s in range(SLOTS):
            ref, at = parts[t][s]
            part = ref[at, :]
            to = pl.ds(s * CHUNK, CHUNK)
            for h in range(group):
                q_s[t, h, to, :] = part[:, h * width : (h + 1) * width]
                do_s[t, h, to, :] = part[:, (group + h) * width : (group + h + 1) * width]
    for n, ref in enumerate(keys):
        for u in range(2):
            part = ref[pl.ds(u * CHUNK, CHUNK), :]
            block, at = n // 2 * 2 + u, pl.ds(n % 2 * CHUNK, CHUNK)
            k_s[block, at, :] = part[:, :width]
            v_s[block, at, :] = part[:, width:]
            t_s[block, :, at] = jnp.transpose(part[:, which * width : (which + 1) * width])


def place(sc, pair, u, t):
    z, x_lo, x_hi, y = (sc[n] for n in range(4))
    plane = (4 * (x_hi ^ u) + y) * PLANE + x_lo * CHUNK
    one, two = plane + sc[8 + 2 * pair] * PAIR, plane + sc[9 + 2 * pair] * PAIR
    row = ((z * 4 + x_lo * 2 + x_hi) ^ (2 * t)) * ROWS
    first, last = sc[4 + 2 * t], sc[5 + 2 * t]
    low, high = jnp.minimum(one, two), jnp.maximum(one, two)
    needed = (low <= row + ROWS - 1) & (high + CHUNK - 1 >= first)
    whole = (high + CHUNK - 1 <= row) & (low >= last)
    return one, two, row, needed, whole


def allowed_of(sc, start, one, two, row):
    index = lax.broadcasted_iota(jnp.int32, (PAIR, 1), 0)
    key_at = index + jnp.where(index < CHUNK, one, two - CHUNK)
    row_at = row + (lax.broadcasted_iota(jnp.int32, (1, ROWS), 1) ^ (sc[3] * CHUNK))
    return (key_at >= start) & (key_at <= row_at)


def forward(group, width, pairs, sc, start, *refs):
    rows, keys, refs = refs[:6], refs[6 : 6 + 2 * pairs], refs[6 + 2 * pairs :]
    acc, stat, q_s, do_s, k_s, v_s, t_s, high, total, mixed = refs
    unit = LOG2E / math.sqrt(width)
    heads = range(group)
    fill(rows, keys, q_s, do_s, k_s, v_s, t_s, group, width, 1)
    acc[...] = jnp.zeros_like(acc)
    high[...] = jnp.full_like(high, FLOOR)
    total[...] = jnp.zeros_like(total)
    mixed[...] = jnp.zeros_like(mixed)

    def block(b, t, one, two, row, masked):
        scores = [dot_t(k_s[b], q_s[t, h]) for h in heads]
        dprobs = [dot_t(v_s[b], do_s[t, h]) for h in heads]
        if masked:
            allowed = allowed_of(sc, start[t], one, two, row)
            scores = [jnp.where(allowed, s, NEG) for s in scores]
        olds = [high[t, h] for h in heads]
        news = [jnp.maximum(o, jnp.max(s, axis=0, keepdims=True)) for o, s in zip(olds, scores)]
        shrinks = [jnp.exp2((o - n) * unit) for o, n in zip(olds, news)]
        es = [jnp.exp2(s * unit - n * unit) for s, n in zip(scores, news)]
        totals = [total[t, h] * shrinks[h] + jnp.sum(es[h], axis=0, keepdims=True) for h in heads]
        mixeds = [
            mixed[t, h] * shrinks[h] + jnp.sum(es[h] * dprobs[h], axis=0, keepdims=True)
            for h in heads
        ]
        accs = [acc[t, h] * shrinks[h] + dot(t_s[b], es[h].astype(BF16)) for h in heads]
        for h in heads:
            high[t, h] = news[h]
            total[t, h] = totals[h]
            mixed[t, h] = mixeds[h]
            acc[t, h] = accs[h]

    def step(n, carry):
        b, t = n // 2, n & 1
        one, two, row, needed, whole = place(sc, n // 4, (n // 2) & 1, t)

        @pl.when(needed & whole)
        def _():
            block(b, t, one, two, row, False)

        @pl.when(needed & jnp.logical_not(whole))
        def _():
            block(b, t, one, two, row, True)

        return carry

    lax.fori_loop(0, 4 * pairs, step, 0)
    for t in range(TILES):
        for h in heads:
            stat[t, h : h + 1, :] = high[t, h]
            stat[t, group + h : group + h + 1, :] = total[t, h]
            stat[t, 2 * group + h : 2 * group + h + 1, :] = mixed[t, h]


def backward(group, width, pairs, begins, ends, sc, start, *refs):
    rows, keys, refs = refs[:6], refs[6 : 6 + 2 * pairs], refs[6 + 2 * pairs :]
    scale = 1.0 / math.sqrt(width)
    unit = LOG2E * scale
    heads = range(group)
    if begins:
        stats, own, values, refs = refs[:SLOTS], refs[SLOTS], refs[SLOTS + 1], refs[SLOTS + 2 :]
    else:
        acc_in, lse_in, delta_in, refs = *refs[:3], refs[3:]
    dkv, refs = refs[0], refs[1:]
    if begins:
        mixed, refs = refs[: TILES * SLOTS], refs[TILES * SLOTS :]
    if ends:
        dq, refs = refs[: TILES * SLOTS], refs[TILES * SLOTS :]
    acc, lse, delta, q_s, do_s, k_s, v_s, t_s, grads = refs
    fill(rows, keys, q_s, do_s, k_s, v_s, t_s, group, width, 0)
    if begins:
        acc[...] = jnp.zeros_like(acc)
        for t in range(TILES):
            for u in range(SLOTS):
                at = pl.ds(u * CHUNK, CHUNK)
                parts = [stats[s][t, :, pl.ds((u ^ s) * CHUNK, CHUNK)] for s in range(SLOTS)]
                top = functools.reduce(jnp.maximum, [p[:group] for p in parts])
                weights = [jnp.exp2((p[:group] - top) * unit) for p in parts]
                total = sum(w * p[group : 2 * group] for w, p in zip(weights, parts))
                product = sum(w * p[2 * group :] for w, p in zip(weights, parts))
                low, small = top * unit + jnp.log2(total), product / total
                part = jnp.exp2(own[t, :group, at] * unit - low)
                for h in heads:
                    lse[t, h, :, at] = low[h : h + 1]
                    delta[t, h, :, at] = small[h : h + 1]
                    mixed[t * SLOTS + u][h * width : (h + 1) * width, :] = (
                        values[t, h, :, at] * part[h : h + 1]
                    ).astype(BF16)
    else:
        acc[...] = acc_in[...]
        lse[...] = lse_in[...]
        delta[...] = delta_in[...]

    def block(b, t, one, two, row, masked):
        scores = [dot_t(k_s[b], q_s[t, h]) for h in heads]
        dprobs = [dot_t(v_s[b], do_s[t, h]) for h in heads]
        if masked:
            allowed = allowed_of(sc, start[t], one, two, row)
            scores = [jnp.where(allowed, s, NEG) for s in scores]
        probs = [jnp.exp2(scores[h] * unit - lse[t, h]) for h in heads]
        dscores = [(probs[h] * (dprobs[h] - delta[t, h])).astype(BF16) for h in heads]
        lows = [p.astype(BF16) for p in probs]
        dk = sum(dot(dscores[h], q_s[t, h]) for h in heads)
        dv = sum(dot(lows[h], do_s[t, h]) for h in heads)
        accs = [acc[t, h] + dot(t_s[b], dscores[h]) for h in heads]
        for h in heads:
            acc[t, h] = accs[h]
        grads[:, :width] = grads[:, :width] + dk * scale
        grads[:, width:] = grads[:, width:] + dv

    def step(b, carry):
        grads[...] = jnp.zeros_like(grads)

        def tile(t, carry):
            one, two, row, needed, whole = place(sc, b // 2, b & 1, t)

            @pl.when(needed & whole)
            def _():
                block(b, t, one, two, row, False)

            @pl.when(needed & jnp.logical_not(whole))
            def _():
                block(b, t, one, two, row, True)

            return carry

        lax.fori_loop(0, TILES, tile, 0)
        for n in range(2):
            dkv[b // 2 * 2 + n, b & 1] = grads[n * CHUNK : (n + 1) * CHUNK, :].astype(BF16)
        return carry

    lax.fori_loop(0, 2 * pairs, step, 0)
    if ends:
        for t in range(TILES):
            for h in heads:
                value = (acc[t, h] * scale).astype(BF16)
                for s in range(SLOTS):
                    dq[t * SLOTS + s][h * width : (h + 1) * width, :] = value[
                        :, s * CHUNK : (s + 1) * CHUNK
                    ]


def combine(group, width, *refs):
    parts, out = refs[:-1], refs[-1]
    for h in range(group):
        at = pl.ds(h * width, width)
        whole = sum(part[at, :].astype(F32) for part in parts)
        out[:, at] = jnp.transpose(whole).astype(BF16)


def add(*parts):
    return sum(part.astype(F32) for part in parts).astype(BF16)


def local(query, key, value, dout, document):
    width = key.shape[1]
    group = query.shape[1] // width
    send = functools.partial(lax.ppermute, axis_name=AXES)
    qrow, kcol = lax.axis_index("qrow"), lax.axis_index("kcol")
    z, x_lo, x_hi, y = qrow // 2, qrow % 2, kcol // 4, kcol % 4

    key_home = jnp.concatenate([key, value], axis=1)
    row_home = jnp.concatenate([query, dout], axis=1)
    row_other = send(row_home, perm=X_LO)
    own = jnp.concatenate([key_home, send(key_home, perm=X_HI)], axis=0)
    a, b = [own], [own]
    for k in range(3):
        a.append(send(b[k], perm=EVEN))
        b.append(send(a[k], perm=ODD))
    both = jnp.concatenate([row_home, row_other], axis=0)
    near, last = send(both, perm=Y[1]), send(both, perm=Y[3])
    far_own, far_other = send(last[:CHUNK], perm=Y[1]), send(near[CHUNK:], perm=Y[3])
    opposite = jnp.concatenate(
        [send(b[3][:CHUNK], perm=EVEN), send(a[3][CHUNK:], perm=ODD)], axis=0
    )
    rows = [row_home, row_other, near, last, far_own, far_other]
    keys = [a[0], a[1], b[1], b[2], a[2], a[3], b[3], opposite]

    numbers = jnp.arange(8, dtype=jnp.int32)
    starts = jnp.sum((document[None, :] < numbers[:, None]).astype(jnp.int32), axis=1)
    place_of = qrow * 8 + kcol
    row_doc = jnp.concatenate(
        [
            lax.dynamic_slice_in_dim(document, (place_of ^ (8 * t + s)) * CHUNK, CHUNK)
            for t in range(TILES)
            for s in range(SLOTS)
        ]
    )
    start = jnp.sum(jnp.where(row_doc[None] == numbers[:, None], starts[:, None], 0), axis=0)
    start = start.reshape(TILES, 1, ROWS)
    side = 1 - 2 * (z % 2)
    sources = jnp.stack([z + side * k for k in (0, 1, -1, -2, 2, 3, -3, 4)]) & 7
    sc = jnp.concatenate(
        [
            jnp.stack([z, x_lo, x_hi, y]),
            jnp.stack([jnp.min(start, axis=(1, 2)), jnp.max(start, axis=(1, 2))], 1).reshape(-1),
            sources,
        ]
    ).astype(jnp.int32)

    smem = pl.BlockSpec(memory_space=pltpu.SMEM)
    vmem = pl.BlockSpec(memory_space=pltpu.VMEM)
    params = pltpu.CompilerParams(vmem_limit_bytes=56 * 1024 * 1024)

    def cost(dots, pairs):
        work = TILES * ROWS * group * pairs * 2 * PAIR * width * 2
        return pl.CostEstimate(flops=dots * work // 2, bytes_accessed=1 << 23, transcendentals=0)

    def scratch(pairs):
        return [
            pltpu.VMEM((TILES, group, ROWS, width), BF16),
            pltpu.VMEM((TILES, group, ROWS, width), BF16),
            pltpu.VMEM((2 * pairs, PAIR, width), BF16),
            pltpu.VMEM((2 * pairs, PAIR, width), BF16),
            pltpu.VMEM((2 * pairs, width, PAIR), BF16),
        ]

    line = (TILES, group, 1, ROWS)
    acc_shape = jax.ShapeDtypeStruct((TILES, group, width, ROWS), F32)
    line_shape = jax.ShapeDtypeStruct(line, F32)
    stat_shape = jax.ShapeDtypeStruct((TILES, 3 * group, ROWS), F32)
    piece = jax.ShapeDtypeStruct((group * width, CHUNK), BF16)

    values, stat = pl.pallas_call(
        functools.partial(forward, group, width, 4),
        out_shape=[acc_shape, stat_shape],
        in_specs=[smem] + [vmem] * 15,
        out_specs=[vmem] * 2,
        scratch_shapes=scratch(4) + [pltpu.VMEM(line, F32)] * 3,
        compiler_params=params,
        cost_estimate=cost(3, 4),
        name="forward",
    )(sc, start, *rows, *keys)

    unit = LOG2E / math.sqrt(width)
    other = send(stat, perm=X_LO)[::-1]
    top = jnp.maximum(stat[:, :group], other[:, :group])
    mine, theirs = (jnp.exp2((s[:, :group] - top) * unit) for s in (stat, other))
    merged = jnp.concatenate(
        [top]
        + [
            stat[:, n * group : (n + 1) * group] * mine
            + other[:, n * group : (n + 1) * group] * theirs
            for n in (1, 2)
        ],
        axis=1,
    )
    stats = [merged] + [send(merged, perm=Y[s]) for s in range(1, SLOTS)]

    def back(pairs, begins, ends, sc, keys, *more):
        dkv_shape = jax.ShapeDtypeStruct((2 * pairs, 2, CHUNK, 2 * width), BF16)
        shapes = [dkv_shape] + [piece] * (TILES * SLOTS * (begins + ends))
        carried = [acc_shape, line_shape, line_shape]
        more_scratch = scratch(pairs) + [pltpu.VMEM((PAIR, 2 * width), F32)]
        if ends:
            more_scratch = [pltpu.VMEM(s.shape, F32) for s in carried] + more_scratch
        else:
            shapes = shapes + carried
        return pl.pallas_call(
            functools.partial(backward, group, width, pairs, begins, ends),
            out_shape=shapes,
            in_specs=[smem] + [vmem] * (7 + 2 * pairs + len(more)),
            out_specs=[vmem] * len(shapes),
            scratch_shapes=more_scratch,
            compiler_params=params,
            cost_estimate=cost(5, pairs),
            name="backward_begin" if begins else "backward_end",
        )(sc, start, *rows, *keys, *more)

    def shifted(skip):
        return jnp.concatenate([sc[:8], sc[8 + skip :]])

    late = back(2, True, False, shifted(4), keys[4:], *stats, stat, values)
    far, mixed, carried = late[0], late[1 : 1 + TILES * SLOTS], late[1 + TILES * SLOTS :]
    end = back(2, False, True, sc, keys[:4], *carried)
    close, dq = end[0], end[1:]

    def spread(parts):
        masks = [8 * t + s for t in range(TILES) for s in range(SLOTS)]
        return [parts[0]] + [send(p, perm=flip(m)) for p, m in zip(parts[1:], masks[1:])]

    flat = (PAIR, 2 * width)
    one = send(far[3, 0], perm=EVEN)
    two = send(far[3, 1], perm=ODD)
    mixed = spread(mixed)
    gb = jnp.concatenate([add(far[2, 0], one), far[2, 1]], axis=0)
    ga = jnp.concatenate([far[1, 0], add(far[1, 1], two)], axis=0)
    for pa, pb in ((far[0], close[3]), (close[1], close[2])):
        sent_b, sent_a = send(gb, perm=ODD), send(ga, perm=EVEN)
        ga, gb = add(pa.reshape(flat), sent_b), add(pb.reshape(flat), sent_a)
    grad = add(close[0].reshape(flat), send(ga, perm=EVEN), send(gb, perm=ODD))
    dq = spread(dq)
    grad = add(grad[:CHUNK], send(grad[CHUNK:], perm=X_HI))

    outs = [
        pl.pallas_call(
            functools.partial(combine, group, width),
            out_shape=jax.ShapeDtypeStruct((CHUNK, group * width), BF16),
            in_specs=[vmem] * (TILES * SLOTS),
            out_specs=vmem,
            name=name,
        )(*parts)
        for parts, name in ((mixed, "attended"), (dq, "grad_query"))
    ]
    return *outs, grad[:, :width], grad[:, width:]


def solution(mesh):
    by_row = P(("qrow", "kcol"), "head")
    by_key = P(("kcol", "qrow"), "head")
    return jax.shard_map(
        local,
        mesh=mesh,
        in_specs=(by_row, by_key, by_key, by_row, P()),
        out_specs=(by_row, by_row, by_key, by_key),
        check_vma=False,
    )
```

time: 664 us -> 152 us (0.23)
  waiting for transfers between devices: 313 us -> 27 us
  blocking collectives: 186 us -> 0 us
  matrix products: 84.2 us -> 0 us
  starting transfers between devices: 0.24 us -> 79.9 us
  Pallas kernels: 0 us -> 24.5 us
  local copies, waits for them, and re-layouts: 39.8 us -> 15.9 us
  other arithmetic: 22 us -> 2.6 us
  between operations: 14.2 us -> 1.36 us
    reduce_scatter x4 -> x0, waiting for transfers between devices: 296 us -> none  [the longest x1 83.2 us: local(): lax.psum_scatter(grad_blocks.reshape(qlen, width), 'kcol', scatter_dimens...]
    all_gather x3 -> x0, blocking collectives: 107 us -> none  [the longest x1 39.2 us: local(): lax.all_gather(key, 'qrow', axis=0, tiled=True)]
    dot_general x14 -> x0, matrix products: 84.2 us -> none  [the longest x2 22.1 us: tile_grads(): jnp.einsum('rhd,cd->hrc', grad_heads, v_all, preferred_element_type=jnp.f...]
    ppermute x0 -> x41, starting transfers between devices: none -> 79.9 us  [the longest x14 29.7 us: spread(): send(p, perm=flip(m))]
    pmax x1 -> x0, blocking collectives: 42 us -> none  [local(): top = lax.pmax(high, 'kcol')]
    psum x1 -> x0, blocking collectives: 36.8 us -> none  [local(): whole = lax.psum(total * jnp.exp(high - top), 'kcol')]
    ppermute x0 -> x41, waiting for transfers between devices: none -> 27 us  [the longest x4 9.49 us: local(): sent_b, sent_a = (send(gb, perm=ODD), send(ga, perm=EVEN))]
    pallas_call x0 -> x5, Pallas kernels: none -> 24.5 us  [the longest x2 13 us: back(): pl.pallas_call(functools.partial(backward, group, width, pairs, begins, e...]
  transfers between devices with their start and end apart: 6 -> 41, of which waited for: 5 -> 13; matrix products, arithmetic and copies ran while one was open for 2% -> 9% of each run, Pallas kernels for 0% -> 6%
where the time goes in v1:
time: 152 us; the launch traced here: 151 us
  starting transfers between devices  79.9 us (53%)
  waiting for transfers between devices  27 us (18%)
  Pallas kernels  24.5 us (16%)
  local copies, waits for them, and re-layouts  15.9 us (10%)
  other arithmetic  2.6 us (2%)
    ppermute x14, starting transfers between devices, spread(): send(p, perm=flip(m))  29.7 us
    pallas_call x2, Pallas kernels, back(): pl.pallas_call(functools.partial(backward, group, width, pairs, begins, e...  13 us
    ppermute x4, starting transfers between devices, local(): sent_b, sent_a = (send(gb, perm=ODD), send(ga, perm=EVEN))  11.5 us
    ppermute x4, waiting for transfers between devices, local(): sent_b, sent_a = (send(gb, perm=ODD), send(ga, perm=EVEN))  9.49 us
    unnamed x98, local copies, waits for them, and re-layouts  9.12 us
    pallas_call x1, Pallas kernels, local(): pl.pallas_call(functools.partial(forward, group, width, 4), out_shape=[ac...  7.2 us
    ppermute x1, starting transfers between devices, local(): two = send(far[3, 1], perm=ODD)  6.42 us
    ppermute x3, starting transfers between devices, local(): b.append(send(a[k], perm=ODD))  5.8 us
  transfers between devices with their start and end apart: 41, of which 13 were waited for; matrix products, arithmetic and copies ran while one was open for 9% of the time, Pallas kernels for 6%

profile of v1, /device:TPU:32, one launch (start us, length us, event | category | flops | bytes accessed | tf_op | source)
XLA Modules:
  0.0 151.3 jit_solution(3282579512582378064)
XLA Ops:
  2.2 3.1 %collective-permute-start.5 = (bf16[128,256]{1,0:T(8,128)(2,1)S(1)}, bf16[128,256]{1,0:T(8,128)(2,1)S(1)}, u32[]{:S(2)}, u32[]{:S(2)}) collective-permute-start(bf16[128,256]{1,0:T(8,128)(2,1)S(1)} %constant_dynamic-update-slice_fusion.3), channel_id=1, source_target_pairs={{0,8},{2,10},{4,12},{6,14},{8,0},{10,2},{12,4},{14,6},{16,24},{18,... | collective-permute-start | bytes 196616 | tf_op jit(solution)/shard_map/ppermute | solution.py:252
  13.0 3.7 %collective-permute-start.6 = (bf16[256,256]{1,0:T(8,128)(2,1)S(1)}, bf16[256,256]{1,0:T(8,128)(2,1)S(1)}, u32[]{:S(2)}, u32[]{:S(2)}) collective-permute-start(bf16[256,256]{1,0:T(8,128)(2,1)S(1)} %pad_maximum_fusion.1.refs_6_), channel_id=1, source_target_pairs={{0,224},{2,226},{4,228},{6,230},{8,232},{10,234},{12,236},{14,238}... | collective-permute-start | bytes 393224 | tf_op jit(solution)/shard_map/ppermute | solution.py:256
  16.8 3.1 %collective-permute-start.2 = (bf16[256,1024]{1,0:T(8,128)(2,1)S(1)}, bf16[256,1024]{1,0:T(8,128)(2,1)S(1)}, u32[]{:S(2)}, u32[]{:S(2)}) collective-permute-start(bf16[256,1024]{1,0:T(8,128)(2,1)S(1)} %pad_maximum_fusion), channel_id=1, source_target_pairs={{0,6},{2,4},{4,2},{6,0},{8,14},{10,12},{12,10},{14,8},{16,22},{18,... | collective-permute-start | bytes 1572872 | tf_op jit(solution)/shard_map/ppermute | solution.py:258
  20.8 3.2 %collective-permute-start.7 = (bf16[256,256]{1,0:T(8,128)(2,1)S(1)}, bf16[256,256]{1,0:T(8,128)(2,1)S(1)}, u32[]{:S(2)}, u32[]{:S(2)}) collective-permute-start(bf16[256,256]{1,0:T(8,128)(2,1)S(1)} %collective-permute-done.6.refs_8_), channel_id=1, source_target_pairs={{0,32},{2,34},{4,36},{6,38},{8,40},{10,42},{12,44},{14,46},{16,48}... | collective-permute-start | bytes 393224 | tf_op jit(solution)/shard_map/ppermute | solution.py:255
  32.2 3.0 %collective-permute-start.12 = (bf16[128,256]{1,0:T(8,128)(2,1)S(1)}, bf16[128,256]{1,0:T(8,128)(2,1)S(1)}, u32[]{:S(2)}, u32[]{:S(2)}) collective-permute-start(bf16[128,256]{1,0:T(8,128)(2,1)S(1)} %slice.122), channel_id=1, source_target_pairs={{0,32},{2,34},{4,36},{6,38},{8,40},{10,42},{12,44},{14,46},{16,48}... | collective-permute-start | bytes 196616 | tf_op jit(solution)/shard_map/ppermute | solution.py:261
  40.0 3.2 %collective-permute-done.13 = bf16[128,256]{1,0:T(8,128)(2,1)S(1)} collective-permute-done((bf16[128,256]{1,0:T(8,128)(2,1)S(1)}, bf16[128,256]{1,0:T(8,128)(2,1)S(1)}, u32[]{:S(2)}, u32[]{:S(2)}) %collective-permute-start.13) | collective-permute-done | bytes 65568 | tf_op jit(solution)/shard_map/ppermute | solution.py:261
  45.8 7.2 %forward.1 = (f32[2,4,128,512]{3,2,1,0:T(8,128)}, f32[2,12,512]{2,1,0:T(8,128)}) custom-call(s32[16]{0:T(128)} %concatenate.42.sc, s32[2,1,512]{2,1,0:T(1,128)} %bitcast.44, bf16[128,1024]{1,0:T(8,128)(2,1)} %copy-done, bf16[128,1024]{1,0:T(8,128)(2,1)} %copy-done.2, bf16[256,1024]{1,0:T(8,128)(2,1)} %copy-done.18, bf16[256,1024]{1,0:T(8,128)(2,1)} %copy-done.17, ...), custom_call_target="tpu_custom_call" | custom-call | flops 3221225472 | bytes 8388608 | tf_op jit(solution)/shard_map/forward/pallas_call | solution.py:311
  54.4 3.0 %collective-permute-done.14 = f32[2,12,512]{2,1,0:T(8,128)S(1)} collective-permute-done((f32[2,12,512]{2,1,0:T(8,128)}, f32[2,12,512]{2,1,0:T(8,128)S(1)}, u32[]{:S(2)}, u32[]{:S(2)}) %collective-permute-start.14) | collective-permute-done | bytes 49184 | tf_op jit(solution)/shard_map/ppermute | solution.py:323
  58.5 4.2 %collective-permute-start.16 = (f32[2,12,512]{2,1,0:T(8,128)S(1)}, f32[2,12,512]{2,1,0:T(8,128)S(1)}, u32[]{:S(2)}, u32[]{:S(2)}) collective-permute-start(f32[2,12,512]{2,1,0:T(8,128)S(1)} %pad_maximum_fusion.4.refs_10_), channel_id=1, source_target_pairs={{0,4},{2,6},{4,0},{6,2},{8,12},{10,14},{12,8},{14,10},{16,20},{18,... | collective-permute-start | bytes 147464 | tf_op jit(solution)/shard_map/ppermute | solution.py:335
  67.6 8.6 %backward_begin.1 = (bf16[4,2,128,256]{3,2,1,0:T(8,128)(2,1)}, bf16[512,128]{1,0:T(8,128)(2,1)}, bf16[512,128]{1,0:T(8,128)(2,1)}, bf16[512,128]{1,0:T(8,128)(2,...) custom-call(s32[12]{0:T(128)} %concatenate.36.sc, ...), custom_call_target="tpu_custom_call" | custom-call | flops 2684354560 | bytes 8388608 | tf_op jit(solution)/shard_map/backward_begin/pallas_call | solution.py:346
  76.4 4.6 %collective-permute-start.20 = (bf16[512,128]{1,0:T(8,128)(2,1)}, bf16[512,128]{1,0:T(8,128)(2,1)S(1)}, u32[]{:S(2)}, u32[]{:S(2)}) collective-permute-start(bf16[512,128]{1,0:T(8,128)(2,1)} %get-tuple-element.32), channel_id=1, source_target_pairs={{0,6},{2,4},{4,2},{6,0},{8,14},{10,12},{12,10},{14,8},{16,22},{18,... | collective-permute-start | bytes 393224 | tf_op jit(solution)/shard_map/ppermute | solution.py:367
  83.2 6.4 %collective-permute-start.32 = (bf16[128,256]{1,0:T(8,128)(2,1)S(1)}, bf16[128,256]{1,0:T(8,128)(2,1)S(1)}, u32[]{:S(2)}, u32[]{:S(2)}) collective-permute-start(bf16[128,256]{1,0:T(8,128)(2,1)S(1)} %get-tuple-element.59), channel_id=1, source_target_pairs={{0,224},{2,226},{4,228},{6,230},{8,232},{10,234},{12,236},{14,238}... | collective-permute-start | bytes 196616 | tf_op jit(solution)/shard_map/ppermute | solution.py:371
  89.6 4.4 %backward_end.1 = (bf16[4,2,128,256]{3,2,1,0:T(8,128)(2,1)}, bf16[512,128]{1,0:T(8,128)(2,1)}, bf16[512,128]{1,0:T(8,128)(2,1)}, bf16[512,128]{1,0:T(8,128)(2,1)...) custom-call(s32[16]{0:T(128)} %concatenate.42.sc, ...), custom_call_target="tpu_custom_call" | custom-call | flops 2684354560 | bytes 8388608 | tf_op jit(solution)/shard_map/backward_end/pallas_call | solution.py:346
  97.0 3.8 %collective-permute-done.37 = bf16[256,256]{1,0:T(8,128)(2,1)S(1)} collective-permute-done((bf16[256,256]{1,0:T(8,128)(2,1)S(1)}, bf16[256,256]{1,0:T(8,128)(2,1)S(1)}, u32[]{:S(2)}, u32[]{:S(2)}) %collective-permute-start.37) | collective-permute-done | bytes 131104 | tf_op jit(solution)/shard_map/ppermute | solution.py:376
  100.8 9.4 %collective-permute-start.33 = (bf16[256,256]{1,0:T(8,128)(2,1)S(1)}, bf16[256,256]{1,0:T(8,128)(2,1)S(1)}, u32[]{:S(2)}, u32[]{:S(2)}) collective-permute-start(bf16[256,256]{1,0:T(8,128)(2,1)S(1)} %pad_maximum_fusion.2), channel_id=1, source_target_pairs={{0,32},{2,34},{4,36},{6,38},{8,40},{10,42},{12,44},{14,46},{16,48}... | collective-permute-start | bytes 393224 | tf_op jit(solution)/shard_map/ppermute | solution.py:376
  110.2 2.9 %collective-permute-done.33 = bf16[256,256]{1,0:T(8,128)(2,1)S(1)} collective-permute-done((bf16[256,256]{1,0:T(8,128)(2,1)S(1)}, bf16[256,256]{1,0:T(8,128)(2,1)S(1)}, u32[]{:S(2)}, u32[]{:S(2)}) %collective-permute-start.33) | collective-permute-done | bytes 131104 | tf_op jit(solution)/shard_map/ppermute | solution.py:376
  115.3 2.8 %collective-permute-done.38 = bf16[256,256]{1,0:T(8,128)(2,1)S(1)} collective-permute-done((bf16[256,256]{1,0:T(8,128)(2,1)S(1)}, bf16[256,256]{1,0:T(8,128)(2,1)S(1)}, u32[]{:S(2)}, u32[]{:S(2)}) %collective-permute-start.38) | collective-permute-done | bytes 131104 | tf_op jit(solution)/shard_map/ppermute | solution.py:376
  118.2 6.3 %collective-permute-start.23 = (bf16[512,128]{1,0:T(8,128)(2,1)S(1)}, bf16[512,128]{1,0:T(8,128)(2,1)S(1)}, u32[]{:S(2)}, u32[]{:S(2)}) collective-permute-start(bf16[512,128]{1,0:T(8,128)(2,1)S(1)} %copy-done.36), channel_id=1, source_target_pairs={{0,20},{2,22},{4,16},{6,18},{8,28},{10,30},{12,24},{14,26},{16,4},... | collective-permute-start | bytes 393224 | tf_op jit(solution)/shard_map/ppermute | solution.py:367
  124.8 5.6 %collective-permute-start.26 = (bf16[512,128]{1,0:T(8,128)(2,1)S(1)}, bf16[512,128]{1,0:T(8,128)(2,1)S(1)}, u32[]{:S(2)}, u32[]{:S(2)}) collective-permute-start(bf16[512,128]{1,0:T(8,128)(2,1)S(1)} %copy-done.38), channel_id=1, source_target_pairs={{0,4},{2,6},{4,0},{6,2},{8,12},{10,14},{12,8},{14,10},{16,20},{18,... | collective-permute-start | bytes 393224 | tf_op jit(solution)/shard_map/ppermute | solution.py:367
  132.3 3.7 %collective-permute-start.27 = (bf16[512,128]{1,0:T(8,128)(2,1)S(1)}, bf16[512,128]{1,0:T(8,128)(2,1)S(1)}, u32[]{:S(2)}, u32[]{:S(2)}) collective-permute-start(bf16[512,128]{1,0:T(8,128)(2,1)S(1)} %copy-done.34), channel_id=1, source_target_pairs={{0,6},{2,4},{4,2},{6,0},{8,14},{10,12},{12,10},{14,8},{16,22},{18,... | collective-permute-start | bytes 393224 | tf_op jit(solution)/shard_map/ppermute | solution.py:367
  136.7 3.0 %collective-permute-start.30 = (bf16[512,128]{1,0:T(8,128)(2,1)S(1)}, bf16[512,128]{1,0:T(8,128)(2,1)S(1)}, u32[]{:S(2)}, u32[]{:S(2)}) collective-permute-start(bf16[512,128]{1,0:T(8,128)(2,1)S(1)} %copy-done.31), channel_id=1, source_target_pairs={{0,20},{2,22},{4,16},{6,18},{8,28},{10,30},{12,24},{14,26},{16,4},... | collective-permute-start | bytes 393224 | tf_op jit(solution)/shard_map/ppermute | solution.py:367
  139.7 3.8 %collective-permute-start.31 = (bf16[512,128]{1,0:T(8,128)(2,1)S(1)}, bf16[512,128]{1,0:T(8,128)(2,1)S(1)}, u32[]{:S(2)}, u32[]{:S(2)}) collective-permute-start(bf16[512,128]{1,0:T(8,128)(2,1)S(1)} %copy-done.30), channel_id=1, source_target_pairs={{0,22},{2,20},{4,18},{6,16},{8,30},{10,28},{12,26},{14,24},{16,6},... | collective-permute-start | bytes 393224 | tf_op jit(solution)/shard_map/ppermute | solution.py:367
  143.9 2.2 %attended.1 = bf16[128,512]{1,0:T(8,128)(2,1)} custom-call(bf16[512,128]{1,0:T(8,128)(2,1)} %get-tuple-element.29.refs_0_, bf16[512,128]{1,0:T(8,128)(2,1)} %copy-done.3, bf16[512,128]{1,0:T(8,128)(2,1)} %copy-done.4, bf16[512,128]{1,0:T(8,128)(2,1)} %copy-done.5, bf16[512,128]{1,0:T(8,128)(2,1)} %copy-done.6, bf16[512,128]{1,0:T(8,128)(2,1)} %copy-done.7, ...), custom_call_target="tpu_custom_call" | custom-call | tf_op jit(solution)/shard_map/attended/pallas_call | solution.py:383
  148.5 2.1 %grad_query.1 = bf16[128,512]{1,0:T(8,128)(2,1)} custom-call(bf16[512,128]{1,0:T(8,128)(2,1)} %get-tuple-element.40.refs_0_, bf16[512,128]{1,0:T(8,128)(2,1)} %copy-done.8, bf16[512,128]{1,0:T(8,128)(2,1)} %copy-done.10, bf16[512,128]{1,0:T(8,128)(2,1)} %copy-done.12, bf16[512,128]{1,0:T(8,128)(2,1)} %copy-done.13, bf16[512,128]{1,0:T(8,128)(2,1)} %copy-done.14, ...), custom_call_target="tpu_custom_call" | custom-call | tf_op jit(solution)/shard_map/grad_query/pallas_call | solution.py:383
  (200 shorter events, 46.4 us)
Async XLA Ops:
  2.2 10.7 %collective-permute-start.5 = (bf16[128,256]{1,0:T(8,128)(2,1)S(1)}, bf16[128,256]{1,0:T(8,128)(2,1)S(1)}, u32[]{:S(2)}, u32[]{:S(2)}) collective-permute-start(bf16[128,256]{1,0:T(8,128)(2,1)S(1)} %constant_dynamic-update-slice_fusion.3), channel_id=1, source_target_pairs={{0,8},{2,10},{4,12},{6,14},{8,0},{10,2},{12,4},{14,6},{16,24},{18,... | collective-permute-start | bytes 196616 | tf_op jit(solution)/shard_map/ppermute | solution.py:252
  7.1 9.7 %collective-permute-start = (bf16[128,1024]{1,0:T(8,128)(2,1)S(1)}, bf16[128,1024]{1,0:T(8,128)(2,1)S(1)}, u32[]{:S(2)}, u32[]{:S(2)}) collective-permute-start(bf16[128,1024]{1,0:T(8,128)(2,1)S(1)} %constant_dynamic-update-slice_fusion.1.refs_0_), channel_id=1, source_target_pairs={{0,16},{2,18},{4,20},{6,22},{8,24},{10,26},{12,28},{14,30},{16,0},... | collective-permute-start | bytes 786440 | tf_op jit(solution)/shard_map/ppermute | solution.py:251
  12.8 11.9 %collective-permute-start.8 = (bf16[256,256]{1,0:T(8,128)(2,1)S(1)}, bf16[256,256]{1,0:T(8,128)(2,1)S(1)}, u32[]{:S(2)}, u32[]{:S(2)}) collective-permute-start(bf16[256,256]{1,0:T(8,128)(2,1)S(1)} %pad_maximum_fusion.1.refs_6_), channel_id=1, source_target_pairs={{0,32},{2,34},{4,36},{6,38},{8,40},{10,42},{12,44},{14,46},{16,48}... | collective-permute-start | bytes 393224 | tf_op jit(solution)/shard_map/ppermute | solution.py:255
  16.8 18.5 %collective-permute-start.2 = (bf16[256,1024]{1,0:T(8,128)(2,1)S(1)}, bf16[256,1024]{1,0:T(8,128)(2,1)S(1)}, u32[]{:S(2)}, u32[]{:S(2)}) collective-permute-start(bf16[256,1024]{1,0:T(8,128)(2,1)S(1)} %pad_maximum_fusion), channel_id=1, source_target_pairs={{0,6},{2,4},{4,2},{6,0},{8,14},{10,12},{12,10},{14,8},{16,22},{18,... | collective-permute-start | bytes 1572872 | tf_op jit(solution)/shard_map/ppermute | solution.py:258
  19.9 17.4 %collective-permute-start.1 = (bf16[256,1024]{1,0:T(8,128)(2,1)S(1)}, bf16[256,1024]{1,0:T(8,128)(2,1)S(1)}, u32[]{:S(2)}, u32[]{:S(2)}) collective-permute-start(bf16[256,1024]{1,0:T(8,128)(2,1)S(1)} %pad_maximum_fusion), channel_id=1, source_target_pairs={{0,2},{2,0},{4,6},{6,4},{8,10},{10,8},{12,14},{14,12},{16,18},{18,... | collective-permute-start | bytes 1572872 | tf_op jit(solution)/shard_map/ppermute | solution.py:258
  30.2 8.7 %collective-permute-start.10 = (bf16[256,256]{1,0:T(8,128)(2,1)}, bf16[256,256]{1,0:T(8,128)(2,1)S(1)}, u32[]{:S(2)}, u32[]{:S(2)}) collective-permute-start(bf16[256,256]{1,0:T(8,128)(2,1)} %collective-permute-done.9.refs_9_), channel_id=1, source_target_pairs={{0,32},{2,34},{4,36},{6,38},{8,40},{10,42},{12,44},{14,46},{16,48}... | collective-permute-start | bytes 393224 | tf_op jit(solution)/shard_map/ppermute | solution.py:255
  76.2 39.0 %collective-permute-start.18 = (bf16[512,128]{1,0:T(8,128)(2,1)}, bf16[512,128]{1,0:T(8,128)(2,1)S(1)}, u32[]{:S(2)}, u32[]{:S(2)}) collective-permute-start(bf16[512,128]{1,0:T(8,128)(2,1)} %get-tuple-element.30), channel_id=1, source_target_pairs={{0,2},{2,0},{4,6},{6,4},{8,10},{10,8},{12,14},{14,12},{16,18},{18,... | collective-permute-start | bytes 393224 | tf_op jit(solution)/shard_map/ppermute | solution.py:367
  76.3 41.9 %collective-permute-start.19 = (bf16[512,128]{1,0:T(8,128)(2,1)}, bf16[512,128]{1,0:T(8,128)(2,1)S(1)}, u32[]{:S(2)}, u32[]{:S(2)}) collective-permute-start(bf16[512,128]{1,0:T(8,128)(2,1)} %get-tuple-element.31), channel_id=1, source_target_pairs={{0,4},{2,6},{4,0},{6,2},{8,12},{10,14},{12,8},{14,10},{16,20},{18,... | collective-permute-start | bytes 393224 | tf_op jit(solution)/shard_map/ppermute | solution.py:367
  76.4 48.2 %collective-permute-start.20 = (bf16[512,128]{1,0:T(8,128)(2,1)}, bf16[512,128]{1,0:T(8,128)(2,1)S(1)}, u32[]{:S(2)}, u32[]{:S(2)}) collective-permute-start(bf16[512,128]{1,0:T(8,128)(2,1)} %get-tuple-element.32), channel_id=1, source_target_pairs={{0,6},{2,4},{4,2},{6,0},{8,14},{10,12},{12,10},{14,8},{16,22},{18,... | collective-permute-start | bytes 393224 | tf_op jit(solution)/shard_map/ppermute | solution.py:367
  81.9 12.2 %collective-permute-start.36 = (bf16[128,256]{1,0:T(8,128)(2,1)S(1)}, bf16[128,256]{1,0:T(8,128)(2,1)S(1)}, u32[]{:S(2)}, u32[]{:S(2)}) collective-permute-start(bf16[128,256]{1,0:T(8,128)(2,1)S(1)} %get-tuple-element.58), channel_id=1, source_target_pairs={{0,32},{2,34},{4,36},{6,38},{8,40},{10,42},{12,44},{14,46},{16,48}... | collective-permute-start | bytes 196616 | tf_op jit(solution)/shard_map/ppermute | solution.py:370
  83.2 12.5 %collective-permute-start.32 = (bf16[128,256]{1,0:T(8,128)(2,1)S(1)}, bf16[128,256]{1,0:T(8,128)(2,1)S(1)}, u32[]{:S(2)}, u32[]{:S(2)}) collective-permute-start(bf16[128,256]{1,0:T(8,128)(2,1)S(1)} %get-tuple-element.59), channel_id=1, source_target_pairs={{0,224},{2,226},{4,228},{6,230},{8,232},{10,234},{12,236},{14,238}... | collective-permute-start | bytes 196616 | tf_op jit(solution)/shard_map/ppermute | solution.py:371
  94.1 30.5 %collective-permute-start.21 = (bf16[512,128]{1,0:T(8,128)(2,1)S(1)}, bf16[512,128]{1,0:T(8,128)(2,1)S(1)}, u32[]{:S(2)}, u32[]{:S(2)}) collective-permute-start(bf16[512,128]{1,0:T(8,128)(2,1)S(1)} %copy-done.39), channel_id=1, source_target_pairs={{0,16},{2,18},{4,20},{6,22},{8,24},{10,26},{12,28},{14,30},{16,0},... | collective-permute-start | bytes 393224 | tf_op jit(solution)/shard_map/ppermute | solution.py:367
  100.8 12.4 %collective-permute-start.33 = (bf16[256,256]{1,0:T(8,128)(2,1)S(1)}, bf16[256,256]{1,0:T(8,128)(2,1)S(1)}, u32[]{:S(2)}, u32[]{:S(2)}) collective-permute-start(bf16[256,256]{1,0:T(8,128)(2,1)S(1)} %pad_maximum_fusion.2), channel_id=1, source_target_pairs={{0,32},{2,34},{4,36},{6,38},{8,40},{10,42},{12,44},{14,46},{16,48}... | collective-permute-start | bytes 393224 | tf_op jit(solution)/shard_map/ppermute | solution.py:376
  115.2 9.5 %collective-permute-start.22 = (bf16[512,128]{1,0:T(8,128)(2,1)S(1)}, bf16[512,128]{1,0:T(8,128)(2,1)S(1)}, u32[]{:S(2)}, u32[]{:S(2)}) collective-permute-start(bf16[512,128]{1,0:T(8,128)(2,1)S(1)} %copy-done.37), channel_id=1, source_target_pairs={{0,18},{2,16},{4,22},{6,20},{8,26},{10,24},{12,30},{14,28},{16,2},... | collective-permute-start | bytes 393224 | tf_op jit(solution)/shard_map/ppermute | solution.py:367
  118.1 12.3 %collective-permute-start.34 = (bf16[256,256]{1,0:T(8,128)(2,1)S(1)}, bf16[256,256]{1,0:T(8,128)(2,1)S(1)}, u32[]{:S(2)}, u32[]{:S(2)}) collective-permute-start(bf16[256,256]{1,0:T(8,128)(2,1)S(1)} %fusion.2), channel_id=1, source_target_pairs={{0,224},{2,226},{4,228},{6,230},{8,232},{10,234},{12,236},{14,238}... | collective-permute-start | bytes 393224 | tf_op jit(solution)/shard_map/ppermute | solution.py:376
  118.2 12.2 %collective-permute-start.23 = (bf16[512,128]{1,0:T(8,128)(2,1)S(1)}, bf16[512,128]{1,0:T(8,128)(2,1)S(1)}, u32[]{:S(2)}, u32[]{:S(2)}) collective-permute-start(bf16[512,128]{1,0:T(8,128)(2,1)S(1)} %copy-done.36), channel_id=1, source_target_pairs={{0,20},{2,22},{4,16},{6,18},{8,28},{10,30},{12,24},{14,26},{16,4},... | collective-permute-start | bytes 393224 | tf_op jit(solution)/shard_map/ppermute | solution.py:367
  124.7 11.3 %collective-permute-start.25 = (bf16[512,128]{1,0:T(8,128)(2,1)S(1)}, bf16[512,128]{1,0:T(8,128)(2,1)S(1)}, u32[]{:S(2)}, u32[]{:S(2)}) collective-permute-start(bf16[512,128]{1,0:T(8,128)(2,1)S(1)} %copy-done.40), channel_id=1, source_target_pairs={{0,2},{2,0},{4,6},{6,4},{8,10},{10,8},{12,14},{14,12},{16,18},{18,... | collective-permute-start | bytes 393224 | tf_op jit(solution)/shard_map/ppermute | solution.py:367
  124.8 11.5 %collective-permute-start.26 = (bf16[512,128]{1,0:T(8,128)(2,1)S(1)}, bf16[512,128]{1,0:T(8,128)(2,1)S(1)}, u32[]{:S(2)}, u32[]{:S(2)}) collective-permute-start(bf16[512,128]{1,0:T(8,128)(2,1)S(1)} %copy-done.38), channel_id=1, source_target_pairs={{0,4},{2,6},{4,0},{6,2},{8,12},{10,14},{12,8},{14,10},{16,20},{18,... | collective-permute-start | bytes 393224 | tf_op jit(solution)/shard_map/ppermute | solution.py:367
  130.5 9.2 %collective-permute-start.35 = (bf16[256,256]{1,0:T(8,128)(2,1)S(1)}, bf16[256,256]{1,0:T(8,128)(2,1)S(1)}, u32[]{:S(2)}, u32[]{:S(2)}) collective-permute-start(bf16[256,256]{1,0:T(8,128)(2,1)S(1)} %fusion.3), channel_id=1, source_target_pairs={{0,32},{2,34},{4,36},{6,38},{8,40},{10,42},{12,44},{14,46},{16,48}... | collective-permute-start | bytes 393224 | tf_op jit(solution)/shard_map/ppermute | solution.py:378
  132.3 11.3 %collective-permute-start.27 = (bf16[512,128]{1,0:T(8,128)(2,1)S(1)}, bf16[512,128]{1,0:T(8,128)(2,1)S(1)}, u32[]{:S(2)}, u32[]{:S(2)}) collective-permute-start(bf16[512,128]{1,0:T(8,128)(2,1)S(1)} %copy-done.34), channel_id=1, source_target_pairs={{0,6},{2,4},{4,2},{6,0},{8,14},{10,12},{12,10},{14,8},{16,22},{18,... | collective-permute-start | bytes 393224 | tf_op jit(solution)/shard_map/ppermute | solution.py:367
  136.0 10.0 %collective-permute-start.28 = (bf16[512,128]{1,0:T(8,128)(2,1)S(1)}, bf16[512,128]{1,0:T(8,128)(2,1)S(1)}, u32[]{:S(2)}, u32[]{:S(2)}) collective-permute-start(bf16[512,128]{1,0:T(8,128)(2,1)S(1)} %copy-done.33), channel_id=1, source_target_pairs={{0,16},{2,18},{4,20},{6,22},{8,24},{10,26},{12,28},{14,30},{16,0},... | collective-permute-start | bytes 393224 | tf_op jit(solution)/shard_map/ppermute | solution.py:367
  136.3 9.7 %collective-permute-start.29 = (bf16[512,128]{1,0:T(8,128)(2,1)S(1)}, bf16[512,128]{1,0:T(8,128)(2,1)S(1)}, u32[]{:S(2)}, u32[]{:S(2)}) collective-permute-start(bf16[512,128]{1,0:T(8,128)(2,1)S(1)} %copy-done.32), channel_id=1, source_target_pairs={{0,18},{2,16},{4,22},{6,20},{8,26},{10,24},{12,30},{14,28},{16,2},... | collective-permute-start | bytes 393224 | tf_op jit(solution)/shard_map/ppermute | solution.py:367
  136.7 9.4 %collective-permute-start.30 = (bf16[512,128]{1,0:T(8,128)(2,1)S(1)}, bf16[512,128]{1,0:T(8,128)(2,1)S(1)}, u32[]{:S(2)}, u32[]{:S(2)}) collective-permute-start(bf16[512,128]{1,0:T(8,128)(2,1)S(1)} %copy-done.31), channel_id=1, source_target_pairs={{0,20},{2,22},{4,16},{6,18},{8,28},{10,30},{12,24},{14,26},{16,4},... | collective-permute-start | bytes 393224 | tf_op jit(solution)/shard_map/ppermute | solution.py:367
  139.7 8.1 %collective-permute-start.31 = (bf16[512,128]{1,0:T(8,128)(2,1)S(1)}, bf16[512,128]{1,0:T(8,128)(2,1)S(1)}, u32[]{:S(2)}, u32[]{:S(2)}) collective-permute-start(bf16[512,128]{1,0:T(8,128)(2,1)S(1)} %copy-done.30), channel_id=1, source_target_pairs={{0,22},{2,20},{4,18},{6,16},{8,30},{10,28},{12,26},{14,24},{16,6},... | collective-permute-start | bytes 393224 | tf_op jit(solution)/shard_map/ppermute | solution.py:367
  (61 other events, 846.5 us)

commit v2 on v1

--- a/solution.py
+++ b/solution.py
@@ -16,6 +16,7 @@
 ROWS = SLOTS * CHUNK
 PAIR = 2 * CHUNK
 PLANE = 16 * CHUNK
+DOCS = 8
 NEG = -1e30
 FLOOR = -1e29
 LOG2E = math.log2(math.e)
@@ -65,26 +66,42 @@
             t_s[block, :, at] = jnp.transpose(part[:, which * width : (which + 1) * width])
 
 
+def start_of(sc, row):
+    start = 0
+    for n in range(DOCS):
+        one = sc[4 + n]
+        start = jnp.maximum(start, jnp.where(one <= row, one, 0))
+    return start
+
+
 def place(sc, pair, u, t):
     z, x_lo, x_hi, y = (sc[n] for n in range(4))
     plane = (4 * (x_hi ^ u) + y) * PLANE + x_lo * CHUNK
-    one, two = plane + sc[8 + 2 * pair] * PAIR, plane + sc[9 + 2 * pair] * PAIR
+    one, two = (plane + sc[4 + DOCS + 2 * pair + n] * PAIR for n in range(2))
     row = ((z * 4 + x_lo * 2 + x_hi) ^ (2 * t)) * ROWS
-    first, last = sc[4 + 2 * t], sc[5 + 2 * t]
     low, high = jnp.minimum(one, two), jnp.maximum(one, two)
-    needed = (low <= row + ROWS - 1) & (high + CHUNK - 1 >= first)
-    whole = (high + CHUNK - 1 <= row) & (low >= last)
+    needed = (low <= row + ROWS - 1) & (high + CHUNK - 1 >= start_of(sc, row))
+    whole = (high + CHUNK - 1 <= row) & (low >= start_of(sc, row + ROWS - 1))
     return one, two, row, needed, whole
 
 
-def allowed_of(sc, start, one, two, row):
+def allowed_of(sc, one, two, row):
     index = lax.broadcasted_iota(jnp.int32, (PAIR, 1), 0)
     key_at = index + jnp.where(index < CHUNK, one, two - CHUNK)
     row_at = row + (lax.broadcasted_iota(jnp.int32, (1, ROWS), 1) ^ (sc[3] * CHUNK))
-    return (key_at >= start) & (key_at <= row_at)
-
-
-def forward(group, width, pairs, sc, start, *refs):
+    return (key_at >= start_of(sc, row_at)) & (key_at <= row_at)
+
+
+def pack(query, key, value, dout, rows, keys):
+    width = query.shape[1]
+    rows[:, :width] = query[...]
+    rows[:, width:] = dout[...]
+    width = key.shape[1]
+    keys[:, :width] = key[...]
+    keys[:, width:] = value[...]
+
+
+def forward(group, width, pairs, sc, *refs):
     rows, keys, refs = refs[:6], refs[6 : 6 + 2 * pairs], refs[6 + 2 * pairs :]
     acc, stat, q_s, do_s, k_s, v_s, t_s, high, total, mixed = refs
     unit = LOG2E / math.sqrt(width)
@@ -99,7 +116,7 @@
         scores = [dot_t(k_s[b], q_s[t, h]) for h in heads]
         dprobs = [dot_t(v_s[b], do_s[t, h]) for h in heads]
         if masked:
-            allowed = allowed_of(sc, start[t], one, two, row)
+            allowed = allowed_of(sc, one, two, row)
             scores = [jnp.where(allowed, s, NEG) for s in scores]
         olds = [high[t, h] for h in heads]
         news = [jnp.maximum(o, jnp.max(s, axis=0, keepdims=True)) for o, s in zip(olds, scores)]
@@ -139,7 +156,7 @@
             stat[t, 2 * group + h : 2 * group + h + 1, :] = mixed[t, h]
 
 
-def backward(group, width, pairs, begins, ends, sc, start, *refs):
+def backward(group, width, pairs, begins, ends, sc, *refs):
     rows, keys, refs = refs[:6], refs[6 : 6 + 2 * pairs], refs[6 + 2 * pairs :]
     scale = 1.0 / math.sqrt(width)
     unit = LOG2E * scale
@@ -150,9 +167,9 @@
         acc_in, lse_in, delta_in, refs = *refs[:3], refs[3:]
     dkv, refs = refs[0], refs[1:]
     if begins:
-        mixed, refs = refs[: TILES * SLOTS], refs[TILES * SLOTS :]
+        mixed, refs = refs[:SLOTS], refs[SLOTS:]
     if ends:
-        dq, refs = refs[: TILES * SLOTS], refs[TILES * SLOTS :]
+        dq, refs = refs[:SLOTS], refs[SLOTS:]
     acc, lse, delta, q_s, do_s, k_s, v_s, t_s, grads = refs
     fill(rows, keys, q_s, do_s, k_s, v_s, t_s, group, width, 0)
     if begins:
@@ -170,7 +187,7 @@
                 for h in heads:
                     lse[t, h, :, at] = low[h : h + 1]
                     delta[t, h, :, at] = small[h : h + 1]
-                    mixed[t * SLOTS + u][h * width : (h + 1) * width, :] = (
+                    mixed[u][t, h * width : (h + 1) * width, :] = (
                         values[t, h, :, at] * part[h : h + 1]
                     ).astype(BF16)
     else:
@@ -182,7 +199,7 @@
         scores = [dot_t(k_s[b], q_s[t, h]) for h in heads]
         dprobs = [dot_t(v_s[b], do_s[t, h]) for h in heads]
         if masked:
-            allowed = allowed_of(sc, start[t], one, two, row)
+            allowed = allowed_of(sc, one, two, row)
             scores = [jnp.where(allowed, s, NEG) for s in scores]
         probs = [jnp.exp2(scores[h] * unit - lse[t, h]) for h in heads]
         dscores = [(probs[h] * (dprobs[h] - delta[t, h])).astype(BF16) for h in heads]
@@ -222,7 +239,7 @@
             for h in heads:
                 value = (acc[t, h] * scale).astype(BF16)
                 for s in range(SLOTS):
-                    dq[t * SLOTS + s][h * width : (h + 1) * width, :] = value[
+                    dq[s][t, h * width : (h + 1) * width, :] = value[
                         :, s * CHUNK : (s + 1) * CHUNK
                     ]
 
@@ -246,8 +263,14 @@
     qrow, kcol = lax.axis_index("qrow"), lax.axis_index("kcol")
     z, x_lo, x_hi, y = qrow // 2, qrow % 2, kcol // 4, kcol % 4
 
-    key_home = jnp.concatenate([key, value], axis=1)
-    row_home = jnp.concatenate([query, dout], axis=1)
+    row_home, key_home = pl.pallas_call(
+        pack,
+        out_shape=[
+            jax.ShapeDtypeStruct((CHUNK, 2 * group * width), BF16),
+            jax.ShapeDtypeStruct((CHUNK, 2 * width), BF16),
+        ],
+        name="pack",
+    )(query, key, value, dout)
     row_other = send(row_home, perm=X_LO)
     own = jnp.concatenate([key_home, send(key_home, perm=X_HI)], axis=0)
     a, b = [own], [own]
@@ -263,27 +286,11 @@
     rows = [row_home, row_other, near, last, far_own, far_other]
     keys = [a[0], a[1], b[1], b[2], a[2], a[3], b[3], opposite]
 
-    numbers = jnp.arange(8, dtype=jnp.int32)
+    numbers = jnp.arange(DOCS, dtype=jnp.int32)
     starts = jnp.sum((document[None, :] < numbers[:, None]).astype(jnp.int32), axis=1)
-    place_of = qrow * 8 + kcol
-    row_doc = jnp.concatenate(
-        [
-            lax.dynamic_slice_in_dim(document, (place_of ^ (8 * t + s)) * CHUNK, CHUNK)
-            for t in range(TILES)
-            for s in range(SLOTS)
-        ]
-    )
-    start = jnp.sum(jnp.where(row_doc[None] == numbers[:, None], starts[:, None], 0), axis=0)
-    start = start.reshape(TILES, 1, ROWS)
     side = 1 - 2 * (z % 2)
     sources = jnp.stack([z + side * k for k in (0, 1, -1, -2, 2, 3, -3, 4)]) & 7
-    sc = jnp.concatenate(
-        [
-            jnp.stack([z, x_lo, x_hi, y]),
-            jnp.stack([jnp.min(start, axis=(1, 2)), jnp.max(start, axis=(1, 2))], 1).reshape(-1),
-            sources,
-        ]
-    ).astype(jnp.int32)
+    sc = jnp.concatenate([jnp.stack([z, x_lo, x_hi, y]), starts, sources]).astype(jnp.int32)
 
     smem = pl.BlockSpec(memory_space=pltpu.SMEM)
     vmem = pl.BlockSpec(memory_space=pltpu.VMEM)
@@ -306,18 +313,18 @@
     acc_shape = jax.ShapeDtypeStruct((TILES, group, width, ROWS), F32)
     line_shape = jax.ShapeDtypeStruct(line, F32)
     stat_shape = jax.ShapeDtypeStruct((TILES, 3 * group, ROWS), F32)
-    piece = jax.ShapeDtypeStruct((group * width, CHUNK), BF16)
+    piece = jax.ShapeDtypeStruct((TILES, group * width, CHUNK), BF16)
 
     values, stat = pl.pallas_call(
         functools.partial(forward, group, width, 4),
         out_shape=[acc_shape, stat_shape],
-        in_specs=[smem] + [vmem] * 15,
+        in_specs=[smem] + [vmem] * 14,
         out_specs=[vmem] * 2,
         scratch_shapes=scratch(4) + [pltpu.VMEM(line, F32)] * 3,
         compiler_params=params,
         cost_estimate=cost(3, 4),
         name="forward",
-    )(sc, start, *rows, *keys)
+    )(sc, *rows, *keys)
 
     unit = LOG2E / math.sqrt(width)
     other = send(stat, perm=X_LO)[::-1]
@@ -336,7 +343,7 @@
 
     def back(pairs, begins, ends, sc, keys, *more):
         dkv_shape = jax.ShapeDtypeStruct((2 * pairs, 2, CHUNK, 2 * width), BF16)
-        shapes = [dkv_shape] + [piece] * (TILES * SLOTS * (begins + ends))
+        shapes = [dkv_shape] + [piece] * (SLOTS * (begins + ends))
         carried = [acc_shape, line_shape, line_shape]
         more_scratch = scratch(pairs) + [pltpu.VMEM((PAIR, 2 * width), F32)]
         if ends:
@@ -346,44 +353,45 @@
         return pl.pallas_call(
             functools.partial(backward, group, width, pairs, begins, ends),
             out_shape=shapes,
-            in_specs=[smem] + [vmem] * (7 + 2 * pairs + len(more)),
+            in_specs=[smem] + [vmem] * (6 + 2 * pairs + len(more)),
             out_specs=[vmem] * len(shapes),
             scratch_shapes=more_scratch,
             compiler_params=params,
             cost_estimate=cost(5, pairs),
             name="backward_begin" if begins else "backward_end",
-        )(sc, start, *rows, *keys, *more)
+        )(sc, *rows, *keys, *more)
 
     def shifted(skip):
-        return jnp.concatenate([sc[:8], sc[8 + skip :]])
+        return jnp.concatenate([sc[: 4 + DOCS], sc[4 + DOCS + skip :]])
 
     late = back(2, True, False, shifted(4), keys[4:], *stats, stat, values)
-    far, mixed, carried = late[0], late[1 : 1 + TILES * SLOTS], late[1 + TILES * SLOTS :]
+    far, mixed, carried = late[0], late[1 : 1 + SLOTS], late[1 + SLOTS :]
     end = back(2, False, True, sc, keys[:4], *carried)
     close, dq = end[0], end[1:]
 
-    def spread(parts):
-        masks = [8 * t + s for t in range(TILES) for s in range(SLOTS)]
-        return [parts[0]] + [send(p, perm=flip(m)) for p, m in zip(parts[1:], masks[1:])]
+    def over_y(parts):
+        return add(parts[0], *[send(parts[s], perm=Y[s]) for s in range(1, SLOTS)])
 
     flat = (PAIR, 2 * width)
     one = send(far[3, 0], perm=EVEN)
     two = send(far[3, 1], perm=ODD)
-    mixed = spread(mixed)
+    mixed = over_y(mixed)
+    mixed = [mixed[0], send(mixed[1], perm=X_LO)]
     gb = jnp.concatenate([add(far[2, 0], one), far[2, 1]], axis=0)
     ga = jnp.concatenate([far[1, 0], add(far[1, 1], two)], axis=0)
     for pa, pb in ((far[0], close[3]), (close[1], close[2])):
         sent_b, sent_a = send(gb, perm=ODD), send(ga, perm=EVEN)
         ga, gb = add(pa.reshape(flat), sent_b), add(pb.reshape(flat), sent_a)
     grad = add(close[0].reshape(flat), send(ga, perm=EVEN), send(gb, perm=ODD))
-    dq = spread(dq)
+    dq = over_y(dq)
+    dq = [dq[0], send(dq[1], perm=X_LO)]
     grad = add(grad[:CHUNK], send(grad[CHUNK:], perm=X_HI))
 
     outs = [
         pl.pallas_call(
             functools.partial(combine, group, width),
             out_shape=jax.ShapeDtypeStruct((CHUNK, group * width), BF16),
-            in_specs=[vmem] * (TILES * SLOTS),
+            in_specs=[vmem] * TILES,
             out_specs=vmem,
             name=name,
         )(*parts)

time: 152 us -> 146 us (0.961)
  local copies, waits for them, and re-layouts: 15.9 us -> 10.1 us
  waiting for transfers between devices: 27 us -> 32 us
  Pallas kernels: 24.5 us -> 20.5 us
    ppermute x14 -> x8, starting transfers between devices: 29.7 us -> 18.4 us  [the longest x6 15.7 us: over_y(): return add(parts[0], *[send(parts[s], perm=Y[s]) for s in range(1, SLOTS)])]
    unnamed x98 -> x51, local copies, waits for them, and re-layouts: 9.12 us -> 4.53 us
    ppermute x1, starting transfers between devices: 0.22 us -> 4.38 us  [local(): grad = add(grad[:CHUNK], send(grad[CHUNK:], perm=X_HI))]
    ppermute x1, starting transfers between devices: 6.42 us -> 2.27 us  [local(): two = send(far[3, 1], perm=ODD)]
    ppermute x14 -> x8, waiting for transfers between devices: 3.49 us -> 0.02 us  [the longest x6 0.02 us: over_y(): return add(parts[0], *[send(parts[s], perm=Y[s]) for s in range(1, SLOTS)])]
    ppermute x1, starting transfers between devices: 1.23 us -> 4.32 us  [local(): one = send(far[3, 0], perm=EVEN)]
    ppermute x2, starting transfers between devices: 0.1 us -> 3.15 us  [local(): grad = add(close[0].reshape(flat), send(ga, perm=EVEN), send(gb, perm=ODD))]
    ppermute x3, waiting for transfers between devices: 2.14 us -> 5.09 us  [local(): b.append(send(a[k], perm=ODD))]
  transfers between devices with their start and end apart: 41 -> 35, of which waited for: 13 -> 14; matrix products, arithmetic and copies ran while one was open for 9% -> 5% of each run, Pallas kernels for 6% -> 6%
where the time goes in v2:
time: 146 us
  starting transfers between devices  80.5 us (55%)
  waiting for transfers between devices  32 us (22%)
  Pallas kernels  20.5 us (14%)
  local copies, waits for them, and re-layouts  10.1 us (7%)
  other arithmetic  1.74 us (1%)
    ppermute x6, starting transfers between devices, over_y(): return add(parts[0], *[send(parts[s], perm=Y[s]) for s in range(1, SLOTS)])  15.7 us
    ppermute x4, starting transfers between devices, local(): sent_b, sent_a = (send(gb, perm=ODD), send(ga, perm=EVEN))  11.3 us
    pallas_call x2, Pallas kernels, back(): pl.pallas_call(functools.partial(backward, group, width, pairs, begins, e...  10.5 us
    ppermute x4, waiting for transfers between devices, local(): sent_b, sent_a = (send(gb, perm=ODD), send(ga, perm=EVEN))  8.65 us
    ppermute x3, starting transfers between devices, local(): b.append(send(a[k], perm=ODD))  6.79 us
    ppermute x3, starting transfers between devices, local(): a.append(send(b[k], perm=EVEN))  5.93 us
    ppermute x3, starting transfers between devices, local(): stats = [merged] + [send(merged, perm=Y[s]) for s in range(1, SLOTS)]  5.68 us
    ppermute x3, waiting for transfers between devices, local(): b.append(send(a[k], perm=ODD))  5.09 us
  transfers between devices with their start and end apart: 35, of which 14 were waited for; matrix products, arithmetic and copies ran while one was open for 5% of the time, Pallas kernels for 6%

profile of v2, /device:TPU:32, one launch (start us, length us, event | category | flops | bytes accessed | tf_op | source)
XLA Modules:
  0.0 145.8 jit_solution(11801071350132576648)
XLA Ops:
  3.9 2.7 %collective-permute-start.5 = (bf16[128,256]{1,0:T(8,128)(2,1)}, bf16[128,256]{1,0:T(8,128)(2,1)S(1)}, u32[]{:S(2)}, u32[]{:S(2)}) collective-permute-start(bf16[128,256]{1,0:T(8,128)(2,1)} %get-tuple-element.22), channel_id=1, source_target_pairs={{0,8},{2,10},{4,12},{6,14},{8,0},{10,2},{12,4},{14,6},{16,24},{18,... | collective-permute-start | bytes 196616 | tf_op jit(solution)/shard_map/ppermute | solution.py:275
  8.5 2.9 %collective-permute-done.refs_1_ = bf16[128,1024]{1,0:T(8,128)(2,1)S(1)} collective-permute-done((bf16[128,1024]{1,0:T(8,128)(2,1)}, bf16[128,1024]{1,0:T(8,128)(2,1)S(1)}, u32[]{:S(2)}, u32[]{:S(2)}) %collective-permute-start) | collective-permute-done | bytes 262176 | tf_op jit(solution)/shard_map/ppermute | solution.py:274
  11.4 3.1 %collective-permute-start.2 = (bf16[256,1024]{1,0:T(8,128)(2,1)S(1)}, bf16[256,1024]{1,0:T(8,128)(2,1)S(1)}, u32[]{:S(2)}, u32[]{:S(2)}) collective-permute-start(bf16[256,1024]{1,0:T(8,128)(2,1)S(1)} %constant_dynamic-update-slice_fusion), channel_id=1, source_target_pairs={{0,6},{2,4},{4,2},{6,0},{8,14},{10,12},{12,10},{14,8},{16,22},{18,... | collective-permute-start | bytes 1572872 | tf_op jit(solution)/shard_map/ppermute | solution.py:281
  14.9 3.7 %collective-permute-start.6 = (bf16[256,256]{1,0:T(8,128)(2,1)S(1)}, bf16[256,256]{1,0:T(8,128)(2,1)S(1)}, u32[]{:S(2)}, u32[]{:S(2)}) collective-permute-start(bf16[256,256]{1,0:T(8,128)(2,1)S(1)} %constant_dynamic-update-slice_fusion.2.refs_6_), channel_id=1, source_target_pairs={{0,224},{2,226},{4,228},{6,230},{8,232},{10,234},{12,236},{14,238}... | collective-permute-start | bytes 393224 | tf_op jit(solution)/shard_map/ppermute | solution.py:279
  22.9 2.8 %collective-permute-start.7 = (bf16[256,256]{1,0:T(8,128)(2,1)S(1)}, bf16[256,256]{1,0:T(8,128)(2,1)S(1)}, u32[]{:S(2)}, u32[]{:S(2)}) collective-permute-start(bf16[256,256]{1,0:T(8,128)(2,1)S(1)} %collective-permute-done.6.refs_8_), channel_id=1, source_target_pairs={{0,32},{2,34},{4,36},{6,38},{8,40},{10,42},{12,44},{14,46},{16,48}... | collective-permute-start | bytes 393224 | tf_op jit(solution)/shard_map/ppermute | solution.py:278
  25.8 3.0 %collective-permute-start.10 = (bf16[256,256]{1,0:T(8,128)(2,1)}, bf16[256,256]{1,0:T(8,128)(2,1)S(1)}, u32[]{:S(2)}, u32[]{:S(2)}) collective-permute-start(bf16[256,256]{1,0:T(8,128)(2,1)} %collective-permute-done.9.refs_9_), channel_id=1, source_target_pairs={{0,32},{2,34},{4,36},{6,38},{8,40},{10,42},{12,44},{14,46},{16,48}... | collective-permute-start | bytes 393224 | tf_op jit(solution)/shard_map/ppermute | solution.py:278
  31.0 3.8 %collective-permute-done.11.refs_12_.refs_8_ = bf16[256,256]{1,0:T(8,128)(2,1)S(1)} collective-permute-done((bf16[256,256]{1,0:T(8,128)(2,1)S(1)}, bf16[256,256]{1,0:T(8,128)(2,1)S(1)}, u32[]{:S(2)}, u32[]{:S(2)}) %collective-permute-start.11) | collective-permute-done | bytes 131104 | tf_op jit(solution)/shard_map/ppermute | solution.py:279
  34.9 3.2 %collective-permute-start.12 = (bf16[128,256]{1,0:T(8,128)(2,1)S(1)}, bf16[128,256]{1,0:T(8,128)(2,1)S(1)}, u32[]{:S(2)}, u32[]{:S(2)}) collective-permute-start(bf16[128,256]{1,0:T(8,128)(2,1)S(1)} %slice.138), channel_id=1, source_target_pairs={{0,32},{2,34},{4,36},{6,38},{8,40},{10,42},{12,44},{14,46},{16,48}... | collective-permute-start | bytes 196616 | tf_op jit(solution)/shard_map/ppermute | solution.py:284
  43.5 3.2 %collective-permute-done.13 = bf16[128,256]{1,0:T(8,128)(2,1)S(1)} collective-permute-done((bf16[128,256]{1,0:T(8,128)(2,1)S(1)}, bf16[128,256]{1,0:T(8,128)(2,1)S(1)}, u32[]{:S(2)}, u32[]{:S(2)}) %collective-permute-start.13) | collective-permute-done | bytes 65568 | tf_op jit(solution)/shard_map/ppermute | solution.py:284
  48.4 4.8 %forward.1 = (f32[2,4,128,512]{3,2,1,0:T(8,128)}, f32[2,12,512]{2,1,0:T(8,128)}) custom-call(s32[20]{0:T(128)} %concatenate.30.sc, bf16[128,1024]{1,0:T(8,128)(2,1)} %get-tuple-element.21.refs_0_, bf16[128,1024]{1,0:T(8,128)(2,1)} %copy-done.3, bf16[256,1024]{1,0:T(8,128)(2,1)} %copy-done.7, bf16[256,1024]{1,0:T(8,128)(2,1)} %copy-done.6, ...), custom_call_target="tpu_custom_call" | custom-call | flops 3221225472 | bytes 8388608 | tf_op jit(solution)/shard_map/forward/pallas_call | solution.py:318
  53.2 3.1 %collective-permute-start.14 = (f32[2,12,512]{2,1,0:T(8,128)}, f32[2,12,512]{2,1,0:T(8,128)S(1)}, u32[]{:S(2)}, u32[]{:S(2)}) collective-permute-start(f32[2,12,512]{2,1,0:T(8,128)} %get-tuple-element.23.refs_14_), channel_id=1, source_target_pairs={{0,16},{2,18},{4,20},{6,22},{8,24},{10,26},{12,28},{14,30},{16,0},... | collective-permute-start | bytes 147464 | tf_op jit(solution)/shard_map/ppermute | solution.py:330
  56.3 2.5 %collective-permute-done.14 = f32[2,12,512]{2,1,0:T(8,128)S(1)} collective-permute-done((f32[2,12,512]{2,1,0:T(8,128)}, f32[2,12,512]{2,1,0:T(8,128)S(1)}, u32[]{:S(2)}, u32[]{:S(2)}) %collective-permute-start.14) | collective-permute-done | bytes 49184 | tf_op jit(solution)/shard_map/ppermute | solution.py:330
  60.3 5.1 %collective-permute-start.16 = (f32[2,12,512]{2,1,0:T(8,128)S(1)}, f32[2,12,512]{2,1,0:T(8,128)S(1)}, u32[]{:S(2)}, u32[]{:S(2)}) collective-permute-start(f32[2,12,512]{2,1,0:T(8,128)S(1)} %pad_maximum_fusion.2.refs_10_), channel_id=1, source_target_pairs={{0,4},{2,6},{4,0},{6,2},{8,12},{10,14},{12,8},{14,10},{16,20},{18,... | collective-permute-start | bytes 147464 | tf_op jit(solution)/shard_map/ppermute | solution.py:342
  70.3 5.8 %backward_begin.1 = (bf16[4,2,128,256]{3,2,1,0:T(8,128)(2,1)}, bf16[2,512,128]{2,1,0:T(8,128)(2,1)}, bf16[2,512,128]{2,1,0:T(8,128)(2,1)}, bf16[2,512,128]{2,1,0...) custom-call(s32[16]{0:T(128)} %concatenate.26.sc, ...), custom_call_target="tpu_custom_call" | custom-call | flops 2684354560 | bytes 8388608 | tf_op jit(solution)/shard_map/backward_begin/pallas_call | solution.py:353
  77.0 4.3 %collective-permute-start.30 = (bf16[128,256]{1,0:T(8,128)(2,1)S(1)}, bf16[128,256]{1,0:T(8,128)(2,1)S(1)}, u32[]{:S(2)}, u32[]{:S(2)}) collective-permute-start(bf16[128,256]{1,0:T(8,128)(2,1)S(1)} %get-tuple-element.44), channel_id=1, source_target_pairs={{0,32},{2,34},{4,36},{6,38},{8,40},{10,42},{12,44},{14,46},{16,48}... | collective-permute-start | bytes 196616 | tf_op jit(solution)/shard_map/ppermute | solution.py:376
  83.6 4.8 %collective-permute-start.18 = (bf16[2,512,128]{2,1,0:T(8,128)(2,1)}, bf16[2,512,128]{2,1,0:T(8,128)(2,1)S(1)}, u32[]{:S(2)}, u32[]{:S(2)}) collective-permute-start(bf16[2,512,128]{2,1,0:T(8,128)(2,1)} %get-tuple-element.26), channel_id=1, source_target_pairs={{0,2},{2,0},{4,6},{6,4},{8,10},{10,8},{12,14},{14,12},{16,18},{18,... | collective-permute-start | bytes 786440 | tf_op jit(solution)/shard_map/ppermute | solution.py:373
  88.4 3.5 %collective-permute-start.19 = (bf16[2,512,128]{2,1,0:T(8,128)(2,1)}, bf16[2,512,128]{2,1,0:T(8,128)(2,1)S(1)}, u32[]{:S(2)}, u32[]{:S(2)}) collective-permute-start(bf16[2,512,128]{2,1,0:T(8,128)(2,1)} %get-tuple-element.27), channel_id=1, source_target_pairs={{0,4},{2,6},{4,0},{6,2},{8,12},{10,14},{12,8},{14,10},{16,20},{18,... | collective-permute-start | bytes 786440 | tf_op jit(solution)/shard_map/ppermute | solution.py:373
  92.5 4.7 %backward_end.1 = (bf16[4,2,128,256]{3,2,1,0:T(8,128)(2,1)}, bf16[2,512,128]{2,1,0:T(8,128)(2,1)}, bf16[2,512,128]{2,1,0:T(8,128)(2,1)}, bf16[2,512,128]{2,1,0:T(8,128)(2,1)}, bf16[2,512,128]{2,1,0:T(8,128)(2,1)}) custom-call(s32[20]{0:T(128)} %concatenate.30.sc, bf16[128,1024]{1,0:T(8,128)(2,1)} %get-tuple-element.21.refs_0_, bf16[128,1024]{1,0:T(8,128)(2,1)} %copy-done.3, ...), custom_call_target="tpu_custom_call" | custom-call | flops 2684354560 | bytes 8388608 | tf_op jit(solution)/shard_map/backward_end/pallas_call | solution.py:353
  97.2 4.0 %collective-permute-start.22 = (bf16[2,512,128]{2,1,0:T(8,128)(2,1)}, bf16[2,512,128]{2,1,0:T(8,128)(2,1)S(1)}, u32[]{:S(2)}, u32[]{:S(2)}) collective-permute-start(bf16[2,512,128]{2,1,0:T(8,128)(2,1)} %get-tuple-element.33), channel_id=1, source_target_pairs={{0,2},{2,0},{4,6},{6,4},{8,10},{10,8},{12,14},{14,12},{16,18},{18,... | collective-permute-start | bytes 786440 | tf_op jit(solution)/shard_map/ppermute | solution.py:373
  102.6 3.7 %collective-permute-done.31 = bf16[256,256]{1,0:T(8,128)(2,1)S(1)} collective-permute-done((bf16[256,256]{1,0:T(8,128)(2,1)S(1)}, bf16[256,256]{1,0:T(8,128)(2,1)S(1)}, u32[]{:S(2)}, u32[]{:S(2)}) %collective-permute-start.31) | collective-permute-done | bytes 131104 | tf_op jit(solution)/shard_map/ppermute | solution.py:383
  106.4 4.9 %collective-permute-done.27 = bf16[256,256]{1,0:T(8,128)(2,1)S(1)} collective-permute-done((bf16[256,256]{1,0:T(8,128)(2,1)S(1)}, bf16[256,256]{1,0:T(8,128)(2,1)S(1)}, u32[]{:S(2)}, u32[]{:S(2)}) %collective-permute-start.27) | collective-permute-done | bytes 131104 | tf_op jit(solution)/shard_map/ppermute | solution.py:383
  114.2 11.2 %collective-permute-start.28 = (bf16[256,256]{1,0:T(8,128)(2,1)S(1)}, bf16[256,256]{1,0:T(8,128)(2,1)S(1)}, u32[]{:S(2)}, u32[]{:S(2)}) collective-permute-start(bf16[256,256]{1,0:T(8,128)(2,1)S(1)} %fusion.2), channel_id=1, source_target_pairs={{0,224},{2,226},{4,228},{6,230},{8,232},{10,234},{12,236},{14,238}... | collective-permute-start | bytes 393224 | tf_op jit(solution)/shard_map/ppermute | solution.py:383
  127.7 3.1 %collective-permute-start.33 = (bf16[256,256]{1,0:T(8,128)(2,1)S(1)}, bf16[256,256]{1,0:T(8,128)(2,1)S(1)}, u32[]{:S(2)}, u32[]{:S(2)}) collective-permute-start(bf16[256,256]{1,0:T(8,128)(2,1)S(1)} %fusion.1), channel_id=1, source_target_pairs={{0,224},{2,226},{4,228},{6,230},{8,232},{10,234},{12,236},{14,238}... | collective-permute-start | bytes 393224 | tf_op jit(solution)/shard_map/ppermute | solution.py:385
  136.0 4.4 %collective-permute-start.34 = (bf16[128,256]{1,0:T(8,128)(2,1)S(1)}, bf16[128,256]{1,0:T(8,128)(2,1)S(1)}, u32[]{:S(2)}, u32[]{:S(2)}) collective-permute-start(bf16[128,256]{1,0:T(8,128)(2,1)S(1)} %slice.148), channel_id=1, source_target_pairs={{0,8},{2,10},{4,12},{6,14},{8,0},{10,2},{12,4},{14,6},{16,24},{18,... | collective-permute-start | bytes 196616 | tf_op jit(solution)/shard_map/ppermute | solution.py:388
  (137 shorter events, 46.4 us)
Async XLA Ops:
  2.4 9.0 %collective-permute-start = (bf16[128,1024]{1,0:T(8,128)(2,1)}, bf16[128,1024]{1,0:T(8,128)(2,1)S(1)}, u32[]{:S(2)}, u32[]{:S(2)}) collective-permute-start(bf16[128,1024]{1,0:T(8,128)(2,1)} %get-tuple-element.21.refs_0_), channel_id=1, source_target_pairs={{0,16},{2,18},{4,20},{6,22},{8,24},{10,26},{12,28},{14,30},{16,0},... | collective-permute-start | bytes 786440 | tf_op jit(solution)/shard_map/ppermute | solution.py:274
  3.9 10.7 %collective-permute-start.5 = (bf16[128,256]{1,0:T(8,128)(2,1)}, bf16[128,256]{1,0:T(8,128)(2,1)S(1)}, u32[]{:S(2)}, u32[]{:S(2)}) collective-permute-start(bf16[128,256]{1,0:T(8,128)(2,1)} %get-tuple-element.22), channel_id=1, source_target_pairs={{0,8},{2,10},{4,12},{6,14},{8,0},{10,2},{12,4},{14,6},{16,24},{18,... | collective-permute-start | bytes 196616 | tf_op jit(solution)/shard_map/ppermute | solution.py:275
  11.4 26.7 %collective-permute-start.2 = (bf16[256,1024]{1,0:T(8,128)(2,1)S(1)}, bf16[256,1024]{1,0:T(8,128)(2,1)S(1)}, u32[]{:S(2)}, u32[]{:S(2)}) collective-permute-start(bf16[256,1024]{1,0:T(8,128)(2,1)S(1)} %constant_dynamic-update-slice_fusion), channel_id=1, source_target_pairs={{0,6},{2,4},{4,2},{6,0},{8,14},{10,12},{12,10},{14,8},{16,22},{18,... | collective-permute-start | bytes 1572872 | tf_op jit(solution)/shard_map/ppermute | solution.py:281
  14.5 25.5 %collective-permute-start.1 = (bf16[256,1024]{1,0:T(8,128)(2,1)S(1)}, bf16[256,1024]{1,0:T(8,128)(2,1)S(1)}, u32[]{:S(2)}, u32[]{:S(2)}) collective-permute-start(bf16[256,1024]{1,0:T(8,128)(2,1)S(1)} %constant_dynamic-update-slice_fusion), channel_id=1, source_target_pairs={{0,2},{2,0},{4,6},{6,4},{8,10},{10,8},{12,14},{14,12},{16,18},{18,... | collective-permute-start | bytes 1572872 | tf_op jit(solution)/shard_map/ppermute | solution.py:281
  14.9 8.1 %collective-permute-start.6 = (bf16[256,256]{1,0:T(8,128)(2,1)S(1)}, bf16[256,256]{1,0:T(8,128)(2,1)S(1)}, u32[]{:S(2)}, u32[]{:S(2)}) collective-permute-start(bf16[256,256]{1,0:T(8,128)(2,1)S(1)} %constant_dynamic-update-slice_fusion.2.refs_6_), channel_id=1, source_target_pairs={{0,224},{2,226},{4,228},{6,230},{8,232},{10,234},{12,236},{14,238}... | collective-permute-start | bytes 393224 | tf_op jit(solution)/shard_map/ppermute | solution.py:279
  22.9 7.0 %collective-permute-start.7 = (bf16[256,256]{1,0:T(8,128)(2,1)S(1)}, bf16[256,256]{1,0:T(8,128)(2,1)S(1)}, u32[]{:S(2)}, u32[]{:S(2)}) collective-permute-start(bf16[256,256]{1,0:T(8,128)(2,1)S(1)} %collective-permute-done.6.refs_8_), channel_id=1, source_target_pairs={{0,32},{2,34},{4,36},{6,38},{8,40},{10,42},{12,44},{14,46},{16,48}... | collective-permute-start | bytes 393224 | tf_op jit(solution)/shard_map/ppermute | solution.py:278
  25.8 16.6 %collective-permute-start.10 = (bf16[256,256]{1,0:T(8,128)(2,1)}, bf16[256,256]{1,0:T(8,128)(2,1)S(1)}, u32[]{:S(2)}, u32[]{:S(2)}) collective-permute-start(bf16[256,256]{1,0:T(8,128)(2,1)} %collective-permute-done.9.refs_9_), channel_id=1, source_target_pairs={{0,32},{2,34},{4,36},{6,38},{8,40},{10,42},{12,44},{14,46},{16,48}... | collective-permute-start | bytes 393224 | tf_op jit(solution)/shard_map/ppermute | solution.py:278
  34.9 8.7 %collective-permute-start.12 = (bf16[128,256]{1,0:T(8,128)(2,1)S(1)}, bf16[128,256]{1,0:T(8,128)(2,1)S(1)}, u32[]{:S(2)}, u32[]{:S(2)}) collective-permute-start(bf16[128,256]{1,0:T(8,128)(2,1)S(1)} %slice.138), channel_id=1, source_target_pairs={{0,32},{2,34},{4,36},{6,38},{8,40},{10,42},{12,44},{14,46},{16,48}... | collective-permute-start | bytes 196616 | tf_op jit(solution)/shard_map/ppermute | solution.py:284
  38.1 8.7 %collective-permute-start.3 = (bf16[128,1024]{1,0:T(8,128)(2,1)S(1)}, bf16[128,1024]{1,0:T(8,128)(2,1)S(1)}, u32[]{:S(2)}, u32[]{:S(2)}) collective-permute-start(bf16[128,1024]{1,0:T(8,128)(2,1)S(1)} %slice.136), channel_id=1, source_target_pairs={{0,2},{2,0},{4,6},{6,4},{8,10},{10,8},{12,14},{14,12},{16,18},{18,... | collective-permute-start | bytes 786440 | tf_op jit(solution)/shard_map/ppermute | solution.py:282
  40.0 7.7 %collective-permute-start.4 = (bf16[128,1024]{1,0:T(8,128)(2,1)S(1)}, bf16[128,1024]{1,0:T(8,128)(2,1)S(1)}, u32[]{:S(2)}, u32[]{:S(2)}) collective-permute-start(bf16[128,1024]{1,0:T(8,128)(2,1)S(1)} %slice.137), channel_id=1, source_target_pairs={{0,6},{2,4},{4,2},{6,0},{8,14},{10,12},{12,10},{14,8},{16,22},{18,... | collective-permute-start | bytes 786440 | tf_op jit(solution)/shard_map/ppermute | solution.py:282
  60.3 7.4 %collective-permute-start.16 = (f32[2,12,512]{2,1,0:T(8,128)S(1)}, f32[2,12,512]{2,1,0:T(8,128)S(1)}, u32[]{:S(2)}, u32[]{:S(2)}) collective-permute-start(f32[2,12,512]{2,1,0:T(8,128)S(1)} %pad_maximum_fusion.2.refs_10_), channel_id=1, source_target_pairs={{0,4},{2,6},{4,0},{6,2},{8,12},{10,14},{12,8},{14,10},{16,20},{18,... | collective-permute-start | bytes 147464 | tf_op jit(solution)/shard_map/ppermute | solution.py:342
  77.0 20.2 %collective-permute-start.30 = (bf16[128,256]{1,0:T(8,128)(2,1)S(1)}, bf16[128,256]{1,0:T(8,128)(2,1)S(1)}, u32[]{:S(2)}, u32[]{:S(2)}) collective-permute-start(bf16[128,256]{1,0:T(8,128)(2,1)S(1)} %get-tuple-element.44), channel_id=1, source_target_pairs={{0,32},{2,34},{4,36},{6,38},{8,40},{10,42},{12,44},{14,46},{16,48}... | collective-permute-start | bytes 196616 | tf_op jit(solution)/shard_map/ppermute | solution.py:376
  81.3 19.9 %collective-permute-start.26 = (bf16[128,256]{1,0:T(8,128)(2,1)S(1)}, bf16[128,256]{1,0:T(8,128)(2,1)S(1)}, u32[]{:S(2)}, u32[]{:S(2)}) collective-permute-start(bf16[128,256]{1,0:T(8,128)(2,1)S(1)} %get-tuple-element.45), channel_id=1, source_target_pairs={{0,224},{2,226},{4,228},{6,230},{8,232},{10,234},{12,236},{14,238}... | collective-permute-start | bytes 196616 | tf_op jit(solution)/shard_map/ppermute | solution.py:377
  83.6 29.2 %collective-permute-start.18 = (bf16[2,512,128]{2,1,0:T(8,128)(2,1)}, bf16[2,512,128]{2,1,0:T(8,128)(2,1)S(1)}, u32[]{:S(2)}, u32[]{:S(2)}) collective-permute-start(bf16[2,512,128]{2,1,0:T(8,128)(2,1)} %get-tuple-element.26), channel_id=1, source_target_pairs={{0,2},{2,0},{4,6},{6,4},{8,10},{10,8},{12,14},{14,12},{16,18},{18,... | collective-permute-start | bytes 786440 | tf_op jit(solution)/shard_map/ppermute | solution.py:373
  88.4 25.8 %collective-permute-start.19 = (bf16[2,512,128]{2,1,0:T(8,128)(2,1)}, bf16[2,512,128]{2,1,0:T(8,128)(2,1)S(1)}, u32[]{:S(2)}, u32[]{:S(2)}) collective-permute-start(bf16[2,512,128]{2,1,0:T(8,128)(2,1)} %get-tuple-element.27), channel_id=1, source_target_pairs={{0,4},{2,6},{4,0},{6,2},{8,12},{10,14},{12,8},{14,10},{16,20},{18,... | collective-permute-start | bytes 786440 | tf_op jit(solution)/shard_map/ppermute | solution.py:373
  91.9 22.3 %collective-permute-start.20 = (bf16[2,512,128]{2,1,0:T(8,128)(2,1)}, bf16[2,512,128]{2,1,0:T(8,128)(2,1)S(1)}, u32[]{:S(2)}, u32[]{:S(2)}) collective-permute-start(bf16[2,512,128]{2,1,0:T(8,128)(2,1)} %get-tuple-element.28), channel_id=1, source_target_pairs={{0,6},{2,4},{4,2},{6,0},{8,14},{10,12},{12,10},{14,8},{16,22},{18,... | collective-permute-start | bytes 786440 | tf_op jit(solution)/shard_map/ppermute | solution.py:373
  97.2 29.0 %collective-permute-start.22 = (bf16[2,512,128]{2,1,0:T(8,128)(2,1)}, bf16[2,512,128]{2,1,0:T(8,128)(2,1)S(1)}, u32[]{:S(2)}, u32[]{:S(2)}) collective-permute-start(bf16[2,512,128]{2,1,0:T(8,128)(2,1)} %get-tuple-element.33), channel_id=1, source_target_pairs={{0,2},{2,0},{4,6},{6,4},{8,10},{10,8},{12,14},{14,12},{16,18},{18,... | collective-permute-start | bytes 786440 | tf_op jit(solution)/shard_map/ppermute | solution.py:373
  111.3 16.2 %collective-permute-start.23 = (bf16[2,512,128]{2,1,0:T(8,128)(2,1)S(1)}, bf16[2,512,128]{2,1,0:T(8,128)(2,1)S(1)}, u32[]{:S(2)}, u32[]{:S(2)}) collective-permute-start(bf16[2,512,128]{2,1,0:T(8,128)(2,1)S(1)} %copy-done.17), channel_id=1, source_target_pairs={{0,4},{2,6},{4,0},{6,2},{8,12},{10,14},{12,8},{14,10},{16,20},{18,... | collective-permute-start | bytes 786440 | tf_op jit(solution)/shard_map/ppermute | solution.py:373
  112.8 14.7 %collective-permute-start.24 = (bf16[2,512,128]{2,1,0:T(8,128)(2,1)S(1)}, bf16[2,512,128]{2,1,0:T(8,128)(2,1)S(1)}, u32[]{:S(2)}, u32[]{:S(2)}) collective-permute-start(bf16[2,512,128]{2,1,0:T(8,128)(2,1)S(1)} %copy-done.16), channel_id=1, source_target_pairs={{0,6},{2,4},{4,2},{6,0},{8,14},{10,12},{12,10},{14,8},{16,22},{18,... | collective-permute-start | bytes 786440 | tf_op jit(solution)/shard_map/ppermute | solution.py:373
  114.2 13.4 %collective-permute-start.32 = (bf16[256,256]{1,0:T(8,128)(2,1)S(1)}, bf16[256,256]{1,0:T(8,128)(2,1)S(1)}, u32[]{:S(2)}, u32[]{:S(2)}) collective-permute-start(bf16[256,256]{1,0:T(8,128)(2,1)S(1)} %fusion), channel_id=1, source_target_pairs={{0,32},{2,34},{4,36},{6,38},{8,40},{10,42},{12,44},{14,46},{16,48}... | collective-permute-start | bytes 393224 | tf_op jit(solution)/shard_map/ppermute | solution.py:383
  114.2 16.6 %collective-permute-start.28 = (bf16[256,256]{1,0:T(8,128)(2,1)S(1)}, bf16[256,256]{1,0:T(8,128)(2,1)S(1)}, u32[]{:S(2)}, u32[]{:S(2)}) collective-permute-start(bf16[256,256]{1,0:T(8,128)(2,1)S(1)} %fusion.2), channel_id=1, source_target_pairs={{0,224},{2,226},{4,228},{6,230},{8,232},{10,234},{12,236},{14,238}... | collective-permute-start | bytes 393224 | tf_op jit(solution)/shard_map/ppermute | solution.py:383
  126.2 14.1 %collective-permute-start.21 = (bf16[512,128]{1,0:T(8,128)(2,1)S(1)}, bf16[512,128]{1,0:T(8,128)(2,1)S(1)}, u32[]{:S(2)}, u32[]{:S(2)}) collective-permute-start(bf16[512,128]{1,0:T(8,128)(2,1)S(1)} %get-tuple-element.50), channel_id=1, source_target_pairs={{0,16},{2,18},{4,20},{6,22},{8,24},{10,26},{12,28},{14,30},{16,0},... | collective-permute-start | bytes 393224 | tf_op jit(solution)/shard_map/ppermute | solution.py:379
  131.6 11.1 %collective-permute-start.25 = (bf16[512,128]{1,0:T(8,128)(2,1)S(1)}, bf16[512,128]{1,0:T(8,128)(2,1)S(1)}, u32[]{:S(2)}, u32[]{:S(2)}) collective-permute-start(bf16[512,128]{1,0:T(8,128)(2,1)S(1)} %get-tuple-element.48), channel_id=1, source_target_pairs={{0,16},{2,18},{4,20},{6,22},{8,24},{10,26},{12,28},{14,30},{16,0},... | collective-permute-start | bytes 393224 | tf_op jit(solution)/shard_map/ppermute | solution.py:387
  136.0 9.1 %collective-permute-start.34 = (bf16[128,256]{1,0:T(8,128)(2,1)S(1)}, bf16[128,256]{1,0:T(8,128)(2,1)S(1)}, u32[]{:S(2)}, u32[]{:S(2)}) collective-permute-start(bf16[128,256]{1,0:T(8,128)(2,1)S(1)} %slice.148), channel_id=1, source_target_pairs={{0,8},{2,10},{4,12},{6,14},{8,0},{10,2},{12,4},{14,6},{16,24},{18,... | collective-permute-start | bytes 196616 | tf_op jit(solution)/shard_map/ppermute | solution.py:388
  (35 other events, 336.4 us)

commit v3 on v2

--- a/solution.py
+++ b/solution.py
@@ -28,10 +28,11 @@
     return [(d, d ^ mask) for d in range(DEVICES)]
 
 
-X_LO, X_HI = flip(8), flip(4)
 Y = [flip(s) for s in range(SLOTS)]
-EVEN = flip(16)
-ODD = [(d, (d + (16 if d // 16 % 2 else -16)) % DEVICES) for d in range(DEVICES)]
+X = [flip(m) for m in (0, 8, 4, 12)]
+NEXT = flip(16)
+NEAR = flip(32)
+REST = [(d, (d + (32 if d // 32 % 2 else -32)) % DEVICES) for d in range(DEVICES)]
 
 
 def dot(a, b):
@@ -59,11 +60,10 @@
                 do_s[t, h, to, :] = part[:, (group + h) * width : (group + h + 1) * width]
     for n, ref in enumerate(keys):
         for u in range(2):
-            part = ref[pl.ds(u * CHUNK, CHUNK), :]
-            block, at = n // 2 * 2 + u, pl.ds(n % 2 * CHUNK, CHUNK)
-            k_s[block, at, :] = part[:, :width]
-            v_s[block, at, :] = part[:, width:]
-            t_s[block, :, at] = jnp.transpose(part[:, which * width : (which + 1) * width])
+            part = ref[pl.ds(u * PAIR, PAIR), :]
+            k_s[2 * n + u] = part[:, :width]
+            v_s[2 * n + u] = part[:, width:]
+            t_s[2 * n + u] = jnp.transpose(part[:, which * width : (which + 1) * width])
 
 
 def start_of(sc, row):
@@ -74,20 +74,17 @@
     return start
 
 
-def place(sc, pair, u, t):
+def place(sc, block, t):
     z, x_lo, x_hi, y = (sc[n] for n in range(4))
-    plane = (4 * (x_hi ^ u) + y) * PLANE + x_lo * CHUNK
-    one, two = (plane + sc[4 + DOCS + 2 * pair + n] * PAIR for n in range(2))
-    row = ((z * 4 + x_lo * 2 + x_hi) ^ (2 * t)) * ROWS
-    low, high = jnp.minimum(one, two), jnp.maximum(one, two)
-    needed = (low <= row + ROWS - 1) & (high + CHUNK - 1 >= start_of(sc, row))
-    whole = (high + CHUNK - 1 <= row) & (low >= start_of(sc, row + ROWS - 1))
-    return one, two, row, needed, whole
-
-
-def allowed_of(sc, one, two, row):
-    index = lax.broadcasted_iota(jnp.int32, (PAIR, 1), 0)
-    key_at = index + jnp.where(index < CHUNK, one, two - CHUNK)
+    base = (4 * (x_hi ^ (block & 1)) + y) * PLANE + sc[4 + DOCS + block // 2] * PAIR
+    row = ((z * 4 + x_lo * 2 + x_hi) ^ (4 * t)) * ROWS
+    needed = (base <= row + ROWS - 1) & (base + PAIR - 1 >= start_of(sc, row))
+    whole = (base + PAIR - 1 <= row) & (base >= start_of(sc, row + ROWS - 1))
+    return base, row, needed, whole
+
+
+def allowed_of(sc, base, row):
+    key_at = base + (lax.broadcasted_iota(jnp.int32, (PAIR, 1), 0) ^ (sc[1] * CHUNK))
     row_at = row + (lax.broadcasted_iota(jnp.int32, (1, ROWS), 1) ^ (sc[3] * CHUNK))
     return (key_at >= start_of(sc, row_at)) & (key_at <= row_at)
 
@@ -101,8 +98,8 @@
     keys[:, width:] = value[...]
 
 
-def forward(group, width, pairs, sc, *refs):
-    rows, keys, refs = refs[:6], refs[6 : 6 + 2 * pairs], refs[6 + 2 * pairs :]
+def forward(group, width, pieces, sc, *refs):
+    rows, keys, refs = refs[:6], refs[6 : 6 + pieces], refs[6 + pieces :]
     acc, stat, q_s, do_s, k_s, v_s, t_s, high, total, mixed = refs
     unit = LOG2E / math.sqrt(width)
     heads = range(group)
@@ -112,11 +109,11 @@
     total[...] = jnp.zeros_like(total)
     mixed[...] = jnp.zeros_like(mixed)
 
-    def block(b, t, one, two, row, masked):
+    def block(b, t, base, row, masked):
         scores = [dot_t(k_s[b], q_s[t, h]) for h in heads]
         dprobs = [dot_t(v_s[b], do_s[t, h]) for h in heads]
         if masked:
-            allowed = allowed_of(sc, one, two, row)
+            allowed = allowed_of(sc, base, row)
             scores = [jnp.where(allowed, s, NEG) for s in scores]
         olds = [high[t, h] for h in heads]
         news = [jnp.maximum(o, jnp.max(s, axis=0, keepdims=True)) for o, s in zip(olds, scores)]
@@ -136,19 +133,19 @@
 
     def step(n, carry):
         b, t = n // 2, n & 1
-        one, two, row, needed, whole = place(sc, n // 4, (n // 2) & 1, t)
+        base, row, needed, whole = place(sc, b, t)
 
         @pl.when(needed & whole)
         def _():
-            block(b, t, one, two, row, False)
+            block(b, t, base, row, False)
 
         @pl.when(needed & jnp.logical_not(whole))
         def _():
-            block(b, t, one, two, row, True)
+            block(b, t, base, row, True)
 
         return carry
 
-    lax.fori_loop(0, 4 * pairs, step, 0)
+    lax.fori_loop(0, 4 * pieces, step, 0)
     for t in range(TILES):
         for h in heads:
             stat[t, h : h + 1, :] = high[t, h]
@@ -156,8 +153,8 @@
             stat[t, 2 * group + h : 2 * group + h + 1, :] = mixed[t, h]
 
 
-def backward(group, width, pairs, begins, ends, sc, *refs):
-    rows, keys, refs = refs[:6], refs[6 : 6 + 2 * pairs], refs[6 + 2 * pairs :]
+def backward(group, width, pieces, begins, ends, sc, *refs):
+    rows, keys, refs = refs[:6], refs[6 : 6 + pieces], refs[6 + pieces :]
     scale = 1.0 / math.sqrt(width)
     unit = LOG2E * scale
     heads = range(group)
@@ -195,11 +192,11 @@
         lse[...] = lse_in[...]
         delta[...] = delta_in[...]
 
-    def block(b, t, one, two, row, masked):
+    def block(b, t, base, row, masked):
         scores = [dot_t(k_s[b], q_s[t, h]) for h in heads]
         dprobs = [dot_t(v_s[b], do_s[t, h]) for h in heads]
         if masked:
-            allowed = allowed_of(sc, one, two, row)
+            allowed = allowed_of(sc, base, row)
             scores = [jnp.where(allowed, s, NEG) for s in scores]
         probs = [jnp.exp2(scores[h] * unit - lse[t, h]) for h in heads]
         dscores = [(probs[h] * (dprobs[h] - delta[t, h])).astype(BF16) for h in heads]
@@ -216,24 +213,23 @@
         grads[...] = jnp.zeros_like(grads)
 
         def tile(t, carry):
-            one, two, row, needed, whole = place(sc, b // 2, b & 1, t)
+            base, row, needed, whole = place(sc, b, t)
 
             @pl.when(needed & whole)
             def _():
-                block(b, t, one, two, row, False)
+                block(b, t, base, row, False)
 
             @pl.when(needed & jnp.logical_not(whole))
             def _():
-                block(b, t, one, two, row, True)
+                block(b, t, base, row, True)
 
             return carry
 
         lax.fori_loop(0, TILES, tile, 0)
-        for n in range(2):
-            dkv[b // 2 * 2 + n, b & 1] = grads[n * CHUNK : (n + 1) * CHUNK, :].astype(BF16)
+        dkv[b] = grads[...].astype(BF16)
         return carry
 
-    lax.fori_loop(0, 2 * pairs, step, 0)
+    lax.fori_loop(0, 2 * pieces, step, 0)
     if ends:
         for t in range(TILES):
             for h in heads:
@@ -271,42 +267,39 @@
         ],
         name="pack",
     )(query, key, value, dout)
-    row_other = send(row_home, perm=X_LO)
-    own = jnp.concatenate([key_home, send(key_home, perm=X_HI)], axis=0)
-    a, b = [own], [own]
-    for k in range(3):
-        a.append(send(b[k], perm=EVEN))
-        b.append(send(a[k], perm=ODD))
+    own = jnp.concatenate(
+        [key_home] + [send(key_home, perm=X[n]) for n in range(1, 4)], axis=0
+    )
+    row_other = send(row_home, perm=NEXT)
+    a, b = send(own, perm=NEAR), send(own, perm=REST)
     both = jnp.concatenate([row_home, row_other], axis=0)
     near, last = send(both, perm=Y[1]), send(both, perm=Y[3])
+    opposite = jnp.concatenate([send(b[:PAIR], perm=NEAR), send(a[PAIR:], perm=REST)], axis=0)
     far_own, far_other = send(last[:CHUNK], perm=Y[1]), send(near[CHUNK:], perm=Y[3])
-    opposite = jnp.concatenate(
-        [send(b[3][:CHUNK], perm=EVEN), send(a[3][CHUNK:], perm=ODD)], axis=0
-    )
     rows = [row_home, row_other, near, last, far_own, far_other]
-    keys = [a[0], a[1], b[1], b[2], a[2], a[3], b[3], opposite]
+    keys = [own, a, b, opposite]
 
     numbers = jnp.arange(DOCS, dtype=jnp.int32)
     starts = jnp.sum((document[None, :] < numbers[:, None]).astype(jnp.int32), axis=1)
-    side = 1 - 2 * (z % 2)
-    sources = jnp.stack([z + side * k for k in (0, 1, -1, -2, 2, 3, -3, 4)]) & 7
+    side = 2 - 4 * (z // 2 % 2)
+    sources = jnp.stack([z, z + side, z - side, z + 4]) & 7
     sc = jnp.concatenate([jnp.stack([z, x_lo, x_hi, y]), starts, sources]).astype(jnp.int32)
 
     smem = pl.BlockSpec(memory_space=pltpu.SMEM)
     vmem = pl.BlockSpec(memory_space=pltpu.VMEM)
     params = pltpu.CompilerParams(vmem_limit_bytes=56 * 1024 * 1024)
 
-    def cost(dots, pairs):
-        work = TILES * ROWS * group * pairs * 2 * PAIR * width * 2
+    def cost(dots, pieces):
+        work = TILES * ROWS * group * pieces * 2 * PAIR * width * 2
         return pl.CostEstimate(flops=dots * work // 2, bytes_accessed=1 << 23, transcendentals=0)
 
-    def scratch(pairs):
+    def scratch(pieces):
         return [
             pltpu.VMEM((TILES, group, ROWS, width), BF16),
             pltpu.VMEM((TILES, group, ROWS, width), BF16),
-            pltpu.VMEM((2 * pairs, PAIR, width), BF16),
-            pltpu.VMEM((2 * pairs, PAIR, width), BF16),
-            pltpu.VMEM((2 * pairs, width, PAIR), BF16),
+            pltpu.VMEM((2 * pieces, PAIR, width), BF16),
+            pltpu.VMEM((2 * pieces, PAIR, width), BF16),
+            pltpu.VMEM((2 * pieces, width, PAIR), BF16),
         ]
 
     line = (TILES, group, 1, ROWS)
@@ -318,7 +311,7 @@
     values, stat = pl.pallas_call(
         functools.partial(forward, group, width, 4),
         out_shape=[acc_shape, stat_shape],
-        in_specs=[smem] + [vmem] * 14,
+        in_specs=[smem] + [vmem] * 10,
         out_specs=[vmem] * 2,
         scratch_shapes=scratch(4) + [pltpu.VMEM(line, F32)] * 3,
         compiler_params=params,
@@ -327,7 +320,7 @@
     )(sc, *rows, *keys)
 
     unit = LOG2E / math.sqrt(width)
-    other = send(stat, perm=X_LO)[::-1]
+    other = send(stat, perm=NEXT)[::-1]
     top = jnp.maximum(stat[:, :group], other[:, :group])
     mine, theirs = (jnp.exp2((s[:, :group] - top) * unit) for s in (stat, other))
     merged = jnp.concatenate(
@@ -341,51 +334,46 @@
     )
     stats = [merged] + [send(merged, perm=Y[s]) for s in range(1, SLOTS)]
 
-    def back(pairs, begins, ends, sc, keys, *more):
-        dkv_shape = jax.ShapeDtypeStruct((2 * pairs, 2, CHUNK, 2 * width), BF16)
+    def back(pieces, begins, ends, sc, keys, *more):
+        dkv_shape = jax.ShapeDtypeStruct((2 * pieces, PAIR, 2 * width), BF16)
         shapes = [dkv_shape] + [piece] * (SLOTS * (begins + ends))
         carried = [acc_shape, line_shape, line_shape]
-        more_scratch = scratch(pairs) + [pltpu.VMEM((PAIR, 2 * width), F32)]
+        more_scratch = scratch(pieces) + [pltpu.VMEM((PAIR, 2 * width), F32)]
         if ends:
             more_scratch = [pltpu.VMEM(s.shape, F32) for s in carried] + more_scratch
         else:
             shapes = shapes + carried
         return pl.pallas_call(
-            functools.partial(backward, group, width, pairs, begins, ends),
+            functools.partial(backward, group, width, pieces, begins, ends),
             out_shape=shapes,
-            in_specs=[smem] + [vmem] * (6 + 2 * pairs + len(more)),
+            in_specs=[smem] + [vmem] * (6 + pieces + len(more)),
             out_specs=[vmem] * len(shapes),
             scratch_shapes=more_scratch,
             compiler_params=params,
-            cost_estimate=cost(5, pairs),
+            cost_estimate=cost(5, pieces),
             name="backward_begin" if begins else "backward_end",
         )(sc, *rows, *keys, *more)
 
     def shifted(skip):
         return jnp.concatenate([sc[: 4 + DOCS], sc[4 + DOCS + skip :]])
 
-    late = back(2, True, False, shifted(4), keys[4:], *stats, stat, values)
+    late = back(2, True, False, shifted(2), keys[2:], *stats, stat, values)
     far, mixed, carried = late[0], late[1 : 1 + SLOTS], late[1 + SLOTS :]
-    end = back(2, False, True, sc, keys[:4], *carried)
+    end = back(2, False, True, sc, keys[:2], *carried)
     close, dq = end[0], end[1:]
 
     def over_y(parts):
         return add(parts[0], *[send(parts[s], perm=Y[s]) for s in range(1, SLOTS)])
 
-    flat = (PAIR, 2 * width)
-    one = send(far[3, 0], perm=EVEN)
-    two = send(far[3, 1], perm=ODD)
+    one, two = send(far[2], perm=NEAR), send(far[3], perm=REST)
     mixed = over_y(mixed)
-    mixed = [mixed[0], send(mixed[1], perm=X_LO)]
-    gb = jnp.concatenate([add(far[2, 0], one), far[2, 1]], axis=0)
-    ga = jnp.concatenate([far[1, 0], add(far[1, 1], two)], axis=0)
-    for pa, pb in ((far[0], close[3]), (close[1], close[2])):
-        sent_b, sent_a = send(gb, perm=ODD), send(ga, perm=EVEN)
-        ga, gb = add(pa.reshape(flat), sent_b), add(pb.reshape(flat), sent_a)
-    grad = add(close[0].reshape(flat), send(ga, perm=EVEN), send(gb, perm=ODD))
+    mixed = [mixed[0], send(mixed[1], perm=NEXT)]
+    ga = send(jnp.concatenate([close[2], add(close[3], two)], axis=0), perm=NEAR)
+    gb = send(jnp.concatenate([add(far[0], one), far[1]], axis=0), perm=REST)
+    grad = add(close[:2].reshape(2 * PAIR, 2 * width), ga, gb).reshape(4, CHUNK, 2 * width)
     dq = over_y(dq)
-    dq = [dq[0], send(dq[1], perm=X_LO)]
-    grad = add(grad[:CHUNK], send(grad[CHUNK:], perm=X_HI))
+    grad = add(grad[0], *[send(grad[n], perm=X[n]) for n in range(1, 4)])
+    dq = [dq[0], send(dq[1], perm=NEXT)]
 
     outs = [
         pl.pallas_call(

time: 146 us -> 147 us (level)
  starting transfers between devices: 80.5 us -> 62.1 us
  Pallas kernels: 20.5 us -> 33.8 us
  waiting for transfers between devices: 32 us -> 38 us
    ppermute x22 -> x18, starting transfers between devices: 52.5 us -> 38.1 us  [the longest x2 8.42 us: local(): one, two = (send(far[2], perm=NEAR), send(far[3], perm=REST))]
    pallas_call x2, Pallas kernels: 10.5 us -> 17.5 us  [back(): pl.pallas_call(functools.partial(backward, group, width, pieces, begins,...]
    pallas_call x1, Pallas kernels: 4.75 us -> 11.1 us  [local(): pl.pallas_call(functools.partial(forward, group, width, 4), out_shape=[ac...]
    ppermute x22 -> x18, waiting for transfers between devices: 27.5 us -> 31.2 us  [the longest x2 9.04 us: local(): one, two = (send(far[2], perm=NEAR), send(far[3], perm=REST))]
    ppermute x1, waiting for transfers between devices: 0.88 us -> 2.93 us  [local(): send(near[CHUNK:], perm=Y[3])]
    ppermute x1, waiting for transfers between devices: 0.01 us -> 1.66 us  [local(): send(last[:CHUNK], perm=Y[1])]
    ppermute x3, starting transfers between devices: 5.68 us -> 4.17 us  [local(): stats = [merged] + [send(merged, perm=Y[s]) for s in range(1, SLOTS)]]
    unnamed x51 -> x47, local copies, waits for them, and re-layouts: 4.53 us -> 3.85 us
  transfers between devices with their start and end apart: 35 -> 31, of which waited for: 14 -> 13; matrix products, arithmetic and copies ran while one was open for 5% -> 5% of each run, Pallas kernels for 6% -> 2%
where the time goes in v3:
time: 147 us
  starting transfers between devices  62.1 us (42%)
  waiting for transfers between devices  38 us (26%)
  Pallas kernels  33.8 us (23%)
  local copies, waits for them, and re-layouts  9.22 us (6%)
  other arithmetic  2.68 us (2%)
    pallas_call x2, Pallas kernels, back(): pl.pallas_call(functools.partial(backward, group, width, pieces, begins,...  17.5 us
    ppermute x6, starting transfers between devices, over_y(): return add(parts[0], *[send(parts[s], perm=Y[s]) for s in range(1, SLOTS)])  14.3 us
    pallas_call x1, Pallas kernels, local(): pl.pallas_call(functools.partial(forward, group, width, 4), out_shape=[ac...  11.1 us
    ppermute x2, waiting for transfers between devices, local(): one, two = (send(far[2], perm=NEAR), send(far[3], perm=REST))  9.04 us
    ppermute x2, waiting for transfers between devices, local(): a, b = (send(own, perm=NEAR), send(own, perm=REST))  8.9 us
    ppermute x2, starting transfers between devices, local(): one, two = (send(far[2], perm=NEAR), send(far[3], perm=REST))  8.42 us
    ppermute x2, starting transfers between devices, local(): a, b = (send(own, perm=NEAR), send(own, perm=REST))  6.94 us
    ppermute x3, starting transfers between devices, local(): grad = add(grad[0], *[send(grad[n], perm=X[n]) for n in range(1, 4)])  5.22 us
  transfers between devices with their start and end apart: 31, of which 13 were waited for; matrix products, arithmetic and copies ran while one was open for 5% of the time, Pallas kernels for 2%

profile of v3, /device:TPU:32, one launch (start us, length us, event | category | flops | bytes accessed | tf_op | source)
XLA Modules:
  0.0 146.9 jit_solution(16825520808452432602)
XLA Ops:
  2.4 2.8 %collective-permute-start.7 = (bf16[128,256]{1,0:T(8,128)(2,1)}, bf16[128,256]{1,0:T(8,128)(2,1)S(1)}, u32[]{:S(2)}, u32[]{:S(2)}) collective-permute-start(bf16[128,256]{1,0:T(8,128)(2,1)} %get-tuple-element.22), channel_id=1, source_target_pairs={{0,24},{2,26},{4,28},{6,30},{8,16},{10,18},{12,20},{14,22},{16,8},... | collective-permute-start | bytes 196616 | tf_op jit(solution)/shard_map/ppermute | solution.py:271
  6.5 1.8 %collective-permute-start = (bf16[128,1024]{1,0:T(8,128)(2,1)}, bf16[128,1024]{1,0:T(8,128)(2,1)S(1)}, u32[]{:S(2)}, u32[]{:S(2)}) collective-permute-start(bf16[128,1024]{1,0:T(8,128)(2,1)} %get-tuple-element.21.refs_0_), channel_id=1, source_target_pairs={{0,32},{2,34},{4,36},{6,38},{8,40},{10,42},{12,44},{14,46},{16,48}... | collective-permute-start | bytes 786440 | tf_op jit(solution)/shard_map/ppermute | solution.py:273
  10.5 3.5 %collective-permute-done.refs_1_ = bf16[128,1024]{1,0:T(8,128)(2,1)S(1)} collective-permute-done((bf16[128,1024]{1,0:T(8,128)(2,1)}, bf16[128,1024]{1,0:T(8,128)(2,1)S(1)}, u32[]{:S(2)}, u32[]{:S(2)}) %collective-permute-start) | collective-permute-done | bytes 262176 | tf_op jit(solution)/shard_map/ppermute | solution.py:273
  14.0 3.1 %collective-permute-start.2 = (bf16[256,1024]{1,0:T(8,128)(2,1)S(1)}, bf16[256,1024]{1,0:T(8,128)(2,1)S(1)}, u32[]{:S(2)}, u32[]{:S(2)}) collective-permute-start(bf16[256,1024]{1,0:T(8,128)(2,1)S(1)} %constant_dynamic-update-slice_fusion), channel_id=1, source_target_pairs={{0,6},{2,4},{4,2},{6,0},{8,14},{10,12},{12,10},{14,8},{16,22},{18,... | collective-permute-start | bytes 1572872 | tf_op jit(solution)/shard_map/ppermute | solution.py:276
  17.2 5.5 %collective-permute-start.8 = (bf16[512,256]{1,0:T(8,128)(2,1)S(1)}, bf16[512,256]{1,0:T(8,128)(2,1)S(1)}, u32[]{:S(2)}, u32[]{:S(2)}) collective-permute-start(bf16[512,256]{1,0:T(8,128)(2,1)S(1)} %constant_dynamic-update-slice_fusion.2.refs_6_), channel_id=1, source_target_pairs={{0,192},{2,194},{4,196},{6,198},{8,200},{10,202},{12,204},{14,206}... | collective-permute-start | bytes 786440 | tf_op jit(solution)/shard_map/ppermute | solution.py:274
  24.2 8.3 %collective-permute-done.8.refs_8_.refs_6_ = bf16[512,256]{1,0:T(8,128)(2,1)S(1)} collective-permute-done((bf16[512,256]{1,0:T(8,128)(2,1)S(1)}, bf16[512,256]{1,0:T(8,128)(2,1)S(1)}, u32[]{:S(2)}, u32[]{:S(2)}) %collective-permute-start.8) | collective-permute-done | bytes 262176 | tf_op jit(solution)/shard_map/ppermute | solution.py:274
  34.2 4.1 %collective-permute-start.11 = (bf16[256,256]{1,0:T(8,128)(2,1)S(1)}, bf16[256,256]{1,0:T(8,128)(2,1)S(1)}, u32[]{:S(2)}, u32[]{:S(2)}) collective-permute-start(bf16[256,256]{1,0:T(8,128)(2,1)S(1)} %slice.135), channel_id=1, source_target_pairs={{0,192},{2,194},{4,196},{6,198},{8,200},{10,202},{12,204},{14,206}... | collective-permute-start | bytes 393224 | tf_op jit(solution)/shard_map/ppermute | solution.py:277
  38.3 1.8 %collective-permute-start.3 = (bf16[128,1024]{1,0:T(8,128)(2,1)S(1)}, bf16[128,1024]{1,0:T(8,128)(2,1)}, u32[]{:S(2)}, u32[]{:S(2)}) collective-permute-start(bf16[128,1024]{1,0:T(8,128)(2,1)S(1)} %slice.132), channel_id=1, source_target_pairs={{0,2},{2,0},{4,6},{6,4},{8,10},{10,8},{12,14},{14,12},{16,18},{18,... | collective-permute-start | bytes 786440 | tf_op jit(solution)/shard_map/ppermute | solution.py:278
  41.4 2.0 %collective-permute-done.11 = bf16[256,256]{1,0:T(8,128)(2,1)S(1)} collective-permute-done((bf16[256,256]{1,0:T(8,128)(2,1)S(1)}, bf16[256,256]{1,0:T(8,128)(2,1)S(1)}, u32[]{:S(2)}, u32[]{:S(2)}) %collective-permute-start.11) | collective-permute-done | bytes 131104 | tf_op jit(solution)/shard_map/ppermute | solution.py:277
  45.0 2.9 %collective-permute-done.4.refs_5_ = bf16[128,1024]{1,0:T(8,128)(2,1)} collective-permute-done((bf16[128,1024]{1,0:T(8,128)(2,1)S(1)}, bf16[128,1024]{1,0:T(8,128)(2,1)}, u32[]{:S(2)}, u32[]{:S(2)}) %collective-permute-start.4) | collective-permute-done | bytes 262176 | tf_op jit(solution)/shard_map/ppermute | solution.py:278
  48.0 11.1 %forward.1 = (f32[2,4,128,512]{3,2,1,0:T(8,128)}, f32[2,12,512]{2,1,0:T(8,128)}) custom-call(s32[16]{0:T(128)} %concatenate.30.sc, bf16[128,1024]{1,0:T(8,128)(2,1)} %get-tuple-element.21.refs_0_, bf16[128,1024]{1,0:T(8,128)(2,1)} %copy-done.3, bf16[256,1024]{1,0:T(8,128)(2,1)} %copy-done.7, bf16[256,1024]{1,0:T(8,128)(2,1)} %copy-done.6, ...), custom_call_target="tpu_custom_call" | custom-call | flops 3221225472 | bytes 8388608 | tf_op jit(solution)/shard_map/forward/pallas_call | solution.py:311
  59.1 4.5 %collective-permute-done.12 = f32[2,12,512]{2,1,0:T(8,128)S(1)} collective-permute-done((f32[2,12,512]{2,1,0:T(8,128)}, f32[2,12,512]{2,1,0:T(8,128)S(1)}, u32[]{:S(2)}, u32[]{:S(2)}) %collective-permute-start.12) | collective-permute-done | bytes 49184 | tf_op jit(solution)/shard_map/ppermute | solution.py:323
  64.9 3.8 %collective-permute-start.13 = (f32[2,12,512]{2,1,0:T(8,128)S(1)}, f32[2,12,512]{2,1,0:T(8,128)S(1)}, u32[]{:S(2)}, u32[]{:S(2)}) collective-permute-start(f32[2,12,512]{2,1,0:T(8,128)S(1)} %pad_maximum_fusion.2.refs_8_), channel_id=1, source_target_pairs={{0,2},{2,0},{4,6},{6,4},{8,10},{10,8},{12,14},{14,12},{16,18},{18,... | collective-permute-start | bytes 147464 | tf_op jit(solution)/shard_map/ppermute | solution.py:335
  72.3 8.4 %backward_begin.1 = (bf16[4,256,256]{2,1,0:T(8,128)(2,1)}, bf16[2,512,128]{2,1,0:T(8,128)(2,1)}, bf16[2,512,128]{2,1,0:T(8,128)(2,1)}, bf16[2,512,128]{2,1,0:T(8...) custom-call(s32[14]{0:T(128)} %concatenate.26.sc, ...), custom_call_target="tpu_custom_call" | custom-call | flops 2684354560 | bytes 8388608 | tf_op jit(solution)/shard_map/backward_begin/pallas_call | solution.py:346
  80.7 9.1 %backward_end.1 = (bf16[4,256,256]{2,1,0:T(8,128)(2,1)}, bf16[2,512,128]{2,1,0:T(8,128)(2,1)}, bf16[2,512,128]{2,1,0:T(8,128)(2,1)}, bf16[2,512,128]{2,1,0:T(8,128)(2,1)}, bf16[2,512,128]{2,1,0:T(8,128)(2,1)}) custom-call(s32[16]{0:T(128)} %concatenate.30.sc, bf16[128,1024]{1,0:T(8,128)(2,1)} %get-tuple-element.21.refs_0_, bf16[128,1024]{1,0:T(8,128)(2,1)} %copy-done.3, ...), custom_call_target="tpu_custom_call" | custom-call | flops 2684354560 | bytes 8388608 | tf_op jit(solution)/shard_map/backward_end/pallas_call | solution.py:346
  91.1 4.6 %collective-permute-start.18 = (bf16[2,512,128]{2,1,0:T(8,128)(2,1)S(1)}, bf16[2,512,128]{2,1,0:T(8,128)(2,1)S(1)}, u32[]{:S(2)}, u32[]{:S(2)}) collective-permute-start(bf16[2,512,128]{2,1,0:T(8,128)(2,1)S(1)} %copy-done.15), channel_id=1, source_target_pairs={{0,6},{2,4},{4,2},{6,0},{8,14},{10,12},{12,10},{14,8},{16,22},{18,... | collective-permute-start | bytes 786440 | tf_op jit(solution)/shard_map/ppermute | solution.py:366
  96.7 7.0 %collective-permute-done.24 = bf16[256,256]{1,0:T(8,128)(2,1)S(1)} collective-permute-done((bf16[256,256]{1,0:T(8,128)(2,1)S(1)}, bf16[256,256]{1,0:T(8,128)(2,1)S(1)}, u32[]{:S(2)}, u32[]{:S(2)}) %collective-permute-start.24) | collective-permute-done | bytes 131104 | tf_op jit(solution)/shard_map/ppermute | solution.py:368
  103.7 8.3 %collective-permute-start.26 = (bf16[256,256]{1,0:T(8,128)(2,1)S(1)}, bf16[256,256]{1,0:T(8,128)(2,1)S(1)}, u32[]{:S(2)}, u32[]{:S(2)}) collective-permute-start(bf16[256,256]{1,0:T(8,128)(2,1)S(1)} %get-tuple-element.40), channel_id=1, source_target_pairs={{0,64},{2,66},{4,68},{6,70},{8,72},{10,74},{12,76},{14,78},{16,80}... | collective-permute-start | bytes 393224 | tf_op jit(solution)/shard_map/ppermute | solution.py:368
  113.0 2.0 %collective-permute-done.26 = bf16[256,256]{1,0:T(8,128)(2,1)S(1)} collective-permute-done((bf16[256,256]{1,0:T(8,128)(2,1)S(1)}, bf16[256,256]{1,0:T(8,128)(2,1)S(1)}, u32[]{:S(2)}, u32[]{:S(2)}) %collective-permute-start.26) | collective-permute-done | bytes 131104 | tf_op jit(solution)/shard_map/ppermute | solution.py:368
  115.0 6.6 %collective-permute-start.21 = (bf16[2,512,128]{2,1,0:T(8,128)(2,1)}, bf16[2,512,128]{2,1,0:T(8,128)(2,1)S(1)}, u32[]{:S(2)}, u32[]{:S(2)}) collective-permute-start(bf16[2,512,128]{2,1,0:T(8,128)(2,1)} %get-tuple-element.34), channel_id=1, source_target_pairs={{0,4},{2,6},{4,0},{6,2},{8,12},{10,14},{12,8},{14,10},{16,20},{18,... | collective-permute-start | bytes 786440 | tf_op jit(solution)/shard_map/ppermute | solution.py:366
  121.7 2.9 %collective-permute-start.22 = (bf16[2,512,128]{2,1,0:T(8,128)(2,1)S(1)}, bf16[2,512,128]{2,1,0:T(8,128)(2,1)S(1)}, u32[]{:S(2)}, u32[]{:S(2)}) collective-permute-start(bf16[2,512,128]{2,1,0:T(8,128)(2,1)S(1)} %copy-done.14), channel_id=1, source_target_pairs={{0,6},{2,4},{4,2},{6,0},{8,14},{10,12},{12,10},{14,8},{16,22},{18,... | collective-permute-start | bytes 786440 | tf_op jit(solution)/shard_map/ppermute | solution.py:366
  124.7 3.5 %collective-permute-start.25 = (bf16[512,256]{1,0:T(8,128)(2,1)S(1)}, bf16[512,256]{1,0:T(8,128)(2,1)S(1)}, u32[]{:S(2)}, u32[]{:S(2)}) collective-permute-start(bf16[512,256]{1,0:T(8,128)(2,1)S(1)} %pad_maximum_fusion), channel_id=1, source_target_pairs={{0,64},{2,66},{4,68},{6,70},{8,72},{10,74},{12,76},{14,78},{16,80}... | collective-permute-start | bytes 786440 | tf_op jit(solution)/shard_map/ppermute | solution.py:371
  133.0 3.1 %collective-permute-done.27 = bf16[512,256]{1,0:T(8,128)(2,1)S(1)} collective-permute-done((bf16[512,256]{1,0:T(8,128)(2,1)S(1)}, bf16[512,256]{1,0:T(8,128)(2,1)S(1)}, u32[]{:S(2)}, u32[]{:S(2)}) %collective-permute-start.27) | collective-permute-done | bytes 262176 | tf_op jit(solution)/shard_map/ppermute | solution.py:372
  136.8 3.3 %collective-permute-start.30 = (bf16[128,256]{1,0:T(8,128)(2,1)S(1)}, bf16[128,256]{1,0:T(8,128)(2,1)S(1)}, u32[]{:S(2)}, u32[]{:S(2)}) collective-permute-start(bf16[128,256]{1,0:T(8,128)(2,1)S(1)} %get-tuple-element.42), channel_id=1, source_target_pairs={{0,24},{2,26},{4,28},{6,30},{8,16},{10,18},{12,20},{14,22},{16,8},... | collective-permute-start | bytes 196616 | tf_op jit(solution)/shard_map/ppermute | solution.py:375
  (121 shorter events, 31.8 us)
Async XLA Ops:
  2.4 14.8 %collective-permute-start.7 = (bf16[128,256]{1,0:T(8,128)(2,1)}, bf16[128,256]{1,0:T(8,128)(2,1)S(1)}, u32[]{:S(2)}, u32[]{:S(2)}) collective-permute-start(bf16[128,256]{1,0:T(8,128)(2,1)} %get-tuple-element.22), channel_id=1, source_target_pairs={{0,24},{2,26},{4,28},{6,30},{8,16},{10,18},{12,20},{14,22},{16,8},... | collective-permute-start | bytes 196616 | tf_op jit(solution)/shard_map/ppermute | solution.py:271
  5.2 12.0 %collective-permute-start.6 = (bf16[128,256]{1,0:T(8,128)(2,1)}, bf16[128,256]{1,0:T(8,128)(2,1)S(1)}, u32[]{:S(2)}, u32[]{:S(2)}) collective-permute-start(bf16[128,256]{1,0:T(8,128)(2,1)} %get-tuple-element.22), channel_id=1, source_target_pairs={{0,8},{2,10},{4,12},{6,14},{8,0},{10,2},{12,4},{14,6},{16,24},{18,... | collective-permute-start | bytes 196616 | tf_op jit(solution)/shard_map/ppermute | solution.py:271
  6.5 7.4 %collective-permute-start = (bf16[128,1024]{1,0:T(8,128)(2,1)}, bf16[128,1024]{1,0:T(8,128)(2,1)S(1)}, u32[]{:S(2)}, u32[]{:S(2)}) collective-permute-start(bf16[128,1024]{1,0:T(8,128)(2,1)} %get-tuple-element.21.refs_0_), channel_id=1, source_target_pairs={{0,32},{2,34},{4,36},{6,38},{8,40},{10,42},{12,44},{14,46},{16,48}... | collective-permute-start | bytes 786440 | tf_op jit(solution)/shard_map/ppermute | solution.py:273
  14.0 24.4 %collective-permute-start.2 = (bf16[256,1024]{1,0:T(8,128)(2,1)S(1)}, bf16[256,1024]{1,0:T(8,128)(2,1)S(1)}, u32[]{:S(2)}, u32[]{:S(2)}) collective-permute-start(bf16[256,1024]{1,0:T(8,128)(2,1)S(1)} %constant_dynamic-update-slice_fusion), channel_id=1, source_target_pairs={{0,6},{2,4},{4,2},{6,0},{8,14},{10,12},{12,10},{14,8},{16,22},{18,... | collective-permute-start | bytes 1572872 | tf_op jit(solution)/shard_map/ppermute | solution.py:276
  17.1 23.1 %collective-permute-start.1 = (bf16[256,1024]{1,0:T(8,128)(2,1)S(1)}, bf16[256,1024]{1,0:T(8,128)(2,1)S(1)}, u32[]{:S(2)}, u32[]{:S(2)}) collective-permute-start(bf16[256,1024]{1,0:T(8,128)(2,1)S(1)} %constant_dynamic-update-slice_fusion), channel_id=1, source_target_pairs={{0,2},{2,0},{4,6},{6,4},{8,10},{10,8},{12,14},{14,12},{16,18},{18,... | collective-permute-start | bytes 1572872 | tf_op jit(solution)/shard_map/ppermute | solution.py:276
  17.2 15.2 %collective-permute-start.8 = (bf16[512,256]{1,0:T(8,128)(2,1)S(1)}, bf16[512,256]{1,0:T(8,128)(2,1)S(1)}, u32[]{:S(2)}, u32[]{:S(2)}) collective-permute-start(bf16[512,256]{1,0:T(8,128)(2,1)S(1)} %constant_dynamic-update-slice_fusion.2.refs_6_), channel_id=1, source_target_pairs={{0,192},{2,194},{4,196},{6,198},{8,200},{10,202},{12,204},{14,206}... | collective-permute-start | bytes 786440 | tf_op jit(solution)/shard_map/ppermute | solution.py:274
  22.7 11.5 %collective-permute-start.10 = (bf16[512,256]{1,0:T(8,128)(2,1)S(1)}, bf16[512,256]{1,0:T(8,128)(2,1)S(1)}, u32[]{:S(2)}, u32[]{:S(2)}) collective-permute-start(bf16[512,256]{1,0:T(8,128)(2,1)S(1)} %constant_dynamic-update-slice_fusion.2.refs_6_), channel_id=1, source_target_pairs={{0,64},{2,66},{4,68},{6,70},{8,72},{10,74},{12,76},{14,78},{16,80}... | collective-permute-start | bytes 786440 | tf_op jit(solution)/shard_map/ppermute | solution.py:274
  32.5 8.9 %collective-permute-start.9 = (bf16[256,256]{1,0:T(8,128)(2,1)S(1)}, bf16[256,256]{1,0:T(8,128)(2,1)S(1)}, u32[]{:S(2)}, u32[]{:S(2)}) collective-permute-start(bf16[256,256]{1,0:T(8,128)(2,1)S(1)} %slice.134), channel_id=1, source_target_pairs={{0,64},{2,66},{4,68},{6,70},{8,72},{10,74},{12,76},{14,78},{16,80}... | collective-permute-start | bytes 393224 | tf_op jit(solution)/shard_map/ppermute | solution.py:277
  34.2 9.1 %collective-permute-start.11 = (bf16[256,256]{1,0:T(8,128)(2,1)S(1)}, bf16[256,256]{1,0:T(8,128)(2,1)S(1)}, u32[]{:S(2)}, u32[]{:S(2)}) collective-permute-start(bf16[256,256]{1,0:T(8,128)(2,1)S(1)} %slice.135), channel_id=1, source_target_pairs={{0,192},{2,194},{4,196},{6,198},{8,200},{10,202},{12,204},{14,206}... | collective-permute-start | bytes 393224 | tf_op jit(solution)/shard_map/ppermute | solution.py:277
  40.2 7.8 %collective-permute-start.4 = (bf16[128,1024]{1,0:T(8,128)(2,1)S(1)}, bf16[128,1024]{1,0:T(8,128)(2,1)}, u32[]{:S(2)}, u32[]{:S(2)}) collective-permute-start(bf16[128,1024]{1,0:T(8,128)(2,1)S(1)} %slice.133), channel_id=1, source_target_pairs={{0,6},{2,4},{4,2},{6,0},{8,14},{10,12},{12,10},{14,8},{16,22},{18,... | collective-permute-start | bytes 786440 | tf_op jit(solution)/shard_map/ppermute | solution.py:278
  90.8 30.9 %collective-permute-start.16 = (bf16[2,512,128]{2,1,0:T(8,128)(2,1)S(1)}, bf16[2,512,128]{2,1,0:T(8,128)(2,1)S(1)}, u32[]{:S(2)}, u32[]{:S(2)}) collective-permute-start(bf16[2,512,128]{2,1,0:T(8,128)(2,1)S(1)} %copy-done.17), channel_id=1, source_target_pairs={{0,2},{2,0},{4,6},{6,4},{8,10},{10,8},{12,14},{14,12},{16,18},{18,... | collective-permute-start | bytes 786440 | tf_op jit(solution)/shard_map/ppermute | solution.py:366
  91.0 33.7 %collective-permute-start.17 = (bf16[2,512,128]{2,1,0:T(8,128)(2,1)S(1)}, bf16[2,512,128]{2,1,0:T(8,128)(2,1)S(1)}, u32[]{:S(2)}, u32[]{:S(2)}) collective-permute-start(bf16[2,512,128]{2,1,0:T(8,128)(2,1)S(1)} %copy-done.16), channel_id=1, source_target_pairs={{0,4},{2,6},{4,0},{6,2},{8,12},{10,14},{12,8},{14,10},{16,20},{18,... | collective-permute-start | bytes 786440 | tf_op jit(solution)/shard_map/ppermute | solution.py:366
  91.1 33.6 %collective-permute-start.18 = (bf16[2,512,128]{2,1,0:T(8,128)(2,1)S(1)}, bf16[2,512,128]{2,1,0:T(8,128)(2,1)S(1)}, u32[]{:S(2)}, u32[]{:S(2)}) collective-permute-start(bf16[2,512,128]{2,1,0:T(8,128)(2,1)S(1)} %copy-done.15), channel_id=1, source_target_pairs={{0,6},{2,4},{4,2},{6,0},{8,14},{10,12},{12,10},{14,8},{16,22},{18,... | collective-permute-start | bytes 786440 | tf_op jit(solution)/shard_map/ppermute | solution.py:366
  95.6 33.4 %collective-permute-start.20 = (bf16[2,512,128]{2,1,0:T(8,128)(2,1)}, bf16[2,512,128]{2,1,0:T(8,128)(2,1)S(1)}, u32[]{:S(2)}, u32[]{:S(2)}) collective-permute-start(bf16[2,512,128]{2,1,0:T(8,128)(2,1)} %get-tuple-element.33), channel_id=1, source_target_pairs={{0,2},{2,0},{4,6},{6,4},{8,10},{10,8},{12,14},{14,12},{16,18},{18,... | collective-permute-start | bytes 786440 | tf_op jit(solution)/shard_map/ppermute | solution.py:366
  95.7 8.0 %collective-permute-start.24 = (bf16[256,256]{1,0:T(8,128)(2,1)S(1)}, bf16[256,256]{1,0:T(8,128)(2,1)S(1)}, u32[]{:S(2)}, u32[]{:S(2)}) collective-permute-start(bf16[256,256]{1,0:T(8,128)(2,1)S(1)} %get-tuple-element.38), channel_id=1, source_target_pairs={{0,192},{2,194},{4,196},{6,198},{8,200},{10,202},{12,204},{14,206}... | collective-permute-start | bytes 393224 | tf_op jit(solution)/shard_map/ppermute | solution.py:368
  103.7 11.3 %collective-permute-start.26 = (bf16[256,256]{1,0:T(8,128)(2,1)S(1)}, bf16[256,256]{1,0:T(8,128)(2,1)S(1)}, u32[]{:S(2)}, u32[]{:S(2)}) collective-permute-start(bf16[256,256]{1,0:T(8,128)(2,1)S(1)} %get-tuple-element.40), channel_id=1, source_target_pairs={{0,64},{2,66},{4,68},{6,70},{8,72},{10,74},{12,76},{14,78},{16,80}... | collective-permute-start | bytes 393224 | tf_op jit(solution)/shard_map/ppermute | solution.py:368
  115.0 15.8 %collective-permute-start.21 = (bf16[2,512,128]{2,1,0:T(8,128)(2,1)}, bf16[2,512,128]{2,1,0:T(8,128)(2,1)S(1)}, u32[]{:S(2)}, u32[]{:S(2)}) collective-permute-start(bf16[2,512,128]{2,1,0:T(8,128)(2,1)} %get-tuple-element.34), channel_id=1, source_target_pairs={{0,4},{2,6},{4,0},{6,2},{8,12},{10,14},{12,8},{14,10},{16,20},{18,... | collective-permute-start | bytes 786440 | tf_op jit(solution)/shard_map/ppermute | solution.py:366
  121.7 9.1 %collective-permute-start.22 = (bf16[2,512,128]{2,1,0:T(8,128)(2,1)S(1)}, bf16[2,512,128]{2,1,0:T(8,128)(2,1)S(1)}, u32[]{:S(2)}, u32[]{:S(2)}) collective-permute-start(bf16[2,512,128]{2,1,0:T(8,128)(2,1)S(1)} %copy-done.14), channel_id=1, source_target_pairs={{0,6},{2,4},{4,2},{6,0},{8,14},{10,12},{12,10},{14,8},{16,22},{18,... | collective-permute-start | bytes 786440 | tf_op jit(solution)/shard_map/ppermute | solution.py:366
  124.7 11.4 %collective-permute-start.27 = (bf16[512,256]{1,0:T(8,128)(2,1)S(1)}, bf16[512,256]{1,0:T(8,128)(2,1)S(1)}, u32[]{:S(2)}, u32[]{:S(2)}) collective-permute-start(bf16[512,256]{1,0:T(8,128)(2,1)S(1)} %pad_maximum_fusion.1), channel_id=1, source_target_pairs={{0,192},{2,194},{4,196},{6,198},{8,200},{10,202},{12,204},{14,206}... | collective-permute-start | bytes 786440 | tf_op jit(solution)/shard_map/ppermute | solution.py:372
  124.7 11.4 %collective-permute-start.25 = (bf16[512,256]{1,0:T(8,128)(2,1)S(1)}, bf16[512,256]{1,0:T(8,128)(2,1)S(1)}, u32[]{:S(2)}, u32[]{:S(2)}) collective-permute-start(bf16[512,256]{1,0:T(8,128)(2,1)S(1)} %pad_maximum_fusion), channel_id=1, source_target_pairs={{0,64},{2,66},{4,68},{6,70},{8,72},{10,74},{12,76},{14,78},{16,80}... | collective-permute-start | bytes 786440 | tf_op jit(solution)/shard_map/ppermute | solution.py:371
  129.0 12.4 %collective-permute-start.19 = (bf16[512,128]{1,0:T(8,128)(2,1)S(1)}, bf16[512,128]{1,0:T(8,128)(2,1)S(1)}, u32[]{:S(2)}, u32[]{:S(2)}) collective-permute-start(bf16[512,128]{1,0:T(8,128)(2,1)S(1)} %get-tuple-element.46), channel_id=1, source_target_pairs={{0,32},{2,34},{4,36},{6,38},{8,40},{10,42},{12,44},{14,46},{16,48}... | collective-permute-start | bytes 393224 | tf_op jit(solution)/shard_map/ppermute | solution.py:370
  131.7 12.2 %collective-permute-start.23 = (bf16[512,128]{1,0:T(8,128)(2,1)S(1)}, bf16[512,128]{1,0:T(8,128)(2,1)S(1)}, u32[]{:S(2)}, u32[]{:S(2)}) collective-permute-start(bf16[512,128]{1,0:T(8,128)(2,1)S(1)} %get-tuple-element.44), channel_id=1, source_target_pairs={{0,32},{2,34},{4,36},{6,38},{8,40},{10,42},{12,44},{14,46},{16,48}... | collective-permute-start | bytes 393224 | tf_op jit(solution)/shard_map/ppermute | solution.py:376
  136.2 10.0 %collective-permute-start.28 = (bf16[128,256]{1,0:T(8,128)(2,1)S(1)}, bf16[128,256]{1,0:T(8,128)(2,1)S(1)}, u32[]{:S(2)}, u32[]{:S(2)}) collective-permute-start(bf16[128,256]{1,0:T(8,128)(2,1)S(1)} %get-tuple-element.41), channel_id=1, source_target_pairs={{0,16},{2,18},{4,20},{6,22},{8,24},{10,26},{12,28},{14,30},{16,0},... | collective-permute-start | bytes 196616 | tf_op jit(solution)/shard_map/ppermute | solution.py:375
  136.8 9.4 %collective-permute-start.30 = (bf16[128,256]{1,0:T(8,128)(2,1)S(1)}, bf16[128,256]{1,0:T(8,128)(2,1)S(1)}, u32[]{:S(2)}, u32[]{:S(2)}) collective-permute-start(bf16[128,256]{1,0:T(8,128)(2,1)S(1)} %get-tuple-element.42), channel_id=1, source_target_pairs={{0,24},{2,26},{4,28},{6,30},{8,16},{10,18},{12,20},{14,22},{16,8},... | collective-permute-start | bytes 196616 | tf_op jit(solution)/shard_map/ppermute | solution.py:375
  (28 other events, 342.0 us)

commit v4 on v3

--- a/solution.py
+++ b/solution.py
@@ -248,6 +248,69 @@
         out[:, at] = jnp.transpose(whole).astype(BF16)
 
 
+SMEM = pl.BlockSpec(memory_space=pltpu.SMEM)
+VMEM = pl.BlockSpec(memory_space=pltpu.VMEM)
+PARAMS = pltpu.CompilerParams(vmem_limit_bytes=28 * 1024 * 1024)
+
+
+def cost(group, width, dots, pieces):
+    work = TILES * ROWS * group * pieces * 2 * PAIR * width * 2
+    return pl.CostEstimate(flops=2 * dots * work, bytes_accessed=1 << 23, transcendentals=0)
+
+
+def scratch(group, width, pieces):
+    return [
+        pltpu.VMEM((TILES, group, ROWS, width), BF16),
+        pltpu.VMEM((TILES, group, ROWS, width), BF16),
+        pltpu.VMEM((2 * pieces, PAIR, width), BF16),
+        pltpu.VMEM((2 * pieces, PAIR, width), BF16),
+        pltpu.VMEM((2 * pieces, width, PAIR), BF16),
+    ]
+
+
+def state_shapes(group, width):
+    acc = jax.ShapeDtypeStruct((TILES, group, width, ROWS), F32)
+    line = jax.ShapeDtypeStruct((TILES, group, 1, ROWS), F32)
+    return [acc, line, line]
+
+
+def run_forward(group, width, sc, rows, keys):
+    pieces = len(keys)
+    acc, line, _ = state_shapes(group, width)
+    return pl.pallas_call(
+        functools.partial(forward, group, width, pieces),
+        out_shape=[acc, jax.ShapeDtypeStruct((TILES, 3 * group, ROWS), F32)],
+        in_specs=[SMEM] + [VMEM] * (6 + pieces),
+        out_specs=[VMEM] * 2,
+        scratch_shapes=scratch(group, width, pieces) + [pltpu.VMEM(line.shape, F32)] * 3,
+        compiler_params=PARAMS,
+        cost_estimate=cost(group, width, 3, pieces),
+        name="forward",
+    )(sc, *rows, *keys)
+
+
+def run_backward(group, width, begins, sc, rows, keys, *more):
+    pieces = len(keys)
+    carried = state_shapes(group, width)
+    piece = jax.ShapeDtypeStruct((TILES, group * width, CHUNK), BF16)
+    shapes = [jax.ShapeDtypeStruct((2 * pieces, PAIR, 2 * width), BF16)] + [piece] * SLOTS
+    spaces = scratch(group, width, pieces) + [pltpu.VMEM((PAIR, 2 * width), F32)]
+    if begins:
+        shapes = shapes + carried
+    else:
+        spaces = [pltpu.VMEM(s.shape, F32) for s in carried] + spaces
+    return pl.pallas_call(
+        functools.partial(backward, group, width, pieces, begins, not begins),
+        out_shape=shapes,
+        in_specs=[SMEM] + [VMEM] * (6 + pieces + len(more)),
+        out_specs=[VMEM] * len(shapes),
+        scratch_shapes=spaces,
+        compiler_params=PARAMS,
+        cost_estimate=cost(group, width, 5, pieces),
+        name="backward_begin" if begins else "backward_end",
+    )(sc, *rows, *keys, *more)
+
+
 def add(*parts):
     return sum(part.astype(F32) for part in parts).astype(BF16)
 
@@ -285,40 +348,7 @@
     sources = jnp.stack([z, z + side, z - side, z + 4]) & 7
     sc = jnp.concatenate([jnp.stack([z, x_lo, x_hi, y]), starts, sources]).astype(jnp.int32)
 
-    smem = pl.BlockSpec(memory_space=pltpu.SMEM)
-    vmem = pl.BlockSpec(memory_space=pltpu.VMEM)
-    params = pltpu.CompilerParams(vmem_limit_bytes=56 * 1024 * 1024)
-
-    def cost(dots, pieces):
-        work = TILES * ROWS * group * pieces * 2 * PAIR * width * 2
-        return pl.CostEstimate(flops=dots * work // 2, bytes_accessed=1 << 23, transcendentals=0)
-
-    def scratch(pieces):
-        return [
-            pltpu.VMEM((TILES, group, ROWS, width), BF16),
-            pltpu.VMEM((TILES, group, ROWS, width), BF16),
-            pltpu.VMEM((2 * pieces, PAIR, width), BF16),
-            pltpu.VMEM((2 * pieces, PAIR, width), BF16),
-            pltpu.VMEM((2 * pieces, width, PAIR), BF16),
-        ]
-
-    line = (TILES, group, 1, ROWS)
-    acc_shape = jax.ShapeDtypeStruct((TILES, group, width, ROWS), F32)
-    line_shape = jax.ShapeDtypeStruct(line, F32)
-    stat_shape = jax.ShapeDtypeStruct((TILES, 3 * group, ROWS), F32)
-    piece = jax.ShapeDtypeStruct((TILES, group * width, CHUNK), BF16)
-
-    values, stat = pl.pallas_call(
-        functools.partial(forward, group, width, 4),
-        out_shape=[acc_shape, stat_shape],
-        in_specs=[smem] + [vmem] * 10,
-        out_specs=[vmem] * 2,
-        scratch_shapes=scratch(4) + [pltpu.VMEM(line, F32)] * 3,
-        compiler_params=params,
-        cost_estimate=cost(3, 4),
-        name="forward",
-    )(sc, *rows, *keys)
-
+    values, stat = run_forward(group, width, sc, rows, keys)
     unit = LOG2E / math.sqrt(width)
     other = send(stat, perm=NEXT)[::-1]
     top = jnp.maximum(stat[:, :group], other[:, :group])
@@ -334,32 +364,12 @@
     )
     stats = [merged] + [send(merged, perm=Y[s]) for s in range(1, SLOTS)]
 
-    def back(pieces, begins, ends, sc, keys, *more):
-        dkv_shape = jax.ShapeDtypeStruct((2 * pieces, PAIR, 2 * width), BF16)
-        shapes = [dkv_shape] + [piece] * (SLOTS * (begins + ends))
-        carried = [acc_shape, line_shape, line_shape]
-        more_scratch = scratch(pieces) + [pltpu.VMEM((PAIR, 2 * width), F32)]
-        if ends:
-            more_scratch = [pltpu.VMEM(s.shape, F32) for s in carried] + more_scratch
-        else:
-            shapes = shapes + carried
-        return pl.pallas_call(
-            functools.partial(backward, group, width, pieces, begins, ends),
-            out_shape=shapes,
-            in_specs=[smem] + [vmem] * (6 + pieces + len(more)),
-            out_specs=[vmem] * len(shapes),
-            scratch_shapes=more_scratch,
-            compiler_params=params,
-            cost_estimate=cost(5, pieces),
-            name="backward_begin" if begins else "backward_end",
-        )(sc, *rows, *keys, *more)
-
     def shifted(skip):
         return jnp.concatenate([sc[: 4 + DOCS], sc[4 + DOCS + skip :]])
 
-    late = back(2, True, False, shifted(2), keys[2:], *stats, stat, values)
+    late = run_backward(group, width, True, shifted(2), rows, keys[2:], *stats, stat, values)
     far, mixed, carried = late[0], late[1 : 1 + SLOTS], late[1 + SLOTS :]
-    end = back(2, False, True, sc, keys[:2], *carried)
+    end = run_backward(group, width, False, sc, rows, keys[:2], *carried)
     close, dq = end[0], end[1:]
 
     def over_y(parts):
@@ -379,8 +389,8 @@
         pl.pallas_call(
             functools.partial(combine, group, width),
             out_shape=jax.ShapeDtypeStruct((CHUNK, group * width), BF16),
-            in_specs=[vmem] * TILES,
-            out_specs=vmem,
+            in_specs=[VMEM] * TILES,
+            out_specs=VMEM,
             name=name,
         )(*parts)
         for parts, name in ((mixed, "attended"), (dq, "grad_query"))

time: 147 us -> 142 us (0.966); the launches traced: 147 us -> 140 us
  Pallas kernels: 33.8 us -> 19.4 us
  starting transfers between devices: 62.1 us -> 66.2 us
  local copies, waits for them, and re-layouts: 9.22 us -> 13.1 us
  other arithmetic: 2.68 us -> 0.93 us
    pallas_call x3, Pallas kernels: 28.6 us -> 14.1 us  [the longest x2 8.04 us: run_backward(): pl.pallas_call(functools.partial(backward, group, width, pieces, begins,...]
    ppermute x1, starting transfers between devices: 0.01 us -> 8.21 us  [local(): gb = send(jnp.concatenate([add(far[0], one), far[1]], axis=0), perm=REST)]
    ppermute x2, starting transfers between devices: 8.42 us -> 13.3 us  [local(): one, two = (send(far[2], perm=NEAR), send(far[3], perm=REST))]
    ppermute x6, starting transfers between devices: 14.3 us -> 9.52 us  [over_y(): return add(parts[0], *[send(parts[s], perm=Y[s]) for s in range(1, SLOTS)])]
    unnamed x47 -> x17, local copies, waits for them, and re-layouts: 3.85 us -> 7.73 us
    ppermute x1, starting transfers between devices: 3.53 us -> 0.01 us  [local(): send(jnp.concatenate([close[2], add(close[3], two)], axis=0), perm=NEAR)]
    ppermute x1, waiting for transfers between devices: 0.01 us -> 1.77 us  [local(): send(jnp.concatenate([close[2], add(close[3], two)], axis=0), perm=NEAR)]
  transfers between devices with their start and end apart: 31 -> 31, of which waited for: 13 -> 13; matrix products, arithmetic and copies ran while one was open for 5% -> 6% of each run, Pallas kernels for 2% -> 2%
where the time goes in v4:
time: 142 us; the launch traced here: 140 us
  starting transfers between devices  66.2 us (47%)
  waiting for transfers between devices  39.3 us (28%)
  Pallas kernels  19.4 us (14%)
  local copies, waits for them, and re-layouts  13.1 us (9%)
    ppermute x2, starting transfers between devices, local(): one, two = (send(far[2], perm=NEAR), send(far[3], perm=REST))  13.3 us
    ppermute x6, starting transfers between devices, over_y(): return add(parts[0], *[send(parts[s], perm=Y[s]) for s in range(1, SLOTS)])  9.52 us
    ppermute x2, waiting for transfers between devices, local(): one, two = (send(far[2], perm=NEAR), send(far[3], perm=REST))  9.41 us
    ppermute x2, waiting for transfers between devices, local(): a, b = (send(own, perm=NEAR), send(own, perm=REST))  8.91 us
    ppermute x1, starting transfers between devices, local(): gb = send(jnp.concatenate([add(far[0], one), far[1]], axis=0), perm=REST)  8.21 us
    pallas_call x2, Pallas kernels, run_backward(): pl.pallas_call(functools.partial(backward, group, width, pieces, begins,...  8.04 us
    unnamed x17, local copies, waits for them, and re-layouts  7.73 us
    ppermute x2, starting transfers between devices, local(): a, b = (send(own, perm=NEAR), send(own, perm=REST))  6.94 us
  transfers between devices with their start and end apart: 31, of which 13 were waited for; matrix products, arithmetic and copies ran while one was open for 6% of the time, Pallas kernels for 2%

profile of v4, /device:TPU:32, one launch (start us, length us, event | category | flops | bytes accessed | tf_op | source)
XLA Modules:
  0.0 139.8 jit_solution(1110284975737517058)
XLA Ops:
  0.6 1.8 %pack.1 = (bf16[128,1024]{1,0:T(8,128)(2,1)}, bf16[128,256]{1,0:T(8,128)(2,1)}) custom-call(bf16[128,512]{1,0:T(8,128)(2,1)} %query.1, bf16[128,128]{1,0:T(8,128)(2,1)} %key.1, bf16[128,128]{1,0:T(8,128)(2,1)} %value.1, bf16[128,512]{1,0:T(8,128)(2,1)} %dout.1), custom_call_target="tpu_custom_call" | custom-call | tf_op jit(solution)/shard_map/pack/pallas_call | solution.py:325
  2.4 2.8 %collective-permute-start.7 = (bf16[128,256]{1,0:T(8,128)(2,1)}, bf16[128,256]{1,0:T(8,128)(2,1)S(1)}, u32[]{:S(2)}, u32[]{:S(2)}) collective-permute-start(bf16[128,256]{1,0:T(8,128)(2,1)} %get-tuple-element.22), channel_id=1, source_target_pairs={{0,24},{2,26},{4,28},{6,30},{8,16},{10,18},{12,20},{14,22},{16,8},... | collective-permute-start | bytes 196616 | tf_op jit(solution)/shard_map/ppermute | solution.py:334
  6.5 1.8 %collective-permute-start = (bf16[128,1024]{1,0:T(8,128)(2,1)}, bf16[128,1024]{1,0:T(8,128)(2,1)S(1)}, u32[]{:S(2)}, u32[]{:S(2)}) collective-permute-start(bf16[128,1024]{1,0:T(8,128)(2,1)} %get-tuple-element.21.refs_0_), channel_id=1, source_target_pairs={{0,32},{2,34},{4,36},{6,38},{8,40},{10,42},{12,44},{14,46},{16,48}... | collective-permute-start | bytes 786440 | tf_op jit(solution)/shard_map/ppermute | solution.py:336
  10.9 3.0 %collective-permute-done.refs_1_ = bf16[128,1024]{1,0:T(8,128)(2,1)S(1)} collective-permute-done((bf16[128,1024]{1,0:T(8,128)(2,1)}, bf16[128,1024]{1,0:T(8,128)(2,1)S(1)}, u32[]{:S(2)}, u32[]{:S(2)}) %collective-permute-start) | collective-permute-done | bytes 262176 | tf_op jit(solution)/shard_map/ppermute | solution.py:336
  14.7 3.0 %collective-permute-start.2 = (bf16[256,1024]{1,0:T(8,128)(2,1)}, bf16[256,1024]{1,0:T(8,128)(2,1)S(1)}, u32[]{:S(2)}, u32[]{:S(2)}) collective-permute-start(bf16[256,1024]{1,0:T(8,128)(2,1)} %constant_dynamic-update-slice_fusion), channel_id=1, source_target_pairs={{0,6},{2,4},{4,2},{6,0},{8,14},{10,12},{12,10},{14,8},{16,22},{18,... | collective-permute-start | bytes 1572872 | tf_op jit(solution)/shard_map/ppermute | solution.py:339
  17.9 5.5 %collective-permute-start.8 = (bf16[512,256]{1,0:T(8,128)(2,1)S(1)}, bf16[512,256]{1,0:T(8,128)(2,1)S(1)}, u32[]{:S(2)}, u32[]{:S(2)}) collective-permute-start(bf16[512,256]{1,0:T(8,128)(2,1)S(1)} %constant_dynamic-update-slice_fusion.2.refs_6_), channel_id=1, source_target_pairs={{0,192},{2,194},{4,196},{6,198},{8,200},{10,202},{12,204},{14,206}... | collective-permute-start | bytes 786440 | tf_op jit(solution)/shard_map/ppermute | solution.py:337
  24.8 8.3 %collective-permute-done.8.refs_8_.refs_6_ = bf16[512,256]{1,0:T(8,128)(2,1)S(1)} collective-permute-done((bf16[512,256]{1,0:T(8,128)(2,1)S(1)}, bf16[512,256]{1,0:T(8,128)(2,1)S(1)}, u32[]{:S(2)}, u32[]{:S(2)}) %collective-permute-start.8) | collective-permute-done | bytes 262176 | tf_op jit(solution)/shard_map/ppermute | solution.py:337
  35.5 4.0 %collective-permute-start.11 = (bf16[256,256]{1,0:T(8,128)(2,1)}, bf16[256,256]{1,0:T(8,128)(2,1)}, u32[]{:S(2)}, u32[]{:S(2)}) collective-permute-start(bf16[256,256]{1,0:T(8,128)(2,1)} %slice.135), channel_id=1, source_target_pairs={{0,192},{2,194},{4,196},{6,198},{8,200},{10,202},{12,204},{14,206}... | collective-permute-start | bytes 393224 | tf_op jit(solution)/shard_map/ppermute | solution.py:340
  39.5 1.8 %collective-permute-start.3 = (bf16[128,1024]{1,0:T(8,128)(2,1)S(1)}, bf16[128,1024]{1,0:T(8,128)(2,1)S(1)}, u32[]{:S(2)}, u32[]{:S(2)}) collective-permute-start(bf16[128,1024]{1,0:T(8,128)(2,1)S(1)} %slice.132), channel_id=1, source_target_pairs={{0,2},{2,0},{4,6},{6,4},{8,10},{10,8},{12,14},{14,12},{16,18},{18,... | collective-permute-start | bytes 786440 | tf_op jit(solution)/shard_map/ppermute | solution.py:341
  46.1 3.8 %collective-permute-done.4.refs_5_ = bf16[128,1024]{1,0:T(8,128)(2,1)S(1)} collective-permute-done((bf16[128,1024]{1,0:T(8,128)(2,1)}, bf16[128,1024]{1,0:T(8,128)(2,1)S(1)}, u32[]{:S(2)}, u32[]{:S(2)}) %collective-permute-start.4) | collective-permute-done | bytes 262176 | tf_op jit(solution)/shard_map/ppermute | solution.py:341
  49.8 6.1 %forward.1 = (f32[2,4,128,512]{3,2,1,0:T(8,128)S(1)}, f32[2,12,512]{2,1,0:T(8,128)S(1)}) custom-call(s32[16]{0:T(128)S(1)} %concatenate.30.sc, bf16[128,1024]{1,0:T(8,128)(2,1)S(1)} %copy-done, bf16[128,1024]{1,0:T(8,128)(2,1)S(1)} %collective-permute-done.refs_1_, bf16[256,1024]{1,0:T(8,128)(2,1)S(1)} %collective-permute-done.1.refs_2_, ...), custom_call_target="tpu_custom_call" | custom-call | flops 12884901888 | bytes 8388608 | tf_op jit(solution)/shard_map/forward/pallas_call | solution.py:280
  57.3 4.3 %collective-permute-done.12 = f32[2,12,512]{2,1,0:T(8,128)S(1)} collective-permute-done((f32[2,12,512]{2,1,0:T(8,128)S(1)}, f32[2,12,512]{2,1,0:T(8,128)S(1)}, u32[]{:S(2)}, u32[]{:S(2)}) %collective-permute-start.12) | collective-permute-done | bytes 49184 | tf_op jit(solution)/shard_map/ppermute | solution.py:353
  61.8 4.0 %collective-permute-start.13 = (f32[2,12,512]{2,1,0:T(8,128)S(1)}, f32[2,12,512]{2,1,0:T(8,128)S(1)}, u32[]{:S(2)}, u32[]{:S(2)}) collective-permute-start(f32[2,12,512]{2,1,0:T(8,128)S(1)} %pad_maximum_fusion.2.refs_8_), channel_id=1, source_target_pairs={{0,2},{2,0},{4,6},{6,4},{8,10},{10,8},{12,14},{14,12},{16,18},{18,... | collective-permute-start | bytes 147464 | tf_op jit(solution)/shard_map/ppermute | solution.py:365
  66.0 1.9 %collective-permute-done.15.refs_11_ = f32[2,12,512]{2,1,0:T(8,128)S(1)} collective-permute-done((f32[2,12,512]{2,1,0:T(8,128)S(1)}, f32[2,12,512]{2,1,0:T(8,128)S(1)}, u32[]{:S(2)}, u32[]{:S(2)}) %collective-permute-start.15) | collective-permute-done | bytes 49184 | tf_op jit(solution)/shard_map/ppermute | solution.py:365
  70.3 4.8 %backward_begin.1 = (bf16[4,256,256]{2,1,0:T(8,128)(2,1)S(1)}, bf16[2,512,128]{2,1,0:T(8,128)(2,1)S(1)}, bf16[2,512,128]{2,1,0:T(8,128)(2,1)S(1)}, bf16[2,512,12...) custom-call(s32[14]{0:T(128)S(1)} %concatenate.26.sc, ...), custom_call_target="tpu_custom_call" | custom-call | flops 10737418240 | bytes 8388608 | tf_op jit(solution)/shard_map/backward_begin/pallas_call | solution.py:302
  75.1 3.3 %backward_end.1 = (bf16[4,256,256]{2,1,0:T(8,128)(2,1)S(1)}, bf16[2,512,128]{2,1,0:T(8,128)(2,1)S(1)}, bf16[2,512,128]{2,1,0:T(8,128)(2,1)S(1)}, bf16[2,512,128]...) custom-call(s32[16]{0:T(128)S(1)} %concatenate.30.sc, bf16[128,1024]{1,0:T(8,128)(2,1)S(1)} %copy-done, ...), custom_call_target="tpu_custom_call" | custom-call | flops 10737418240 | bytes 8388608 | tf_op jit(solution)/shard_map/backward_end/pallas_call | solution.py:302
  78.6 4.6 %collective-permute-start.18 = (bf16[2,512,128]{2,1,0:T(8,128)(2,1)S(1)}, bf16[2,512,128]{2,1,0:T(8,128)(2,1)S(1)}, u32[]{:S(2)}, u32[]{:S(2)}) collective-permute-start(bf16[2,512,128]{2,1,0:T(8,128)(2,1)S(1)} %get-tuple-element.28), channel_id=1, source_target_pairs={{0,6},{2,4},{4,2},{6,0},{8,14},{10,12},{12,10},{14,8},{16,22},{18,... | collective-permute-start | bytes 786440 | tf_op jit(solution)/shard_map/ppermute | solution.py:376
  83.2 13.3 %collective-permute-start.24 = (bf16[256,256]{1,0:T(8,128)(2,1)S(1)}, bf16[256,256]{1,0:T(8,128)(2,1)S(1)}, u32[]{:S(2)}, u32[]{:S(2)}) collective-permute-start(bf16[256,256]{1,0:T(8,128)(2,1)S(1)} %get-tuple-element.38), channel_id=1, source_target_pairs={{0,192},{2,194},{4,196},{6,198},{8,200},{10,202},{12,204},{14,206}... | collective-permute-start | bytes 393224 | tf_op jit(solution)/shard_map/ppermute | solution.py:378
  96.5 3.5 %collective-permute-done.24 = bf16[256,256]{1,0:T(8,128)(2,1)S(1)} collective-permute-done((bf16[256,256]{1,0:T(8,128)(2,1)S(1)}, bf16[256,256]{1,0:T(8,128)(2,1)S(1)}, u32[]{:S(2)}, u32[]{:S(2)}) %collective-permute-start.24) | collective-permute-done | bytes 131104 | tf_op jit(solution)/shard_map/ppermute | solution.py:378
  100.1 5.9 %collective-permute-done.26 = bf16[256,256]{1,0:T(8,128)(2,1)S(1)} collective-permute-done((bf16[256,256]{1,0:T(8,128)(2,1)S(1)}, bf16[256,256]{1,0:T(8,128)(2,1)S(1)}, u32[]{:S(2)}, u32[]{:S(2)}) %collective-permute-start.26) | collective-permute-done | bytes 131104 | tf_op jit(solution)/shard_map/ppermute | solution.py:378
  106.0 3.1 %collective-permute-start.21 = (bf16[2,512,128]{2,1,0:T(8,128)(2,1)S(1)}, bf16[2,512,128]{2,1,0:T(8,128)(2,1)S(1)}, u32[]{:S(2)}, u32[]{:S(2)}) collective-permute-start(bf16[2,512,128]{2,1,0:T(8,128)(2,1)S(1)} %get-tuple-element.34), channel_id=1, source_target_pairs={{0,4},{2,6},{4,0},{6,2},{8,12},{10,14},{12,8},{14,10},{16,20},{18,... | collective-permute-start | bytes 786440 | tf_op jit(solution)/shard_map/ppermute | solution.py:376
  110.8 8.2 %collective-permute-start.27 = (bf16[512,256]{1,0:T(8,128)(2,1)S(1)}, bf16[512,256]{1,0:T(8,128)(2,1)S(1)}, u32[]{:S(2)}, u32[]{:S(2)}) collective-permute-start(bf16[512,256]{1,0:T(8,128)(2,1)S(1)} %pad_maximum_fusion.1), channel_id=1, source_target_pairs={{0,192},{2,194},{4,196},{6,198},{8,200},{10,202},{12,204},{14,206}... | collective-permute-start | bytes 786440 | tf_op jit(solution)/shard_map/ppermute | solution.py:382
  122.7 3.6 %collective-permute-done.27 = bf16[512,256]{1,0:T(8,128)(2,1)S(1)} collective-permute-done((bf16[512,256]{1,0:T(8,128)(2,1)S(1)}, bf16[512,256]{1,0:T(8,128)(2,1)S(1)}, u32[]{:S(2)}, u32[]{:S(2)}) %collective-permute-start.27) | collective-permute-done | bytes 262176 | tf_op jit(solution)/shard_map/ppermute | solution.py:382
  128.8 4.1 %collective-permute-start.30 = (bf16[128,256]{1,0:T(8,128)(2,1)S(1)}, bf16[128,256]{1,0:T(8,128)(2,1)S(1)}, u32[]{:S(2)}, u32[]{:S(2)}) collective-permute-start(bf16[128,256]{1,0:T(8,128)(2,1)S(1)} %get-tuple-element.42), channel_id=1, source_target_pairs={{0,24},{2,26},{4,28},{6,30},{8,16},{10,18},{12,20},{14,22},{16,8},... | collective-permute-start | bytes 196616 | tf_op jit(solution)/shard_map/ppermute | solution.py:385
  (91 shorter events, 32.5 us)
Async XLA Ops:
  2.4 15.4 %collective-permute-start.7 = (bf16[128,256]{1,0:T(8,128)(2,1)}, bf16[128,256]{1,0:T(8,128)(2,1)S(1)}, u32[]{:S(2)}, u32[]{:S(2)}) collective-permute-start(bf16[128,256]{1,0:T(8,128)(2,1)} %get-tuple-element.22), channel_id=1, source_target_pairs={{0,24},{2,26},{4,28},{6,30},{8,16},{10,18},{12,20},{14,22},{16,8},... | collective-permute-start | bytes 196616 | tf_op jit(solution)/shard_map/ppermute | solution.py:334
  5.2 12.6 %collective-permute-start.6 = (bf16[128,256]{1,0:T(8,128)(2,1)}, bf16[128,256]{1,0:T(8,128)(2,1)S(1)}, u32[]{:S(2)}, u32[]{:S(2)}) collective-permute-start(bf16[128,256]{1,0:T(8,128)(2,1)} %get-tuple-element.22), channel_id=1, source_target_pairs={{0,8},{2,10},{4,12},{6,14},{8,0},{10,2},{12,4},{14,6},{16,24},{18,... | collective-permute-start | bytes 196616 | tf_op jit(solution)/shard_map/ppermute | solution.py:334
  6.5 7.4 %collective-permute-start = (bf16[128,1024]{1,0:T(8,128)(2,1)}, bf16[128,1024]{1,0:T(8,128)(2,1)S(1)}, u32[]{:S(2)}, u32[]{:S(2)}) collective-permute-start(bf16[128,1024]{1,0:T(8,128)(2,1)} %get-tuple-element.21.refs_0_), channel_id=1, source_target_pairs={{0,32},{2,34},{4,36},{6,38},{8,40},{10,42},{12,44},{14,46},{16,48}... | collective-permute-start | bytes 786440 | tf_op jit(solution)/shard_map/ppermute | solution.py:336
  14.7 24.8 %collective-permute-start.2 = (bf16[256,1024]{1,0:T(8,128)(2,1)}, bf16[256,1024]{1,0:T(8,128)(2,1)S(1)}, u32[]{:S(2)}, u32[]{:S(2)}) collective-permute-start(bf16[256,1024]{1,0:T(8,128)(2,1)} %constant_dynamic-update-slice_fusion), channel_id=1, source_target_pairs={{0,6},{2,4},{4,2},{6,0},{8,14},{10,12},{12,10},{14,8},{16,22},{18,... | collective-permute-start | bytes 1572872 | tf_op jit(solution)/shard_map/ppermute | solution.py:339
  17.7 23.6 %collective-permute-start.1 = (bf16[256,1024]{1,0:T(8,128)(2,1)}, bf16[256,1024]{1,0:T(8,128)(2,1)S(1)}, u32[]{:S(2)}, u32[]{:S(2)}) collective-permute-start(bf16[256,1024]{1,0:T(8,128)(2,1)} %constant_dynamic-update-slice_fusion), channel_id=1, source_target_pairs={{0,2},{2,0},{4,6},{6,4},{8,10},{10,8},{12,14},{14,12},{16,18},{18,... | collective-permute-start | bytes 1572872 | tf_op jit(solution)/shard_map/ppermute | solution.py:339
  17.9 15.2 %collective-permute-start.8 = (bf16[512,256]{1,0:T(8,128)(2,1)S(1)}, bf16[512,256]{1,0:T(8,128)(2,1)S(1)}, u32[]{:S(2)}, u32[]{:S(2)}) collective-permute-start(bf16[512,256]{1,0:T(8,128)(2,1)S(1)} %constant_dynamic-update-slice_fusion.2.refs_6_), channel_id=1, source_target_pairs={{0,192},{2,194},{4,196},{6,198},{8,200},{10,202},{12,204},{14,206}... | collective-permute-start | bytes 786440 | tf_op jit(solution)/shard_map/ppermute | solution.py:337
  23.3 11.5 %collective-permute-start.10 = (bf16[512,256]{1,0:T(8,128)(2,1)S(1)}, bf16[512,256]{1,0:T(8,128)(2,1)S(1)}, u32[]{:S(2)}, u32[]{:S(2)}) collective-permute-start(bf16[512,256]{1,0:T(8,128)(2,1)S(1)} %constant_dynamic-update-slice_fusion.2.refs_6_), channel_id=1, source_target_pairs={{0,64},{2,66},{4,68},{6,70},{8,72},{10,74},{12,76},{14,78},{16,80}... | collective-permute-start | bytes 786440 | tf_op jit(solution)/shard_map/ppermute | solution.py:337
  33.1 9.4 %collective-permute-start.9 = (bf16[256,256]{1,0:T(8,128)(2,1)S(1)}, bf16[256,256]{1,0:T(8,128)(2,1)}, u32[]{:S(2)}, u32[]{:S(2)}) collective-permute-start(bf16[256,256]{1,0:T(8,128)(2,1)S(1)} %slice.134), channel_id=1, source_target_pairs={{0,64},{2,66},{4,68},{6,70},{8,72},{10,74},{12,76},{14,78},{16,80}... | collective-permute-start | bytes 393224 | tf_op jit(solution)/shard_map/ppermute | solution.py:340
  35.5 9.3 %collective-permute-start.11 = (bf16[256,256]{1,0:T(8,128)(2,1)}, bf16[256,256]{1,0:T(8,128)(2,1)}, u32[]{:S(2)}, u32[]{:S(2)}) collective-permute-start(bf16[256,256]{1,0:T(8,128)(2,1)} %slice.135), channel_id=1, source_target_pairs={{0,192},{2,194},{4,196},{6,198},{8,200},{10,202},{12,204},{14,206}... | collective-permute-start | bytes 393224 | tf_op jit(solution)/shard_map/ppermute | solution.py:340
  42.0 7.8 %collective-permute-start.4 = (bf16[128,1024]{1,0:T(8,128)(2,1)}, bf16[128,1024]{1,0:T(8,128)(2,1)S(1)}, u32[]{:S(2)}, u32[]{:S(2)}) collective-permute-start(bf16[128,1024]{1,0:T(8,128)(2,1)} %slice.133), channel_id=1, source_target_pairs={{0,6},{2,4},{4,2},{6,0},{8,14},{10,12},{12,10},{14,8},{16,22},{18,... | collective-permute-start | bytes 786440 | tf_op jit(solution)/shard_map/ppermute | solution.py:341
  61.8 6.9 %collective-permute-start.13 = (f32[2,12,512]{2,1,0:T(8,128)S(1)}, f32[2,12,512]{2,1,0:T(8,128)S(1)}, u32[]{:S(2)}, u32[]{:S(2)}) collective-permute-start(f32[2,12,512]{2,1,0:T(8,128)S(1)} %pad_maximum_fusion.2.refs_8_), channel_id=1, source_target_pairs={{0,2},{2,0},{4,6},{6,4},{8,10},{10,8},{12,14},{14,12},{16,18},{18,... | collective-permute-start | bytes 147464 | tf_op jit(solution)/shard_map/ppermute | solution.py:365
  78.4 30.8 %collective-permute-start.16 = (bf16[2,512,128]{2,1,0:T(8,128)(2,1)S(1)}, bf16[2,512,128]{2,1,0:T(8,128)(2,1)S(1)}, u32[]{:S(2)}, u32[]{:S(2)}) collective-permute-start(bf16[2,512,128]{2,1,0:T(8,128)(2,1)S(1)} %get-tuple-element.26), channel_id=1, source_target_pairs={{0,2},{2,0},{4,6},{6,4},{8,10},{10,8},{12,14},{14,12},{16,18},{18,... | collective-permute-start | bytes 786440 | tf_op jit(solution)/shard_map/ppermute | solution.py:376
  78.5 32.3 %collective-permute-start.17 = (bf16[2,512,128]{2,1,0:T(8,128)(2,1)S(1)}, bf16[2,512,128]{2,1,0:T(8,128)(2,1)S(1)}, u32[]{:S(2)}, u32[]{:S(2)}) collective-permute-start(bf16[2,512,128]{2,1,0:T(8,128)(2,1)S(1)} %get-tuple-element.27), channel_id=1, source_target_pairs={{0,4},{2,6},{4,0},{6,2},{8,12},{10,14},{12,8},{14,10},{16,20},{18,... | collective-permute-start | bytes 786440 | tf_op jit(solution)/shard_map/ppermute | solution.py:376
  78.6 40.4 %collective-permute-start.18 = (bf16[2,512,128]{2,1,0:T(8,128)(2,1)S(1)}, bf16[2,512,128]{2,1,0:T(8,128)(2,1)S(1)}, u32[]{:S(2)}, u32[]{:S(2)}) collective-permute-start(bf16[2,512,128]{2,1,0:T(8,128)(2,1)S(1)} %get-tuple-element.28), channel_id=1, source_target_pairs={{0,6},{2,4},{4,2},{6,0},{8,14},{10,12},{12,10},{14,8},{16,22},{18,... | collective-permute-start | bytes 786440 | tf_op jit(solution)/shard_map/ppermute | solution.py:376
  83.2 36.7 %collective-permute-start.20 = (bf16[2,512,128]{2,1,0:T(8,128)(2,1)S(1)}, bf16[2,512,128]{2,1,0:T(8,128)(2,1)S(1)}, u32[]{:S(2)}, u32[]{:S(2)}) collective-permute-start(bf16[2,512,128]{2,1,0:T(8,128)(2,1)S(1)} %get-tuple-element.33), channel_id=1, source_target_pairs={{0,2},{2,0},{4,6},{6,4},{8,10},{10,8},{12,14},{14,12},{16,18},{18,... | collective-permute-start | bytes 786440 | tf_op jit(solution)/shard_map/ppermute | solution.py:376
  83.2 16.8 %collective-permute-start.24 = (bf16[256,256]{1,0:T(8,128)(2,1)S(1)}, bf16[256,256]{1,0:T(8,128)(2,1)S(1)}, u32[]{:S(2)}, u32[]{:S(2)}) collective-permute-start(bf16[256,256]{1,0:T(8,128)(2,1)S(1)} %get-tuple-element.38), channel_id=1, source_target_pairs={{0,192},{2,194},{4,196},{6,198},{8,200},{10,202},{12,204},{14,206}... | collective-permute-start | bytes 393224 | tf_op jit(solution)/shard_map/ppermute | solution.py:378
  106.0 15.2 %collective-permute-start.21 = (bf16[2,512,128]{2,1,0:T(8,128)(2,1)S(1)}, bf16[2,512,128]{2,1,0:T(8,128)(2,1)S(1)}, u32[]{:S(2)}, u32[]{:S(2)}) collective-permute-start(bf16[2,512,128]{2,1,0:T(8,128)(2,1)S(1)} %get-tuple-element.34), channel_id=1, source_target_pairs={{0,4},{2,6},{4,0},{6,2},{8,12},{10,14},{12,8},{14,10},{16,20},{18,... | collective-permute-start | bytes 786440 | tf_op jit(solution)/shard_map/ppermute | solution.py:376
  109.2 12.0 %collective-permute-start.22 = (bf16[2,512,128]{2,1,0:T(8,128)(2,1)S(1)}, bf16[2,512,128]{2,1,0:T(8,128)(2,1)S(1)}, u32[]{:S(2)}, u32[]{:S(2)}) collective-permute-start(bf16[2,512,128]{2,1,0:T(8,128)(2,1)S(1)} %get-tuple-element.35), channel_id=1, source_target_pairs={{0,6},{2,4},{4,2},{6,0},{8,14},{10,12},{12,10},{14,8},{16,22},{18,... | collective-permute-start | bytes 786440 | tf_op jit(solution)/shard_map/ppermute | solution.py:376
  110.8 15.5 %collective-permute-start.27 = (bf16[512,256]{1,0:T(8,128)(2,1)S(1)}, bf16[512,256]{1,0:T(8,128)(2,1)S(1)}, u32[]{:S(2)}, u32[]{:S(2)}) collective-permute-start(bf16[512,256]{1,0:T(8,128)(2,1)S(1)} %pad_maximum_fusion.1), channel_id=1, source_target_pairs={{0,192},{2,194},{4,196},{6,198},{8,200},{10,202},{12,204},{14,206}... | collective-permute-start | bytes 786440 | tf_op jit(solution)/shard_map/ppermute | solution.py:382
  119.0 9.0 %collective-permute-start.25 = (bf16[512,256]{1,0:T(8,128)(2,1)S(1)}, bf16[512,256]{1,0:T(8,128)(2,1)S(1)}, u32[]{:S(2)}, u32[]{:S(2)}) collective-permute-start(bf16[512,256]{1,0:T(8,128)(2,1)S(1)} %pad_maximum_fusion), channel_id=1, source_target_pairs={{0,64},{2,66},{4,68},{6,70},{8,72},{10,74},{12,76},{14,78},{16,80}... | collective-permute-start | bytes 786440 | tf_op jit(solution)/shard_map/ppermute | solution.py:381
  119.9 14.4 %collective-permute-start.19 = (bf16[512,128]{1,0:T(8,128)(2,1)S(1)}, bf16[512,128]{1,0:T(8,128)(2,1)S(1)}, u32[]{:S(2)}, u32[]{:S(2)}) collective-permute-start(bf16[512,128]{1,0:T(8,128)(2,1)S(1)} %get-tuple-element.46), channel_id=1, source_target_pairs={{0,32},{2,34},{4,36},{6,38},{8,40},{10,42},{12,44},{14,46},{16,48}... | collective-permute-start | bytes 393224 | tf_op jit(solution)/shard_map/ppermute | solution.py:380
  122.0 14.7 %collective-permute-start.23 = (bf16[512,128]{1,0:T(8,128)(2,1)S(1)}, bf16[512,128]{1,0:T(8,128)(2,1)S(1)}, u32[]{:S(2)}, u32[]{:S(2)}) collective-permute-start(bf16[512,128]{1,0:T(8,128)(2,1)S(1)} %get-tuple-element.44), channel_id=1, source_target_pairs={{0,32},{2,34},{4,36},{6,38},{8,40},{10,42},{12,44},{14,46},{16,48}... | collective-permute-start | bytes 393224 | tf_op jit(solution)/shard_map/ppermute | solution.py:386
  128.2 10.8 %collective-permute-start.28 = (bf16[128,256]{1,0:T(8,128)(2,1)S(1)}, bf16[128,256]{1,0:T(8,128)(2,1)S(1)}, u32[]{:S(2)}, u32[]{:S(2)}) collective-permute-start(bf16[128,256]{1,0:T(8,128)(2,1)S(1)} %get-tuple-element.41), channel_id=1, source_target_pairs={{0,16},{2,18},{4,20},{6,22},{8,24},{10,26},{12,28},{14,30},{16,0},... | collective-permute-start | bytes 196616 | tf_op jit(solution)/shard_map/ppermute | solution.py:385
  128.8 10.2 %collective-permute-start.30 = (bf16[128,256]{1,0:T(8,128)(2,1)S(1)}, bf16[128,256]{1,0:T(8,128)(2,1)S(1)}, u32[]{:S(2)}, u32[]{:S(2)}) collective-permute-start(bf16[128,256]{1,0:T(8,128)(2,1)S(1)} %get-tuple-element.42), channel_id=1, source_target_pairs={{0,24},{2,26},{4,28},{6,30},{8,16},{10,18},{12,20},{14,22},{16,8},... | collective-permute-start | bytes 196616 | tf_op jit(solution)/shard_map/ppermute | solution.py:385
  (13 other events, 125.3 us)

commit v5 on v4

--- a/solution.py
+++ b/solution.py
@@ -100,7 +100,7 @@
 
 def forward(group, width, pieces, sc, *refs):
     rows, keys, refs = refs[:6], refs[6 : 6 + pieces], refs[6 + pieces :]
-    acc, stat, q_s, do_s, k_s, v_s, t_s, high, total, mixed = refs
+    values, stat, acc, q_s, do_s, k_s, v_s, t_s, high, total, mixed = refs
     unit = LOG2E / math.sqrt(width)
     heads = range(group)
     fill(rows, keys, q_s, do_s, k_s, v_s, t_s, group, width, 1)
@@ -148,6 +148,7 @@
     lax.fori_loop(0, 4 * pieces, step, 0)
     for t in range(TILES):
         for h in heads:
+            values[t, h] = (acc[t, h] * (1.0 / jnp.maximum(total[t, h], 1e-30))).astype(BF16)
             stat[t, h : h + 1, :] = high[t, h]
             stat[t, group + h : group + h + 1, :] = total[t, h]
             stat[t, 2 * group + h : 2 * group + h + 1, :] = mixed[t, h]
@@ -180,12 +181,12 @@
                 total = sum(w * p[group : 2 * group] for w, p in zip(weights, parts))
                 product = sum(w * p[2 * group :] for w, p in zip(weights, parts))
                 low, small = top * unit + jnp.log2(total), product / total
-                part = jnp.exp2(own[t, :group, at] * unit - low)
+                part = own[t, group : 2 * group, at] * jnp.exp2(own[t, :group, at] * unit - low)
                 for h in heads:
                     lse[t, h, :, at] = low[h : h + 1]
                     delta[t, h, :, at] = small[h : h + 1]
                     mixed[u][t, h * width : (h + 1) * width, :] = (
-                        values[t, h, :, at] * part[h : h + 1]
+                        values[t, h, :, at].astype(F32) * part[h : h + 1]
                     ).astype(BF16)
     else:
         acc[...] = acc_in[...]
@@ -279,35 +280,41 @@
     acc, line, _ = state_shapes(group, width)
     return pl.pallas_call(
         functools.partial(forward, group, width, pieces),
-        out_shape=[acc, jax.ShapeDtypeStruct((TILES, 3 * group, ROWS), F32)],
+        out_shape=[
+            jax.ShapeDtypeStruct(acc.shape, BF16),
+            jax.ShapeDtypeStruct((TILES, 3 * group, ROWS), F32),
+        ],
         in_specs=[SMEM] + [VMEM] * (6 + pieces),
         out_specs=[VMEM] * 2,
-        scratch_shapes=scratch(group, width, pieces) + [pltpu.VMEM(line.shape, F32)] * 3,
+        scratch_shapes=[pltpu.VMEM(acc.shape, F32)]
+        + scratch(group, width, pieces)
+        + [pltpu.VMEM(line.shape, F32)] * 3,
         compiler_params=PARAMS,
         cost_estimate=cost(group, width, 3, pieces),
         name="forward",
     )(sc, *rows, *keys)
 
 
-def run_backward(group, width, begins, sc, rows, keys, *more):
+def run_backward(group, width, begins, ends, sc, rows, keys, *more):
     pieces = len(keys)
     carried = state_shapes(group, width)
     piece = jax.ShapeDtypeStruct((TILES, group * width, CHUNK), BF16)
-    shapes = [jax.ShapeDtypeStruct((2 * pieces, PAIR, 2 * width), BF16)] + [piece] * SLOTS
+    shapes = [jax.ShapeDtypeStruct((2 * pieces, PAIR, 2 * width), BF16)]
+    shapes = shapes + [piece] * (SLOTS * (begins + ends))
     spaces = scratch(group, width, pieces) + [pltpu.VMEM((PAIR, 2 * width), F32)]
-    if begins:
+    if not ends:
         shapes = shapes + carried
     else:
         spaces = [pltpu.VMEM(s.shape, F32) for s in carried] + spaces
     return pl.pallas_call(
-        functools.partial(backward, group, width, pieces, begins, not begins),
+        functools.partial(backward, group, width, pieces, begins, ends),
         out_shape=shapes,
         in_specs=[SMEM] + [VMEM] * (6 + pieces + len(more)),
         out_specs=[VMEM] * len(shapes),
         scratch_shapes=spaces,
         compiler_params=PARAMS,
         cost_estimate=cost(group, width, 5, pieces),
-        name="backward_begin" if begins else "backward_end",
+        name="backward_begin" if begins else "backward_end" if ends else "backward_middle",
     )(sc, *rows, *keys, *more)
 
 
@@ -364,23 +371,25 @@
     )
     stats = [merged] + [send(merged, perm=Y[s]) for s in range(1, SLOTS)]
 
-    def shifted(skip):
-        return jnp.concatenate([sc[: 4 + DOCS], sc[4 + DOCS + skip :]])
-
-    late = run_backward(group, width, True, shifted(2), rows, keys[2:], *stats, stat, values)
-    far, mixed, carried = late[0], late[1 : 1 + SLOTS], late[1 + SLOTS :]
-    end = run_backward(group, width, False, sc, rows, keys[:2], *carried)
-    close, dq = end[0], end[1:]
-
     def over_y(parts):
         return add(parts[0], *[send(parts[s], perm=Y[s]) for s in range(1, SLOTS)])
 
-    one, two = send(far[2], perm=NEAR), send(far[3], perm=REST)
+    def part_of(begin, end):
+        return jnp.concatenate([sc[: 4 + DOCS], sc[4 + DOCS + begin : 4 + DOCS + end]])
+
+    back = functools.partial(run_backward, group, width)
+    out = back(True, False, part_of(3, 4), rows, keys[3:], *stats, stat, values)
+    far, mixed, carried = out[0], out[1 : 1 + SLOTS], out[1 + SLOTS :]
+    one, two = send(far[0], perm=NEAR), send(far[1], perm=REST)
     mixed = over_y(mixed)
+    near_by, *carried = back(False, False, part_of(1, 3), rows, keys[1:3], *carried)
+    ga = jnp.concatenate([near_by[0], add(near_by[1], two)], axis=0)
+    gb = jnp.concatenate([add(near_by[2], one), near_by[3]], axis=0)
+    ga, gb, mixed, carried = lax.optimization_barrier((ga, gb, mixed, carried))
+    ga, gb = send(ga, perm=NEAR), send(gb, perm=REST)
     mixed = [mixed[0], send(mixed[1], perm=NEXT)]
-    ga = send(jnp.concatenate([close[2], add(close[3], two)], axis=0), perm=NEAR)
-    gb = send(jnp.concatenate([add(far[0], one), far[1]], axis=0), perm=REST)
-    grad = add(close[:2].reshape(2 * PAIR, 2 * width), ga, gb).reshape(4, CHUNK, 2 * width)
+    close, *dq = back(False, True, part_of(0, 1), rows, keys[:1], *carried)
+    grad = add(close.reshape(2 * PAIR, 2 * width), ga, gb).reshape(4, CHUNK, 2 * width)
     dq = over_y(dq)
     grad = add(grad[0], *[send(grad[n], perm=X[n]) for n in range(1, 4)])
     dq = [dq[0], send(dq[1], perm=NEXT)]

time: 142 us -> 131 us (0.923); the launches traced: 140 us -> 131 us
  waiting for transfers between devices: 39.3 us -> 27.9 us
  Pallas kernels: 19.4 us -> 26.2 us
  starting transfers between devices: 66.2 us -> 60.6 us
  other arithmetic: 0.93 us -> 2.72 us
    ppermute x4, waiting for transfers between devices: 14.8 us -> 0.01 us  [the longest x2 0.01 us: local(): one, two = (send(far[0], perm=NEAR), send(far[1], perm=REST))]
    ppermute x4, starting transfers between devices: 21.5 us -> 12.8 us  [the longest x2 7.04 us: local(): ga, gb = (send(ga, perm=NEAR), send(gb, perm=REST))]
    ppermute x3, waiting for transfers between devices: 0.01 us -> 4.33 us  [local(): grad = add(grad[0], *[send(grad[n], perm=X[n]) for n in range(1, 4)])]
    pallas_call x2 -> x3, Pallas kernels: 8.04 us -> 12.3 us  [run_backward(): pl.pallas_call(functools.partial(backward, group, width, pieces, begins,...]
    ppermute x1, starting transfers between devices: 1.34 us -> 5.36 us  [local(): mixed = [mixed[0], send(mixed[1], perm=NEXT)]]
    ppermute x3, waiting for transfers between devices: 2.78 us -> 0.01 us  [local(): stats = [merged] + [send(merged, perm=Y[s]) for s in range(1, SLOTS)]]
    pallas_call x1, Pallas kernels: 6.09 us -> 8.59 us  [run_forward(): pl.pallas_call(functools.partial(forward, group, width, pieces), out_shap...]
    unnamed x17, local copies, waits for them, and re-layouts: 7.73 us -> 5.44 us
  transfers between devices with their start and end apart: 31 -> 31, of which waited for: 13 -> 9; matrix products, arithmetic and copies ran while one was open for 6% -> 9% of each run, Pallas kernels for 2% -> 8%
where the time goes in v5:
time: 131 us
  starting transfers between devices  60.6 us (46%)
  waiting for transfers between devices  27.9 us (21%)
  Pallas kernels  26.2 us (20%)
  local copies, waits for them, and re-layouts  12.7 us (10%)
  other arithmetic  2.72 us (2%)
    pallas_call x3, Pallas kernels, run_backward(): pl.pallas_call(functools.partial(backward, group, width, pieces, begins,...  12.3 us
    ppermute x6, starting transfers between devices, over_y(): return add(parts[0], *[send(parts[s], perm=Y[s]) for s in range(1, SLOTS)])  9.47 us
    ppermute x2, waiting for transfers between devices, local(): a, b = (send(own, perm=NEAR), send(own, perm=REST))  8.91 us
    pallas_call x1, Pallas kernels, run_forward(): pl.pallas_call(functools.partial(forward, group, width, pieces), out_shap...  8.59 us
    ppermute x2, starting transfers between devices, local(): ga, gb = (send(ga, perm=NEAR), send(gb, perm=REST))  7.04 us
    ppermute x2, starting transfers between devices, local(): a, b = (send(own, perm=NEAR), send(own, perm=REST))  6.94 us
    ppermute x2, starting transfers between devices, local(): one, two = (send(far[0], perm=NEAR), send(far[1], perm=REST))  5.77 us
    unnamed x17, local copies, waits for them, and re-layouts  5.44 us
  transfers between devices with their start and end apart: 31, of which 9 were waited for; matrix products, arithmetic and copies ran while one was open for 9% of the time, Pallas kernels for 8%

profile of v5, /device:TPU:32, one launch (start us, length us, event | category | flops | bytes accessed | tf_op | source)
XLA Modules:
  0.0 131.1 jit_solution(11924084365290792118)
XLA Ops:
  3.9 2.7 %collective-permute-start.6 = (bf16[128,256]{1,0:T(8,128)(2,1)}, bf16[128,256]{1,0:T(8,128)(2,1)S(1)}, u32[]{:S(2)}, u32[]{:S(2)}) collective-permute-start(bf16[128,256]{1,0:T(8,128)(2,1)} %get-tuple-element.32), channel_id=1, source_target_pairs={{0,8},{2,10},{4,12},{6,14},{8,0},{10,2},{12,4},{14,6},{16,24},{18,... | collective-permute-start | bytes 196616 | tf_op jit(solution)/shard_map/ppermute | solution.py:341
  7.1 1.8 %collective-permute-start = (bf16[128,1024]{1,0:T(8,128)(2,1)}, bf16[128,1024]{1,0:T(8,128)(2,1)S(1)}, u32[]{:S(2)}, u32[]{:S(2)}) collective-permute-start(bf16[128,1024]{1,0:T(8,128)(2,1)} %get-tuple-element.31.refs_0_), channel_id=1, source_target_pairs={{0,32},{2,34},{4,36},{6,38},{8,40},{10,42},{12,44},{14,46},{16,48}... | collective-permute-start | bytes 786440 | tf_op jit(solution)/shard_map/ppermute | solution.py:343
  11.5 3.0 %collective-permute-done.refs_1_ = bf16[128,1024]{1,0:T(8,128)(2,1)S(1)} collective-permute-done((bf16[128,1024]{1,0:T(8,128)(2,1)}, bf16[128,1024]{1,0:T(8,128)(2,1)S(1)}, u32[]{:S(2)}, u32[]{:S(2)}) %collective-permute-start) | collective-permute-done | bytes 262176 | tf_op jit(solution)/shard_map/ppermute | solution.py:343
  15.3 3.0 %collective-permute-start.2 = (bf16[256,1024]{1,0:T(8,128)(2,1)}, bf16[256,1024]{1,0:T(8,128)(2,1)S(1)}, u32[]{:S(2)}, u32[]{:S(2)}) collective-permute-start(bf16[256,1024]{1,0:T(8,128)(2,1)} %constant_dynamic-update-slice_fusion), channel_id=1, source_target_pairs={{0,6},{2,4},{4,2},{6,0},{8,14},{10,12},{12,10},{14,8},{16,22},{18,... | collective-permute-start | bytes 1572872 | tf_op jit(solution)/shard_map/ppermute | solution.py:346
  18.5 5.5 %collective-permute-start.9 = (bf16[512,256]{1,0:T(8,128)(2,1)S(1)}, bf16[512,256]{1,0:T(8,128)(2,1)S(1)}, u32[]{:S(2)}, u32[]{:S(2)}) collective-permute-start(bf16[512,256]{1,0:T(8,128)(2,1)S(1)} %constant_dynamic-update-slice_fusion.2.refs_6_), channel_id=1, source_target_pairs={{0,192},{2,194},{4,196},{6,198},{8,200},{10,202},{12,204},{14,206}... | collective-permute-start | bytes 786440 | tf_op jit(solution)/shard_map/ppermute | solution.py:344
  25.4 8.3 %collective-permute-done.9.refs_8_.refs_7_ = bf16[512,256]{1,0:T(8,128)(2,1)S(1)} collective-permute-done((bf16[512,256]{1,0:T(8,128)(2,1)S(1)}, bf16[512,256]{1,0:T(8,128)(2,1)S(1)}, u32[]{:S(2)}, u32[]{:S(2)}) %collective-permute-start.9) | collective-permute-done | bytes 262176 | tf_op jit(solution)/shard_map/ppermute | solution.py:344
  36.1 4.0 %collective-permute-start.11 = (bf16[256,256]{1,0:T(8,128)(2,1)}, bf16[256,256]{1,0:T(8,128)(2,1)S(1)}, u32[]{:S(2)}, u32[]{:S(2)}) collective-permute-start(bf16[256,256]{1,0:T(8,128)(2,1)} %slice.141), channel_id=1, source_target_pairs={{0,192},{2,194},{4,196},{6,198},{8,200},{10,202},{12,204},{14,206}... | collective-permute-start | bytes 393224 | tf_op jit(solution)/shard_map/ppermute | solution.py:347
  45.3 2.2 %collective-permute-done.3.refs_4_ = bf16[128,1024]{1,0:T(8,128)(2,1)S(1)} collective-permute-done((bf16[128,1024]{1,0:T(8,128)(2,1)}, bf16[128,1024]{1,0:T(8,128)(2,1)S(1)}, u32[]{:S(2)}, u32[]{:S(2)}) %collective-permute-start.3) | collective-permute-done | bytes 262176 | tf_op jit(solution)/shard_map/ppermute | solution.py:348
  47.5 3.5 %collective-permute-done.4.refs_5_ = bf16[128,1024]{1,0:T(8,128)(2,1)S(1)} collective-permute-done((bf16[128,1024]{1,0:T(8,128)(2,1)}, bf16[128,1024]{1,0:T(8,128)(2,1)S(1)}, u32[]{:S(2)}, u32[]{:S(2)}) %collective-permute-start.4) | collective-permute-done | bytes 262176 | tf_op jit(solution)/shard_map/ppermute | solution.py:348
  51.0 8.6 %forward.1 = (bf16[2,4,128,512]{3,2,1,0:T(8,128)(2,1)S(1)}, f32[2,12,512]{2,1,0:T(8,128)S(1)}) custom-call(s32[16]{0:T(128)S(1)} %concatenate.39.sc, bf16[128,1024]{1,0:T(8,128)(2,1)S(1)} %copy-done, bf16[128,1024]{1,0:T(8,128)(2,1)S(1)} %collective-permute-done.refs_1_, bf16[256,1024]{1,0:T(8,128)(2,1)S(1)} %collective-permute-done.1.refs_2_, ...), custom_call_target="tpu_custom_call" | custom-call | flops 12884901888 | bytes 8388608 | tf_op jit(solution)/shard_map/forward/pallas_call | solution.py:281
  60.6 4.3 %collective-permute-done.12 = f32[2,12,512]{2,1,0:T(8,128)S(1)} collective-permute-done((f32[2,12,512]{2,1,0:T(8,128)S(1)}, f32[2,12,512]{2,1,0:T(8,128)S(1)}, u32[]{:S(2)}, u32[]{:S(2)}) %collective-permute-start.12) | collective-permute-done | bytes 49184 | tf_op jit(solution)/shard_map/ppermute | solution.py:360
  65.4 4.4 %collective-permute-start.15 = (f32[2,12,512]{2,1,0:T(8,128)S(1)}, f32[2,12,512]{2,1,0:T(8,128)S(1)}, u32[]{:S(2)}, u32[]{:S(2)}) collective-permute-start(f32[2,12,512]{2,1,0:T(8,128)S(1)} %pad_maximum_fusion.2.refs_7_), channel_id=1, source_target_pairs={{0,6},{2,4},{4,2},{6,0},{8,14},{10,12},{12,10},{14,8},{16,22},{18,... | collective-permute-start | bytes 147464 | tf_op jit(solution)/shard_map/ppermute | solution.py:372
  73.3 2.9 %backward_begin.1 = (bf16[2,256,256]{2,1,0:T(8,128)(2,1)S(1)}, bf16[2,512,128]{2,1,0:T(8,128)(2,1)S(1)}, bf16[2,512,128]{2,1,0:T(8,128)(2,1)S(1)}, bf16[2,512,12...) custom-call(s32[13]{0:T(128)S(1)} %concatenate.37.sc, ...), custom_call_target="tpu_custom_call" | custom-call | flops 5368709120 | bytes 8388608 | tf_op jit(solution)/shard_map/backward_begin/pallas_call | solution.py:309
  76.4 3.2 %collective-permute-start.19 = (bf16[2,512,128]{2,1,0:T(8,128)(2,1)S(1)}, bf16[2,512,128]{2,1,0:T(8,128)(2,1)S(1)}, u32[]{:S(2)}, u32[]{:S(2)}) collective-permute-start(bf16[2,512,128]{2,1,0:T(8,128)(2,1)S(1)} %get-tuple-element.42), channel_id=1, source_target_pairs={{0,4},{2,6},{4,0},{6,2},{8,12},{10,14},{12,8},{14,10},{16,20},{18,... | collective-permute-start | bytes 786440 | tf_op jit(solution)/shard_map/ppermute | solution.py:375
  81.2 5.7 %collective-permute-start.17 = (bf16[256,256]{1,0:T(8,128)(2,1)S(1)}, bf16[256,256]{1,0:T(8,128)(2,1)S(1)}, u32[]{:S(2)}, u32[]{:S(2)}) collective-permute-start(bf16[256,256]{1,0:T(8,128)(2,1)S(1)} %get-tuple-element.69), channel_id=1, source_target_pairs={{0,64},{2,66},{4,68},{6,70},{8,72},{10,74},{12,76},{14,78},{16,80}... | collective-permute-start | bytes 393224 | tf_op jit(solution)/shard_map/ppermute | solution.py:383
  86.8 4.4 %backward_middle.1 = (bf16[4,256,256]{2,1,0:T(8,128)(2,1)S(1)}, f32[2,4,128,512]{3,2,1,0:T(8,128)S(1)}, f32[2,4,1,512]{3,2,1,0:T(1,128)S(1)}, f32[2,4,1,512]{3,2,1,0:T(1,128)S(1)}) custom-call(s32[14]{0:T(128)S(1)} %concatenate.34.sc, bf16[128,1024]{1,0:T(8,128)(2,1)S(1)} %copy-done, bf16[128,1024]{1,0:T(8,128)(2,1)S(1)} %collective-permute-done.refs_1_, ...), custom_call_target="tpu_custom_call" | custom-call | flops 10737418240 | bytes 8388608 | tf_op jit(solution)/shard_map/backward_middle/pallas_call | solution.py:309
  92.4 2.9 %collective-permute-start.26 = (bf16[512,256]{1,0:T(8,128)(2,1)}, bf16[512,256]{1,0:T(8,128)(2,1)}, u32[]{:S(2)}, u32[]{:S(2)}) collective-permute-start(bf16[512,256]{1,0:T(8,128)(2,1)} %get-tuple-element.56), channel_id=1, source_target_pairs={{0,64},{2,66},{4,68},{6,70},{8,72},{10,74},{12,76},{14,78},{16,80}... | collective-permute-start | bytes 786440 | tf_op jit(solution)/shard_map/ppermute | solution.py:389
  95.3 4.1 %collective-permute-start.27 = (bf16[512,256]{1,0:T(8,128)(2,1)}, bf16[512,256]{1,0:T(8,128)(2,1)}, u32[]{:S(2)}, u32[]{:S(2)}) collective-permute-start(bf16[512,256]{1,0:T(8,128)(2,1)} %get-tuple-element.57), channel_id=1, source_target_pairs={{0,192},{2,194},{4,196},{6,198},{8,200},{10,202},{12,204},{14,206}... | collective-permute-start | bytes 786440 | tf_op jit(solution)/shard_map/ppermute | solution.py:389
  100.1 5.4 %collective-permute-start.21 = (bf16[512,128]{1,0:T(8,128)(2,1)S(1)}, bf16[512,128]{1,0:T(8,128)(2,1)S(1)}, u32[]{:S(2)}, u32[]{:S(2)}) collective-permute-start(bf16[512,128]{1,0:T(8,128)(2,1)S(1)} %get-tuple-element.67), channel_id=1, source_target_pairs={{0,32},{2,34},{4,36},{6,38},{8,40},{10,42},{12,44},{14,46},{16,48}... | collective-permute-start | bytes 393224 | tf_op jit(solution)/shard_map/ppermute | solution.py:390
  105.4 5.0 %backward_end.1 = (bf16[2,256,256]{2,1,0:T(8,128)(2,1)S(1)}, bf16[2,512,128]{2,1,0:T(8,128)(2,1)S(1)}, bf16[2,512,128]{2,1,0:T(8,128)(2,1)}, bf16[2,512,128]{2,1,0:T(8,128)(2,1)S(1)}, bf16[2,512,128]{2,1,0:T(8,128)(2,1)S(1)}) custom-call(s32[13]{0:T(128)S(1)} %concatenate.43.sc, bf16[128,1024]{1,0:T(8,128)(2,1)S(1)} %copy-done, ...), custom_call_target="tpu_custom_call" | custom-call | flops 5368709120 | bytes 8388608 | tf_op jit(solution)/shard_map/backward_end/pallas_call | solution.py:309
  110.5 4.7 %collective-permute-start.24 = (bf16[2,512,128]{2,1,0:T(8,128)(2,1)S(1)}, bf16[2,512,128]{2,1,0:T(8,128)(2,1)S(1)}, u32[]{:S(2)}, u32[]{:S(2)}) collective-permute-start(bf16[2,512,128]{2,1,0:T(8,128)(2,1)S(1)} %get-tuple-element.54), channel_id=1, source_target_pairs={{0,6},{2,4},{4,2},{6,0},{8,14},{10,12},{12,10},{14,8},{16,22},{18,... | collective-permute-start | bytes 786440 | tf_op jit(solution)/shard_map/ppermute | solution.py:375
  118.3 4.2 %collective-permute-start.29 = (bf16[128,256]{1,0:T(8,128)(2,1)S(1)}, bf16[128,256]{1,0:T(8,128)(2,1)S(1)}, u32[]{:S(2)}, u32[]{:S(2)}) collective-permute-start(bf16[128,256]{1,0:T(8,128)(2,1)S(1)} %get-tuple-element.64), channel_id=1, source_target_pairs={{0,8},{2,10},{4,12},{6,14},{8,0},{10,2},{12,4},{14,6},{16,24},{18,... | collective-permute-start | bytes 196616 | tf_op jit(solution)/shard_map/ppermute | solution.py:394
  123.7 1.8 %collective-permute-done.29 = bf16[128,256]{1,0:T(8,128)(2,1)S(1)} collective-permute-done((bf16[128,256]{1,0:T(8,128)(2,1)S(1)}, bf16[128,256]{1,0:T(8,128)(2,1)S(1)}, u32[]{:S(2)}, u32[]{:S(2)}) %collective-permute-start.29) | collective-permute-done | bytes 65568 | tf_op jit(solution)/shard_map/ppermute | solution.py:394
  125.5 2.5 %collective-permute-done.30 = bf16[128,256]{1,0:T(8,128)(2,1)S(1)} collective-permute-done((bf16[128,256]{1,0:T(8,128)(2,1)S(1)}, bf16[128,256]{1,0:T(8,128)(2,1)S(1)}, u32[]{:S(2)}, u32[]{:S(2)}) %collective-permute-start.30) | collective-permute-done | bytes 65568 | tf_op jit(solution)/shard_map/ppermute | solution.py:394
  (92 shorter events, 32.0 us)
Async XLA Ops:
  2.4 9.1 %collective-permute-start.5 = (bf16[128,256]{1,0:T(8,128)(2,1)}, bf16[128,256]{1,0:T(8,128)(2,1)S(1)}, u32[]{:S(2)}, u32[]{:S(2)}) collective-permute-start(bf16[128,256]{1,0:T(8,128)(2,1)} %get-tuple-element.32), channel_id=1, source_target_pairs={{0,16},{2,18},{4,20},{6,22},{8,24},{10,26},{12,28},{14,30},{16,0},... | collective-permute-start | bytes 196616 | tf_op jit(solution)/shard_map/ppermute | solution.py:341
  3.9 14.5 %collective-permute-start.6 = (bf16[128,256]{1,0:T(8,128)(2,1)}, bf16[128,256]{1,0:T(8,128)(2,1)S(1)}, u32[]{:S(2)}, u32[]{:S(2)}) collective-permute-start(bf16[128,256]{1,0:T(8,128)(2,1)} %get-tuple-element.32), channel_id=1, source_target_pairs={{0,8},{2,10},{4,12},{6,14},{8,0},{10,2},{12,4},{14,6},{16,24},{18,... | collective-permute-start | bytes 196616 | tf_op jit(solution)/shard_map/ppermute | solution.py:341
  6.6 11.8 %collective-permute-start.7 = (bf16[128,256]{1,0:T(8,128)(2,1)}, bf16[128,256]{1,0:T(8,128)(2,1)S(1)}, u32[]{:S(2)}, u32[]{:S(2)}) collective-permute-start(bf16[128,256]{1,0:T(8,128)(2,1)} %get-tuple-element.32), channel_id=1, source_target_pairs={{0,24},{2,26},{4,28},{6,30},{8,16},{10,18},{12,20},{14,22},{16,8},... | collective-permute-start | bytes 196616 | tf_op jit(solution)/shard_map/ppermute | solution.py:341
  7.1 7.4 %collective-permute-start = (bf16[128,1024]{1,0:T(8,128)(2,1)}, bf16[128,1024]{1,0:T(8,128)(2,1)S(1)}, u32[]{:S(2)}, u32[]{:S(2)}) collective-permute-start(bf16[128,1024]{1,0:T(8,128)(2,1)} %get-tuple-element.31.refs_0_), channel_id=1, source_target_pairs={{0,32},{2,34},{4,36},{6,38},{8,40},{10,42},{12,44},{14,46},{16,48}... | collective-permute-start | bytes 786440 | tf_op jit(solution)/shard_map/ppermute | solution.py:343
  15.3 24.8 %collective-permute-start.2 = (bf16[256,1024]{1,0:T(8,128)(2,1)}, bf16[256,1024]{1,0:T(8,128)(2,1)S(1)}, u32[]{:S(2)}, u32[]{:S(2)}) collective-permute-start(bf16[256,1024]{1,0:T(8,128)(2,1)} %constant_dynamic-update-slice_fusion), channel_id=1, source_target_pairs={{0,6},{2,4},{4,2},{6,0},{8,14},{10,12},{12,10},{14,8},{16,22},{18,... | collective-permute-start | bytes 1572872 | tf_op jit(solution)/shard_map/ppermute | solution.py:346
  18.3 24.2 %collective-permute-start.1 = (bf16[256,1024]{1,0:T(8,128)(2,1)}, bf16[256,1024]{1,0:T(8,128)(2,1)S(1)}, u32[]{:S(2)}, u32[]{:S(2)}) collective-permute-start(bf16[256,1024]{1,0:T(8,128)(2,1)} %constant_dynamic-update-slice_fusion), channel_id=1, source_target_pairs={{0,2},{2,0},{4,6},{6,4},{8,10},{10,8},{12,14},{14,12},{16,18},{18,... | collective-permute-start | bytes 1572872 | tf_op jit(solution)/shard_map/ppermute | solution.py:346
  18.5 15.2 %collective-permute-start.9 = (bf16[512,256]{1,0:T(8,128)(2,1)S(1)}, bf16[512,256]{1,0:T(8,128)(2,1)S(1)}, u32[]{:S(2)}, u32[]{:S(2)}) collective-permute-start(bf16[512,256]{1,0:T(8,128)(2,1)S(1)} %constant_dynamic-update-slice_fusion.2.refs_6_), channel_id=1, source_target_pairs={{0,192},{2,194},{4,196},{6,198},{8,200},{10,202},{12,204},{14,206}... | collective-permute-start | bytes 786440 | tf_op jit(solution)/shard_map/ppermute | solution.py:344
  23.9 11.5 %collective-permute-start.8 = (bf16[512,256]{1,0:T(8,128)(2,1)S(1)}, bf16[512,256]{1,0:T(8,128)(2,1)S(1)}, u32[]{:S(2)}, u32[]{:S(2)}) collective-permute-start(bf16[512,256]{1,0:T(8,128)(2,1)S(1)} %constant_dynamic-update-slice_fusion.2.refs_6_), channel_id=1, source_target_pairs={{0,64},{2,66},{4,68},{6,70},{8,72},{10,74},{12,76},{14,78},{16,80}... | collective-permute-start | bytes 786440 | tf_op jit(solution)/shard_map/ppermute | solution.py:344
  33.7 10.0 %collective-permute-start.10 = (bf16[256,256]{1,0:T(8,128)(2,1)S(1)}, bf16[256,256]{1,0:T(8,128)(2,1)S(1)}, u32[]{:S(2)}, u32[]{:S(2)}) collective-permute-start(bf16[256,256]{1,0:T(8,128)(2,1)S(1)} %slice.140), channel_id=1, source_target_pairs={{0,64},{2,66},{4,68},{6,70},{8,72},{10,74},{12,76},{14,78},{16,80}... | collective-permute-start | bytes 393224 | tf_op jit(solution)/shard_map/ppermute | solution.py:347
  36.1 9.2 %collective-permute-start.11 = (bf16[256,256]{1,0:T(8,128)(2,1)}, bf16[256,256]{1,0:T(8,128)(2,1)S(1)}, u32[]{:S(2)}, u32[]{:S(2)}) collective-permute-start(bf16[256,256]{1,0:T(8,128)(2,1)} %slice.141), channel_id=1, source_target_pairs={{0,192},{2,194},{4,196},{6,198},{8,200},{10,202},{12,204},{14,206}... | collective-permute-start | bytes 393224 | tf_op jit(solution)/shard_map/ppermute | solution.py:347
  43.2 7.8 %collective-permute-start.4 = (bf16[128,1024]{1,0:T(8,128)(2,1)}, bf16[128,1024]{1,0:T(8,128)(2,1)S(1)}, u32[]{:S(2)}, u32[]{:S(2)}) collective-permute-start(bf16[128,1024]{1,0:T(8,128)(2,1)} %slice.139), channel_id=1, source_target_pairs={{0,6},{2,4},{4,2},{6,0},{8,14},{10,12},{12,10},{14,8},{16,22},{18,... | collective-permute-start | bytes 786440 | tf_op jit(solution)/shard_map/ppermute | solution.py:348
  65.0 7.1 %collective-permute-start.13 = (f32[2,12,512]{2,1,0:T(8,128)S(1)}, f32[2,12,512]{2,1,0:T(8,128)S(1)}, u32[]{:S(2)}, u32[]{:S(2)}) collective-permute-start(f32[2,12,512]{2,1,0:T(8,128)S(1)} %pad_maximum_fusion.2.refs_7_), channel_id=1, source_target_pairs={{0,2},{2,0},{4,6},{6,4},{8,10},{10,8},{12,14},{14,12},{16,18},{18,... | collective-permute-start | bytes 147464 | tf_op jit(solution)/shard_map/ppermute | solution.py:372
  76.3 15.9 %collective-permute-start.18 = (bf16[2,512,128]{2,1,0:T(8,128)(2,1)S(1)}, bf16[2,512,128]{2,1,0:T(8,128)(2,1)S(1)}, u32[]{:S(2)}, u32[]{:S(2)}) collective-permute-start(bf16[2,512,128]{2,1,0:T(8,128)(2,1)S(1)} %get-tuple-element.41), channel_id=1, source_target_pairs={{0,2},{2,0},{4,6},{6,4},{8,10},{10,8},{12,14},{14,12},{16,18},{18,... | collective-permute-start | bytes 786440 | tf_op jit(solution)/shard_map/ppermute | solution.py:375
  76.4 15.9 %collective-permute-start.19 = (bf16[2,512,128]{2,1,0:T(8,128)(2,1)S(1)}, bf16[2,512,128]{2,1,0:T(8,128)(2,1)S(1)}, u32[]{:S(2)}, u32[]{:S(2)}) collective-permute-start(bf16[2,512,128]{2,1,0:T(8,128)(2,1)S(1)} %get-tuple-element.42), channel_id=1, source_target_pairs={{0,4},{2,6},{4,0},{6,2},{8,12},{10,14},{12,8},{14,10},{16,20},{18,... | collective-permute-start | bytes 786440 | tf_op jit(solution)/shard_map/ppermute | solution.py:375
  79.5 12.7 %collective-permute-start.20 = (bf16[2,512,128]{2,1,0:T(8,128)(2,1)S(1)}, bf16[2,512,128]{2,1,0:T(8,128)(2,1)S(1)}, u32[]{:S(2)}, u32[]{:S(2)}) collective-permute-start(bf16[2,512,128]{2,1,0:T(8,128)(2,1)S(1)} %get-tuple-element.43), channel_id=1, source_target_pairs={{0,6},{2,4},{4,2},{6,0},{8,14},{10,12},{12,10},{14,8},{16,22},{18,... | collective-permute-start | bytes 786440 | tf_op jit(solution)/shard_map/ppermute | solution.py:375
  81.1 10.2 %collective-permute-start.16 = (bf16[256,256]{1,0:T(8,128)(2,1)S(1)}, bf16[256,256]{1,0:T(8,128)(2,1)S(1)}, u32[]{:S(2)}, u32[]{:S(2)}) collective-permute-start(bf16[256,256]{1,0:T(8,128)(2,1)S(1)} %get-tuple-element.70), channel_id=1, source_target_pairs={{0,192},{2,194},{4,196},{6,198},{8,200},{10,202},{12,204},{14,206}... | collective-permute-start | bytes 393224 | tf_op jit(solution)/shard_map/ppermute | solution.py:383
  81.2 10.1 %collective-permute-start.17 = (bf16[256,256]{1,0:T(8,128)(2,1)S(1)}, bf16[256,256]{1,0:T(8,128)(2,1)S(1)}, u32[]{:S(2)}, u32[]{:S(2)}) collective-permute-start(bf16[256,256]{1,0:T(8,128)(2,1)S(1)} %get-tuple-element.69), channel_id=1, source_target_pairs={{0,64},{2,66},{4,68},{6,70},{8,72},{10,74},{12,76},{14,78},{16,80}... | collective-permute-start | bytes 393224 | tf_op jit(solution)/shard_map/ppermute | solution.py:383
  92.4 24.5 %collective-permute-start.26 = (bf16[512,256]{1,0:T(8,128)(2,1)}, bf16[512,256]{1,0:T(8,128)(2,1)}, u32[]{:S(2)}, u32[]{:S(2)}) collective-permute-start(bf16[512,256]{1,0:T(8,128)(2,1)} %get-tuple-element.56), channel_id=1, source_target_pairs={{0,64},{2,66},{4,68},{6,70},{8,72},{10,74},{12,76},{14,78},{16,80}... | collective-permute-start | bytes 786440 | tf_op jit(solution)/shard_map/ppermute | solution.py:389
  95.3 21.6 %collective-permute-start.27 = (bf16[512,256]{1,0:T(8,128)(2,1)}, bf16[512,256]{1,0:T(8,128)(2,1)}, u32[]{:S(2)}, u32[]{:S(2)}) collective-permute-start(bf16[512,256]{1,0:T(8,128)(2,1)} %get-tuple-element.57), channel_id=1, source_target_pairs={{0,192},{2,194},{4,196},{6,198},{8,200},{10,202},{12,204},{14,206}... | collective-permute-start | bytes 786440 | tf_op jit(solution)/shard_map/ppermute | solution.py:389
  100.1 10.4 %collective-permute-start.21 = (bf16[512,128]{1,0:T(8,128)(2,1)S(1)}, bf16[512,128]{1,0:T(8,128)(2,1)S(1)}, u32[]{:S(2)}, u32[]{:S(2)}) collective-permute-start(bf16[512,128]{1,0:T(8,128)(2,1)S(1)} %get-tuple-element.67), channel_id=1, source_target_pairs={{0,32},{2,34},{4,36},{6,38},{8,40},{10,42},{12,44},{14,46},{16,48}... | collective-permute-start | bytes 393224 | tf_op jit(solution)/shard_map/ppermute | solution.py:390
  110.5 12.1 %collective-permute-start.22 = (bf16[2,512,128]{2,1,0:T(8,128)(2,1)}, bf16[2,512,128]{2,1,0:T(8,128)(2,1)S(1)}, u32[]{:S(2)}, u32[]{:S(2)}) collective-permute-start(bf16[2,512,128]{2,1,0:T(8,128)(2,1)} %get-tuple-element.52), channel_id=1, source_target_pairs={{0,2},{2,0},{4,6},{6,4},{8,10},{10,8},{12,14},{14,12},{16,18},{18,... | collective-permute-start | bytes 786440 | tf_op jit(solution)/shard_map/ppermute | solution.py:375
  110.5 12.4 %collective-permute-start.23 = (bf16[2,512,128]{2,1,0:T(8,128)(2,1)S(1)}, bf16[2,512,128]{2,1,0:T(8,128)(2,1)S(1)}, u32[]{:S(2)}, u32[]{:S(2)}) collective-permute-start(bf16[2,512,128]{2,1,0:T(8,128)(2,1)S(1)} %get-tuple-element.53), channel_id=1, source_target_pairs={{0,4},{2,6},{4,0},{6,2},{8,12},{10,14},{12,8},{14,10},{16,20},{18,... | collective-permute-start | bytes 786440 | tf_op jit(solution)/shard_map/ppermute | solution.py:375
  110.5 12.4 %collective-permute-start.24 = (bf16[2,512,128]{2,1,0:T(8,128)(2,1)S(1)}, bf16[2,512,128]{2,1,0:T(8,128)(2,1)S(1)}, u32[]{:S(2)}, u32[]{:S(2)}) collective-permute-start(bf16[2,512,128]{2,1,0:T(8,128)(2,1)S(1)} %get-tuple-element.54), channel_id=1, source_target_pairs={{0,6},{2,4},{4,2},{6,0},{8,14},{10,12},{12,10},{14,8},{16,22},{18,... | collective-permute-start | bytes 786440 | tf_op jit(solution)/shard_map/ppermute | solution.py:375
  118.3 7.1 %collective-permute-start.29 = (bf16[128,256]{1,0:T(8,128)(2,1)S(1)}, bf16[128,256]{1,0:T(8,128)(2,1)S(1)}, u32[]{:S(2)}, u32[]{:S(2)}) collective-permute-start(bf16[128,256]{1,0:T(8,128)(2,1)S(1)} %get-tuple-element.64), channel_id=1, source_target_pairs={{0,8},{2,10},{4,12},{6,14},{8,0},{10,2},{12,4},{14,6},{16,24},{18,... | collective-permute-start | bytes 196616 | tf_op jit(solution)/shard_map/ppermute | solution.py:394
  (13 other events, 130.9 us)
